TPU v7x, 32 devices: a whole 2x2x4 slice. The times are simulated.
32 devices in a mesh: wide: 16 (over z, x, core), narrow: 2 (over y).
Axes of the slice: x: 2, y: 2, z: 4, core: 2. Of those that a mesh axis runs over, the one named last changes fastest.
Arguments:
- three_index: bfloat16 [16, 3072, 1024], P('wide', None, 'narrow'), may hold values from -0.59765625 to 0.59765625
- orbital_map: int32 [16], replicated, may hold values from 0 to 15, each once
- occ_energy: float32 [16], replicated, may hold values from -2 to -0.3
- vir_energy: float32 [1024], replicated, may hold values from 0.2 to 3
- pair_kept: int32 [6, 16], P(None, 'wide'), may hold values 0 or 1
Outputs:
- density: float32 [16, 3072, 1024], P('wide', None, 'narrow')
Inputs may be any that keep to these rules, and one draw needn't show every extreme that they name: `orbital_map`: each of the 16 orbitals once.
All inputs are finite; a program needn't handle non-finite values. No bound on the sum of `pair_kept` on one device may be relied on, other than what follows from the above.
Results may differ from a plain program's by a relative error of at most 0.0015.
Values may be sent and summed in bfloat16 or wider, within the bound.
No kernel may reach another device: no remote copies, remote signals or barrier semaphores. Data moves between devices by JAX's collectives and lax.ppermute only.
A program may use at most 192 MiB of HBM per device.

v0:
```python
import jax
import jax.numpy as jnp
import numpy as np
from jax import lax
from jax.experimental import pallas as pl
from jax.experimental.pallas import tpu as pltpu
from jax.sharding import PartitionSpec as P

ROUNDS = 5
TAIL = 16
CHUNK = 512
VMEM = 48 * 1024 * 1024


def passed_along(array, axis, by):
    length = lax.axis_size(axis)
    return lax.ppermute(array, axis, [(i, (i + by) % length) for i in range(length)])


def block_energy(orbital_map, occ_energy, block_id, occ_count):
    orbits = lax.dynamic_slice_in_dim(orbital_map, block_id * occ_count, occ_count)
    labels = jnp.arange(occ_energy.shape[0], dtype=jnp.int32)
    chosen = orbits[:, None] == labels[None, :]
    return jnp.sum(jnp.where(chosen, occ_energy[None, :], 0.0), axis=1)


def amplitudes(gathered, visiting, left_energy, right_energy, vir_all, vir_local, weight):
    coulomb = jnp.einsum("ipa,jpb->ijab", gathered, visiting, preferred_element_type=jnp.float32)
    denominator = (vir_all[:, None] + vir_local[None, :])[None, None] - (
        left_energy[:, None] + right_energy[None, :]
    )[:, :, None, None]
    return (weight * coulomb / denominator).astype(jnp.bfloat16)


def ring_plan(three_index, orbital_map, occ_energy, vir_energy, pair_kept):
    occ_count = three_index.shape[0]
    vir_count = three_index.shape[2]
    blocks = lax.axis_size("wide")
    own_block = lax.axis_index("wide")
    vir_local = lax.dynamic_slice_in_dim(
        vir_energy, lax.axis_index("narrow") * vir_count, vir_count
    )
    own_energy = block_energy(orbital_map, occ_energy, own_block, occ_count)
    weights = pair_kept.astype(jnp.float32)
    gathered = lax.all_gather(three_index, "narrow", axis=2, tiled=True)
    amplitude = amplitudes(
        gathered, three_index, own_energy, own_energy, vir_energy, vir_local, weights[0, 0]
    )
    forward = jnp.einsum(
        "ijab,jpb->ipa", amplitude, three_index, preferred_element_type=jnp.float32
    )
    visiting = three_index
    stored_amps = []
    for round_index in range(1, ROUNDS + 1):
        visiting = passed_along(visiting, "wide", 1)
        partner = (own_block - round_index) % blocks
        partner_energy = block_energy(orbital_map, occ_energy, partner, occ_count)
        amplitude = amplitudes(
            gathered,
            visiting,
            own_energy,
            partner_energy,
            vir_energy,
            vir_local,
            weights[round_index, 0],
        )
        forward = forward + jnp.einsum(
            "ijab,jpb->ipa", amplitude, visiting, preferred_element_type=jnp.float32
        )
        stored_amps.append(amplitude)
    carried = None
    for round_index in range(1, ROUNDS + 1):
        backward = jnp.einsum(
            "ijab,ipa->jpb",
            stored_amps[round_index - 1],
            gathered,
            preferred_element_type=jnp.float32,
        )
        if round_index > 1:
            carried = passed_along(carried, "wide", 1) + backward
        else:
            carried = backward
    returned = passed_along(carried, "wide", -ROUNDS)
    scattered = lax.psum_scatter(forward, "narrow", scatter_dimension=2, tiled=True)
    return scattered + returned


class Routes:
    def __init__(self, blocks):
        self.blocks = blocks
        everyone = range(blocks)
        self.lead = [self.place(w)[1] == self.place(w)[2] for w in everyone]
        self.swap = [(w, w ^ 1) for w in everyone]
        onward = [(w, self.along_z(w, 1)) for w in everyone]
        backward = [(w, self.along_z(w, -1)) for w in everyone]
        across = [(w, self.across_x(w)) for w in everyone]
        self.rounds = [
            self.either(across, onward),
            self.either(onward, across),
            self.either(across, backward),
            self.either(backward, across),
            self.either(backward, across),
        ]

    def place(self, w):
        return w // 4, (w // 2) % 2, w % 2

    def along_z(self, w, step):
        z, x, core = self.place(w)
        z = (z + (step if x == 1 else -step)) % (self.blocks // 4)
        return (z * 2 + x) * 2 + core

    def across_x(self, w):
        z, x, core = self.place(w)
        return (z * 2 + 1 - x) * 2 + 1 - core

    def either(self, of_lead, of_other):
        return [a if lead else b for lead, a, b in zip(self.lead, of_lead, of_other)]

    def moved(self, ids, pairs):
        out = [0] * self.blocks
        for source, target in pairs:
            out[target] = ids[source]
        return out


class Slab:
    def __init__(self, array, ids, far=0):
        self.pieces = list(array) if isinstance(array, (list, tuple)) else [array]
        self.array = self.pieces[0]
        self.ids = ids
        self.far = far


def pick(step, values):
    out = values[0]
    for index, value in enumerate(values):
        if index and value != values[0]:
            out = jnp.where(step == index, value, out)
    return out


def amplitude_call(jobs, table, lines, turned, vir_rows, vir_cols, earlier):
    slabs = []
    for slab, _ in jobs:
        if slab not in slabs:
            slabs.append(slab)
    count, blocks = len(slabs), len(turned)
    cols, aux = turned[0][0].shape[0], sum(piece.shape[1] for piece in turned[0])
    held_rows = aux + TAIL
    pieces = [len(slab.pieces) for slab in slabs]
    begins = [sum(pieces[:s]) for s in range(count)]
    of_job = [slabs.index(slab) for slab, _ in jobs]
    block_of = [block for _, block in jobs]
    far_of = [slab.far for slab, _ in jobs]
    line_of = [lines[slab] for slab, _ in jobs]
    row_pieces = [len(block) for block in turned]
    chunks = aux // CHUNK
    opens = [t for t in range(len(jobs)) if t == 0 or of_job[t] != of_job[t - 1]]
    half = cols // 2

    def kernel(scalars, *refs):
        sources, refs = refs[: sum(pieces)], refs[sum(pieces) :]
        row_sources, refs = refs[: sum(row_pieces)], refs[sum(row_pieces) + len(earlier) :]
        vir_row, vir_col, out, held, rows, held_sems, row_sems = refs
        step = pl.program_id(0)

        def slab_copies(s):
            row = 0
            for index in range(pieces[s]):
                source = sources[begins[s] + index]
                for begin, size in chunks_of(source.shape[0]):
                    target = held.at[s % 2, pl.ds(row, size), :]
                    yield pltpu.make_async_copy(
                        source.at[pl.ds(begin, size)], target, held_sems.at[s % 2, row // CHUNK]
                    )
                    row += size

        def row_copies(block):
            column = 0
            for source in row_sources[sum(row_pieces[:block]) : sum(row_pieces[: block + 1])]:
                for begin, size in chunks_of(source.shape[1]):
                    target = rows.at[block, :, pl.ds(column, size)]
                    yield pltpu.make_async_copy(
                        source.at[:, pl.ds(begin, size)], target, row_sems.at[block, column // CHUNK]
                    )
                    column += size

        @pl.when(step == 0)
        def _():
            for pair in zip(slab_copies(0), row_copies(block_of[0])):
                for copy in pair:
                    copy.start()
            for copy in list(slab_copies(0))[chunks:]:
                copy.start()
            for block in list(dict.fromkeys(block_of))[1:]:
                for copy in row_copies(block):
                    copy.start()

        for s, t in enumerate(opens):

            @pl.when(step == t)
            def _(s=s):
                if s:
                    for copy in slab_copies(s):
                        copy.wait()
                if s + 1 < count:
                    for copy in slab_copies(s + 1):
                        copy.start()

        for block in list(dict.fromkeys(block_of))[1:]:

            @pl.when(step == block_of.index(block))
            def _(block=block):
                for copy in row_copies(block):
                    copy.wait()

        slot = pick(step, [s % 2 for s in of_job])
        block = pick(step, block_of)
        line = pick(step, line_of)
        @pl.when(step == 0)
        def _():
            for copy in list(slab_copies(0))[chunks:]:
                copy.wait()

        plan = held[slot, aux:, :128].astype(jnp.float32)
        lane = lax.broadcasted_iota(jnp.int32, plan.shape, 1).astype(jnp.float32)
        row = lax.broadcasted_iota(jnp.int32, plan.shape, 0)
        told = jnp.where(jnp.logical_and(row == 0, lane == scalars[line, 2]), plan, 0.0)
        weight = scalars[line, 1] + jnp.sum(told, keepdims=True)

        def finish(part, coulomb):
            denominator = (vir_row[0] + vir_col[0, :, part]) - scalars[line, 0]
            out[0, :, part] = (weight * coulomb / denominator).astype(out.dtype)

        @pl.when(step == 0)
        def _():
            coulomb = None
            for index, pair in enumerate(zip(row_copies(block_of[0]), slab_copies(0))):
                for copy in pair:
                    copy.wait()
                chunk = pl.ds(index * CHUNK, CHUNK)
                term = jnp.dot(
                    rows[block_of[0], :, chunk], held[0, chunk, :], preferred_element_type=jnp.float32
                )
                coulomb = term if coulomb is None else coulomb + term
            finish(pl.ds(0, cols), coulomb)

        @pl.when(step > 0)
        def _():
            for begin in range(0, cols, half):
                part = pl.ds(begin, half)
                finish(part, jnp.dot(rows[block], held[slot, :aux, part], preferred_element_type=jnp.float32))

    return pl.pallas_call(
        kernel,
        grid=(len(jobs),),
        in_specs=[pl.BlockSpec(memory_space=pltpu.SMEM)]
        + [pl.BlockSpec(memory_space=pl.ANY)] * (sum(pieces) + sum(row_pieces) + len(earlier))
        + [
            pl.BlockSpec((1, cols, 1), lambda t: (pick(t, block_of), 0, 0)),
            pl.BlockSpec((1, 1, cols), lambda t: (pick(t, far_of), 0, 0)),
        ],
        out_specs=pl.BlockSpec((1, cols, cols), lambda t: (t, 0, 0)),
        out_shape=jax.ShapeDtypeStruct((len(jobs), cols, cols), jnp.bfloat16),
        scratch_shapes=[
            pltpu.VMEM((2, held_rows, cols), jnp.bfloat16),
            pltpu.VMEM((blocks, cols, aux), jnp.bfloat16),
            pltpu.SemaphoreType.DMA((2, chunks + 1)),
            pltpu.SemaphoreType.DMA((blocks, chunks)),
        ],
        compiler_params=pltpu.CompilerParams(vmem_limit_bytes=VMEM),
        cost_estimate=pl.CostEstimate(
            flops=2 * len(jobs) * cols * aux * cols,
            bytes_accessed=2 * cols * (blocks * aux + count * aux + len(jobs) * cols),
            transcendentals=0,
        ),
    )(table, *[p for s in slabs for p in s.pieces], *[p for b in turned for p in b], *earlier, vir_rows, vir_cols)


def chunks_of(rows):
    return [(begin, min(CHUNK, rows - begin)) for begin in range(0, rows, CHUNK)]


def copies_in(sources, held, sems):
    row, index = 0, 0
    for source in sources:
        for begin, size in chunks_of(source.shape[0]):
            yield pltpu.make_async_copy(
                source.at[pl.ds(begin, size)], held.at[pl.ds(row + begin, size)], sems.at[index]
            )
            index += 1
        row += source.shape[0]


def copies_out(held, targets, sems):
    row, index = 0, 0
    for target in targets:
        for begin, size in chunks_of(target.shape[0]):
            yield pltpu.make_async_copy(
                held.at[pl.ds(row + begin, size)], target.at[pl.ds(begin, size)], sems.at[index]
            )
            index += 1
        row += target.shape[0]


def copy_scratch(rows, cols):
    count = len(chunks_of(rows)) + 1
    return [
        pltpu.VMEM((rows, cols), jnp.bfloat16),
        pltpu.SemaphoreType.DMA((count,)),
        pltpu.SemaphoreType.DMA((count,)),
    ]


def copy_through(sources, targets, held, in_sems, out_sems):
    if [x.shape[0] for x in sources] != [x.shape[0] for x in targets]:
        loads, stores = [list(copies_in(sources, held, in_sems))], [list(copies_out(held, targets, out_sems))]
    else:
        loads = [[copy] for copy in copies_in(sources, held, in_sems)]
        stores = [[copy] for copy in copies_out(held, targets, out_sems)]
    for copies in loads:
        for copy in copies:
            copy.start()
    for before, behind in zip(loads, stores):
        for copy in before:
            copy.wait()
        for copy in behind:
            copy.start()
    for copies in stores:
        for copy in copies:
            copy.wait()


def append_call(array, tail, cuts):
    rows, cols = array.shape[0] + tail.shape[0], array.shape[1]
    begins = [0, *cuts, rows]
    sizes = [end - begin for begin, end in zip(begins, begins[1:])]

    def kernel(array_ref, tail_ref, out, *refs):
        pieces, (held, in_sems, out_sems, piece_sems) = refs[: len(sizes)], refs[len(sizes) :]
        loads = list(copies_in([array_ref, tail_ref], held, in_sems))
        stores = list(copies_out(held, [out], out_sems))
        piece_stores = list(copies_out(held, pieces, piece_sems))
        for copy in loads:
            copy.start()
        for load, *behind in zip(loads, stores, piece_stores):
            load.wait()
            for copy in behind:
                copy.start()
        for copy in stores + piece_stores:
            copy.wait()

    scratch = copy_scratch(rows, cols)
    return pl.pallas_call(
        kernel,
        in_specs=[pl.BlockSpec(memory_space=pl.ANY)] * 2,
        out_specs=[pl.BlockSpec(memory_space=pl.ANY)] * (1 + len(sizes)),
        out_shape=[jax.ShapeDtypeStruct((size, cols), array.dtype) for size in (rows, *sizes)],
        scratch_shapes=scratch + scratch[-1:],
        compiler_params=pltpu.CompilerParams(vmem_limit_bytes=VMEM),
    )(array, tail)


def choice_call(flag, a, b, earlier, cuts=(), keep=False):
    rows, cols = a.shape
    begins = [0, *cuts, rows]
    pieces = len(cuts) + 1
    shapes = [(end - begin, cols) for begin, end in zip(begins, begins[1:])]
    kept = [(rows, cols)] if keep else []

    def kernel(flag_ref, a_ref, b_ref, *refs):
        refs = refs[len(earlier) :]
        outs, kept_outs, scratch = refs[:pieces], refs[pieces : pieces + len(kept)], refs[pieces + len(kept) :]
        if keep:
            held, loads, stores, other_held, other_loads, other_stores = scratch
            leads = flag_ref[0] == 1
            ours = list(copies_in([a_ref], held, loads))
            theirs = list(copies_in([b_ref], other_held, other_loads))
            kept_copies = list(copies_out(held, kept_outs, stores))
            ours_out = list(copies_out(held, outs, other_stores))
            theirs_out = list(copies_out(other_held, outs, other_stores))
            for copy in ours:
                copy.start()

            @pl.when(jnp.logical_not(leads))
            def _():
                for copy in theirs:
                    copy.start()

            for load, store, also in zip(ours, kept_copies, ours_out):
                load.wait()
                store.start()
                pl.when(leads)(also.start)

            @pl.when(jnp.logical_not(leads))
            def _():
                for load, store in zip(theirs, theirs_out):
                    load.wait()
                    store.start()

            for store, also in zip(kept_copies, ours_out):
                store.wait()
                also.wait()
        else:
            for value, source in ((1, a_ref), (0, b_ref)):

                @pl.when(flag_ref[0] == value)
                def _(source=source):
                    parts = [source.at[pl.ds(at, out.shape[0])] for at, out in zip(begins, outs)]
                    copy_through(parts, outs, *scratch)

    return pl.pallas_call(
        kernel,
        in_specs=[pl.BlockSpec(memory_space=pltpu.SMEM)]
        + [pl.BlockSpec(memory_space=pl.ANY)] * (2 + len(earlier)),
        out_specs=[pl.BlockSpec(memory_space=pl.ANY)] * (pieces + len(kept)),
        out_shape=[jax.ShapeDtypeStruct(shape, a.dtype) for shape in shapes + kept],
        scratch_shapes=copy_scratch(rows, cols) * (1 + len(kept)),
        compiler_params=pltpu.CompilerParams(vmem_limit_bytes=VMEM),
        cost_estimate=pl.CostEstimate(flops=0, bytes_accessed=2 * a.size * a.dtype.itemsize, transcendentals=0),
    )(flag, a, b, *earlier)


def turn_call(array, rows, earlier):
    cols = array.shape[1]

    def kernel(array_ref, *refs):
        refs[-1][...] = array_ref[...].T

    return pl.pallas_call(
        kernel,
        grid=(rows // CHUNK,),
        in_specs=[pl.BlockSpec((CHUNK, cols), lambda i: (i, 0))]
        + [pl.BlockSpec(memory_space=pl.ANY)] * len(earlier),
        out_specs=pl.BlockSpec((cols, CHUNK), lambda i: (0, i)),
        out_shape=jax.ShapeDtypeStruct((cols, rows), array.dtype),
        compiler_params=pltpu.CompilerParams(vmem_limit_bytes=VMEM),
    )(array, *earlier)


def join_call(earlier):
    def kernel(*refs):
        refs[-1][...] = jnp.zeros_like(refs[-1])

    return pl.pallas_call(
        kernel,
        in_specs=[pl.BlockSpec(memory_space=pl.ANY)] * len(earlier),
        out_specs=pl.BlockSpec(memory_space=pltpu.VMEM),
        out_shape=jax.ShapeDtypeStruct((8, 128), jnp.float32),
    )(*earlier)


def density_call(terms, parts, out_dtype, aux, earlier, rows=None, copied=None, cuts=()):
    count = len(terms)
    depth = terms[0][0].array.shape[1]
    extra = list(copied or [])
    total_rows = sum(x.shape[0] for x in extra)
    ends = [0, *cuts, total_rows]
    whole = [jax.ShapeDtypeStruct((b - a, depth), jnp.bfloat16) for a, b in zip(ends, ends[1:]) if extra]
    pieces = [len(t[0].pieces) for t in terms]
    begins = [sum(pieces[:s]) for s in range(count)]
    cols = depth
    begin, length = rows or (0, aux)
    tile = 512
    while length % tile or begin % tile:
        tile //= 2
    steps = length // tile
    spans = []
    for part in parts:
        ends = np.cumsum([piece.shape[0] // tile for piece in part])
        shift = begin // tile if ends[-1] == aux // tile else 0
        spans.append([(int(end) - piece.shape[0] // tile - shift, int(end) - shift) for end, piece in zip(ends, part)])
    parts = [p for part in parts for p in part]

    def kernel(*refs):
        sources, refs = refs[: sum(pieces)], refs[sum(pieces) :]
        amps, refs = refs[:count], refs[count + len(earlier) :]
        source, refs = refs[: len(extra)], refs[len(extra) :]
        part_refs, out, refs = refs[: len(parts)], refs[len(parts)], refs[len(parts) + 1 :]
        target, refs = refs[: len(whole)], refs[len(whole) :]
        (left, right, left_sems, right_sems), scratch = refs[:4], refs[4:]
        step = pl.program_id(0)
        slot = step % 2

        def amp_copies():
            for s, (_, _, place) in enumerate(terms):
                yield pltpu.make_async_copy(
                    amps[s].at[place], right.at[:, pl.ds(s * depth, depth)], right_sems.at[s]
                )

        def slab_copies(which, start, of=range(count)):
            for s in of:
                end = 0
                for index in range(pieces[s]):
                    source = sources[begins[s] + index]
                    first = end
                    end += source.shape[0] // tile

                    def act(source=source, first=first, s=s):
                        row = pl.multiple_of((begin // tile + which - first) * tile, tile)
                        copy = pltpu.make_async_copy(
                            source.at[pl.ds(row, tile), :],
                            left.at[which % 2, :, pl.ds(s * depth, depth)],
                            left_sems.at[which % 2, s],
                        )
                        copy.start() if start else copy.wait()

                    at = begin // tile + which
                    if pieces[s] == 1:
                        act()
                    else:
                        pl.when(jnp.logical_and(at >= first, at < end))(act)

        @pl.when(step == 0)
        def _():
            for s, copy in enumerate(amp_copies()):
                copy.start()
                slab_copies(step, True, [s])
            if extra:
                for copy in copies_in(source, scratch[0], scratch[1]):
                    copy.start()

        @pl.when(step + 1 < steps)
        def _():
            slab_copies(step + 1, True)

        def finish(total):
            at = 0
            for span in spans:
                part = part_refs[at][...]
                for index in range(1, len(span)):
                    part = jnp.where(step >= span[index][0], part_refs[at + index][...], part)
                total = total + part.astype(jnp.float32)
                at += len(span)
            out[...] = total.astype(out.dtype)

        def product(a, b):
            return lax.dot_general(a, b, (((1,), (1,)), ((), ())), preferred_element_type=jnp.float32)

        @pl.when(step == 0)
        def _():
            total = None
            for s, copy in enumerate(amp_copies()):
                copy.wait()
                slab_copies(step, False, [s])
                at = pl.ds(s * depth, depth)
                term = product(left[0, :, at], right[:, at])
                total = term if total is None else total + term
            finish(total)

        @pl.when(step > 0)
        def _():
            slab_copies(step, False)
            finish(product(left[slot], right[...]))

        if extra:

            @pl.when(step == 1)
            def _():
                for copy in copies_in(source, scratch[0], scratch[1]):
                    copy.wait()
                for copy in copies_out(scratch[0], target, scratch[2]):
                    copy.start()

            @pl.when(step == steps - 1)
            def _():
                for copy in copies_out(scratch[0], target, scratch[2]):
                    copy.wait()

    def rows_of(start, end):
        return pl.BlockSpec((tile, cols), lambda i: (jnp.clip(i - start, 0, end - start - 1), 0))

    bytes_moved = 2 * count * (length * depth + cols * depth)
    bytes_moved += sum(length * cols * p.dtype.itemsize for p in parts)
    return pl.pallas_call(
        kernel,
        grid=(steps,),
        in_specs=[pl.BlockSpec(memory_space=pl.ANY)] * (sum(pieces) + count + len(earlier) + len(extra))
        + [rows_of(*ends) for span in spans for ends in span],
        out_specs=[pl.BlockSpec((tile, cols), lambda i: (i, 0))]
        + [pl.BlockSpec(memory_space=pl.ANY)] * len(whole),
        out_shape=[jax.ShapeDtypeStruct((length, cols), out_dtype)]
        + whole,
        scratch_shapes=[
            pltpu.VMEM((2, tile, count * depth), jnp.bfloat16),
            pltpu.VMEM((cols, count * depth), jnp.bfloat16),
            pltpu.SemaphoreType.DMA((2, count)),
            pltpu.SemaphoreType.DMA((count,)),
            *(copy_scratch(total_rows, depth) if extra else []),
        ],
        compiler_params=pltpu.CompilerParams(vmem_limit_bytes=VMEM),
        cost_estimate=pl.CostEstimate(
            flops=2 * length * depth * cols * count,
            bytes_accessed=(bytes_moved + length * cols * jnp.dtype(out_dtype).itemsize),
            transcendentals=0,
        ),
    )(*[p for t in terms for p in t[0].pieces], *[t[1] for t in terms], *earlier, *extra, *parts)


def paired_plan(three_index, orbital_map, occ_energy, vir_energy, pair_kept):
    blocks = lax.axis_size("wide")
    routes = Routes(blocks)
    here = lax.axis_index("wide")
    side = lax.axis_index("narrow")
    aux, vir_count = three_index.shape[1:]

    def moved(slab, pairs):
        sent = [lax.ppermute(piece, "wide", pairs) for piece in slab.pieces]
        return Slab(sent, routes.moved(slab.ids, pairs), slab.far)

    def swapped(slab):
        return moved(slab, routes.swap)

    flag = jnp.asarray(np.array(routes.lead, np.int32))[here].reshape(1)

    def copied(array, *earlier, cuts=()):
        return choice_call(flag, array, array, earlier, cuts)

    def sibling(array):
        return lax.ppermute(array, "narrow", [(0, 1), (1, 0)])

    plan = jnp.zeros((TAIL, vir_count), jnp.bfloat16)
    plan = plan.at[0, : ROUNDS + 1].set(pair_kept[:, 0].astype(jnp.bfloat16))
    whole, *split = append_call(three_index[0], plan, [aux // 2])
    own = Slab(whole, list(range(blocks)))

    r1 = moved(own, routes.rounds[0])
    own_far = Slab([sibling(piece) for piece in split], own.ids, 1)
    mate = swapped(own)

    labels = jnp.arange(occ_energy.shape[0], dtype=jnp.int32)
    picked = orbital_map[:, None] == labels[None, :]
    energy = jnp.sum(jnp.where(picked, occ_energy[None, :], 0.0), axis=1)

    def table_of(ids):
        ids = np.array(ids, np.int32).T
        places = np.arange(blocks)[:, None]
        back, forth = (places - ids) % blocks, (ids - places) % blocks
        behind = back <= ROUNDS
        known = np.stack([ids, np.where(behind, back, -1), np.where(behind, -1, forth)])
        block, mine, theirs = jnp.asarray(known.astype(np.int32))[:, here]
        places = jnp.arange(blocks, dtype=jnp.int32)[None, :]
        both = jnp.where(places == here, energy[None, :], 0.0)
        both = both + jnp.where(places == block[:, None], energy[None, :], 0.0)
        entries = jnp.arange(ROUNDS + 1, dtype=jnp.int32)[None, :]
        kept = pair_kept[:, 0].astype(jnp.float32)[None, :]
        weight = jnp.sum(jnp.where(entries == mine[:, None], kept, 0.0), axis=1)
        return jnp.stack([jnp.sum(both, axis=1), weight, theirs.astype(jnp.float32)], axis=1)

    vir = jnp.stack(
        [lax.dynamic_slice_in_dim(vir_energy, s * vir_count, vir_count) for s in (side, 1 - side)]
    )
    vir_rows, vir_cols = vir[:, :, None], vir[:, None, :]

    def moved_ids(ids_lead, ids_other, pairs):
        return routes.moved(routes.either(ids_lead, ids_other), pairs)

    def swapped_ids(ids):
        return routes.moved(ids, routes.swap)

    r2_ids = moved_ids(own.ids, r1.ids, routes.rounds[1])
    r3_ids = moved_ids(r2_ids, own.ids, routes.rounds[2])
    r4_ids = routes.moved(r3_ids, routes.rounds[3])
    r5_ids = routes.moved(own.ids, routes.rounds[4])
    all_ids = [own.ids, mate.ids]
    for ids in (r1.ids, r2_ids, r3_ids, r4_ids, r5_ids):
        all_ids += [ids, swapped_ids(ids)]
    table = table_of(all_ids)
    near, far = 0, 1
    rows_near = [own.array[:aux].T]
    stacks = {}

    def amps(jobs, turned, *earlier):
        lines = {slab: all_ids.index(slab.ids) for slab, _ in jobs}
        stack = amplitude_call(jobs, table, lines, turned, vir_rows, vir_cols, earlier)
        for place, job in enumerate(jobs):
            stacks[job] = (stack, place)
        return stack

    def density(slabs, block, parts, dtype, *earlier, rows=None, copied=None, cuts=()):
        terms = [(slab, *stacks[slab, block]) for slab in slabs]
        out, *copy = density_call(terms, parts, dtype, aux, earlier, rows, copied, cuts)
        return (out, *copy) if copy else out

    f32, bf16 = jnp.float32, jnp.bfloat16
    done = amps([(own, near), (mate, near)], [rows_near])

    parts = own_far.pieces
    sent, kept = choice_call(1 - flag, r1.array, own.array, [parts[0], done], keep=True)
    r1 = Slab(kept, r1.ids)
    sent2 = Slab(sent, routes.either(own.ids, r1.ids))
    r2 = moved(sent2, routes.rounds[1])
    s1 = swapped(r1)
    done = amps([(r1, near), (s1, near)], [rows_near], sent2.array)
    part = density([own, mate, r1, s1], near, [], f32, done)
    cut = parts[0].shape[0]
    rows_far = [turn_call(parts[0], cut, [part])]

    sent, kept = choice_call(flag, r2.array, own.array, [parts[1], *rows_far], keep=True)
    r2 = Slab(kept, r2.ids)
    sent3 = Slab(sent, routes.either(r2.ids, own.ids))
    r3 = moved(sent3, routes.rounds[2])
    s2 = swapped(r2)
    mate_far = swapped(own_far)
    rows_far.append(turn_call(parts[1], aux - cut, [sent3.array]))
    jobs = [(r2, near), (r2, far), (s2, far), (s2, near), (r1, far), (s1, far)]
    jobs += [(own_far, near)]
    done = amps(jobs, [rows_near, rows_far])
    part = density([own_far, r2, s2], near, [[part]], f32, done)

    r3 = Slab(copied(r3.array, part), r3.ids)
    r4 = moved(r3, routes.rounds[3])
    s3 = swapped(r3)
    out_part, again = density([r1, s1, r2, s2], far, [], f32, r3.array, copied=own.pieces)
    r5 = moved(Slab(again, own.ids), routes.rounds[4])
    jobs = [(mate_far, near), (r3, near), (r3, far), (s3, far), (s3, near)]
    done = amps(jobs, [rows_near, rows_far], out_part)

    done = amps([(r4, far)], [rows_near, rows_far], done)
    half = aux // 2
    slabs = [r3, s3, r4]
    sent0, again = density(
        slabs, far, [[out_part]], bf16, done, rows=(0, half), copied=own_far.pieces
    )
    r6 = moved(Slab(again, own.ids, 1), routes.rounds[4])
    sent1 = density(slabs, far, [[out_part]], bf16, sent0, rows=(half, half))
    incoming = [sibling(sent0), sibling(sent1)]
    done = amps([(r4, near)], [rows_near], sent1)
    part = density([mate_far, r3, s3, r4], near, [[part]], f32, done)

    thirds = [aux // 3, aux // 3 * 2]
    r5 = Slab(copied(r5.array, part, cuts=thirds), r5.ids)
    s5 = swapped(r5)
    done = amps([(r5, near)], [rows_near], *r5.pieces)
    done = join_call([incoming[0], done])
    done = amps([(s5, near)], [rows_near], done)
    part = density([r5, s5], near, [[part]], f32, done)
    r6 = Slab(copied(r6.array, part, cuts=thirds), r6.ids, 1)
    s6 = swapped(r6)
    done = amps([(r6, near)], [rows_near], *r6.pieces)
    done = join_call([incoming[1], done])
    done = amps([(s6, near)], [rows_near], done)
    return density([r6, s6], near, [[part], incoming], f32, done)[None]


def solution(mesh):
    wide, narrow = mesh.shape["wide"], mesh.shape["narrow"]
    paired = narrow == 2 and wide % 4 == 0 and wide > 2 * ROUNDS + 1 and ROUNDS == 5

    def per_device(three_index, *rest):
        if paired and three_index.shape[0] == 1:
            return paired_plan(three_index, *rest)
        return ring_plan(three_index, *rest)

    placed = (P("wide", None, "narrow"), P(), P(), P(), P(None, "wide"))
    return jax.shard_map(
        per_device, mesh=mesh, in_specs=placed, out_specs=P("wide", None, "narrow"), check_vma=False
    )
```

profile of v0, /device:TPU:3, one launch (start us, length us, event | category | flops | bytes accessed | tf_op | source)
XLA Modules:
  0.0 278.0 jit_solution(14189312845610860509)
XLA Ops:
  0.7 3.0 %shard_map.73 = (bf16[3088,512]{1,0:T(8,128)(2,1)}, bf16[1536,512]{1,0:T(8,128)(2,1)S(1)}, bf16[1552,512]{1,0:T(8,128)(2,1)S(1)}) custom-call(bf16[3072,512]{1,0:T(8,128)(2,1)} %bitcast.20, bf16[16,512]{1,0:T(8,128)(2,1)S(1)} %scatter.4.tail_ref), custom_call_target="tpu_custom_call" | custom-call | tf_op jit(solution)/shard_map/pallas_call | solution.py:355
  4.5 1.4 collective-permute-start.1
  6.0 5.6 %copy.43 = bf16[3088,512]{0,1:T(8,128)(2,1)} copy(bf16[3088,512]{1,0:T(8,128)(2,1)} %get-tuple-element.34.refs_0_.b_ref.refs_9_) | data formatting | bytes 6324224 | tf_op jit(solution)/shard_map/pallas_call | solution.py:355
  13.0 1.0 copy.45.refs_3_.refs_4_.refs_9_.refs_8_.refs_5_.refs_7_
  15.3 2.1 slice_bitcast_fusion.refs_2_.refs_6_.refs_4_.refs_1_.refs_3_
  17.5 7.1 %shard_map.74.refs_1_.refs_4_.refs_5_ = bf16[2,512,512]{2,1,0:T(8,128)(2,1)S(1)} custom-call(f32[12,3]{1,0:T(8,128)S(1)} %copy.44.scalars, bf16[3088,512]{1,0:T(8,128)(2,1)} %get-tuple-element.34.refs_0_.b_ref.refs_9_, bf16[3088,512]{1,0:T(8,128)(2,1)} %collective-permute-done.2.refs_1_, ...), custom_call_target="tpu_custom_call" | custom-call | flops 3221225472 | bytes 10485760 | tf_op jit(solution)/shard_map/pallas_call | solution.py:255
  24.5 14.3 %collective-permute-done.1.refs_0_.array_ref.refs_4_.refs_7_ = bf16[1536,512]{1,0:T(8,128)(2,1)} collective-permute-done((bf16[1536,512]{1,0:T(8,128)(2,1)S(1)}, bf16[1536,512]{1,0:T(8,128)(2,1)}, u32[]{:S(2)}, u32[]{:S(2)}) %collective-permute-start.1) | collective-permute-done | bytes 1572896 | tf_op jit(solution)/shard_map/ppermute | solution.py:621
  38.9 3.1 %collective-permute-done.a_ref = bf16[3088,512]{1,0:T(8,128)(2,1)} collective-permute-done((bf16[3088,512]{1,0:T(8,128)(2,1)}, bf16[3088,512]{1,0:T(8,128)(2,1)}, u32[]{:S(2)}, u32[]{:S(2)}) %collective-permute-start) | collective-permute-done | bytes 3162144 | tf_op jit(solution)/shard_map/ppermute | solution.py:609
  42.0 5.5 %shard_map.75 = (bf16[3088,512]{1,0:T(8,128)(2,1)}, bf16[3088,512]{1,0:T(8,128)(2,1)}) custom-call(s32[1]{0:T(128)S(6)} %sub.6.flag_ref, bf16[3088,512]{1,0:T(8,128)(2,1)} %collective-permute-done.a_ref, bf16[3088,512]{1,0:T(8,128)(2,1)} %get-tuple-element.34.refs_0_.b_ref.refs_9_, ...), custom_call_target="tpu_custom_call" | custom-call | bytes 6324224 | tf_op jit(solution)/shard_map/pallas_call | solution.py:413
  48.9 1.2 collective-permute-start.4
  50.2 3.7 %collective-permute-done.5.refs_1_.refs_3_ = bf16[3088,512]{1,0:T(8,128)(2,1)} collective-permute-done((bf16[3088,512]{1,0:T(8,128)(2,1)}, bf16[3088,512]{1,0:T(8,128)(2,1)}, u32[]{:S(2)}, u32[]{:S(2)}) %collective-permute-start.5) | collective-permute-done | bytes 3162144 | tf_op jit(solution)/shard_map/ppermute | solution.py:609
  53.8 6.8 %shard_map.76.refs_6_.refs_7_.refs_8_ = bf16[2,512,512]{2,1,0:T(8,128)(2,1)S(1)} custom-call(f32[12,3]{1,0:T(8,128)S(1)} %copy.44.scalars, bf16[3088,512]{1,0:T(8,128)(2,1)} %get-tuple-element.38.refs_0_.refs_2_, bf16[3088,512]{1,0:T(8,128)(2,1)} %collective-permute-done.5.refs_1_.refs_3_, ...), custom_call_target="tpu_custom_call" | custom-call | flops 3221225472 | bytes 10485760 | tf_op jit(solution)/shard_map/pallas_call | solution.py:255
  60.6 11.4 %shard_map.77.refs_0_.refs_8_ = f32[3072,512]{1,0:T(8,128)} custom-call(bf16[3088,512]{1,0:T(8,128)(2,1)S(1)} %copy-done.3, bf16[3088,512]{1,0:T(8,128)(2,1)} %collective-permute-done.2.refs_1_, bf16[3088,512]{1,0:T(8,128)(2,1)} %get-tuple-element.38.refs_0_.refs_2_, bf16[3088,512]{1,0:T(8,128)(2,1)} %collective-permute-done.5.refs_1_.refs_3_, ...), custom_call_target="tpu_custom_call" | custom-call | flops 6442450944 | bytes 20971520 | tf_op jit(solution)/shard_map/pallas_call | solution.py:576
  72.0 2.6 shard_map.78.refs_1_.refs_7_.refs_5_.refs_2_
  74.6 11.1 %collective-permute-done.4.refs_0_.array_ref.refs_5_.refs_1_.refs_8_ = bf16[1552,512]{1,0:T(8,128)(2,1)S(1)} collective-permute-done((bf16[1552,512]{1,0:T(8,128)(2,1)S(1)}, bf16[1552,512]{1,0:T(8,128)(2,1)S(1)}, u32[]{:S(2)}, u32[]{:S(2)}) %collective-permute-start.4) | collective-permute-done | bytes 1589280 | tf_op jit(solution)/shard_map/ppermute | solution.py:621
  86.6 4.6 %shard_map.79 = (bf16[3088,512]{1,0:T(8,128)(2,1)}, bf16[3088,512]{1,0:T(8,128)(2,1)}) custom-call(s32[1]{0:T(128)} %dynamic_slice.12.flag_ref, bf16[3088,512]{1,0:T(8,128)(2,1)} %collective-permute-done.3.a_ref, bf16[3088,512]{1,0:T(8,128)(2,1)} %get-tuple-element.34.refs_0_.b_ref.refs_9_, ...), custom_call_target="tpu_custom_call" | custom-call | bytes 6324224 | tf_op jit(solution)/shard_map/pallas_call | solution.py:413
  91.2 1.1 collective-permute-start.7
  93.0 4.8 %collective-permute-done.7.refs_1_.refs_3_ = bf16[3088,512]{1,0:T(8,128)(2,1)S(1)} collective-permute-done((bf16[3088,512]{1,0:T(8,128)(2,1)}, bf16[3088,512]{1,0:T(8,128)(2,1)S(1)}, u32[]{:S(2)}, u32[]{:S(2)}) %collective-permute-start.7) | collective-permute-done | bytes 3162144 | tf_op jit(solution)/shard_map/ppermute | solution.py:609
  97.8 1.7 copy-done.20
  99.5 18.7 %shard_map.81.refs_4_.refs_5_.refs_6_.refs_7_ = bf16[7,512,512]{2,1,0:T(8,128)(2,1)} custom-call(f32[12,3]{1,0:T(8,128)S(1)} %copy.44.scalars, bf16[3088,512]{1,0:T(8,128)(2,1)} %get-tuple-element.40.refs_0_.refs_2_, bf16[3088,512]{1,0:T(8,128)(2,1)} %copy-done.20, bf16[3088,512]{1,0:T(8,128)(2,1)} %get-tuple-element.38.refs_0_.refs_2_, ...), custom_call_target="tpu_custom_call" | custom-call | flops 11274289152 | bytes 25690112 | tf_op jit(solution)/shard_map/pallas_call | solution.py:255
  118.1 12.4 %shard_map.82.refs_0_.refs_10_ = f32[3072,512]{1,0:T(8,128)} custom-call(bf16[1536,512]{1,0:T(8,128)(2,1)} %collective-permute-done.1.refs_0_.array_ref.refs_4_.refs_7_, bf16[1552,512]{1,0:T(8,128)(2,1)S(1)} %copy-done.7, bf16[3088,512]{1,0:T(8,128)(2,1)} %get-tuple-element.40.refs_0_.refs_2_, bf16[3088,512]{1,0:T(8,128)(2,1)} %copy-done.20, ...), custom_call_target="tpu_custom_call" | custom-call | flops 4831838208 | bytes 23592960 | tf_op jit(solution)/shard_map/pallas_call | solution.py:576
  130.6 1.7 copy-done.21
  132.2 2.7 shard_map.83.refs_8_.refs_2_.refs_0_
  135.4 3.5 %collective-permute-start.9 = (bf16[3088,512]{1,0:T(8,128)(2,1)S(1)}, bf16[3088,512]{1,0:T(8,128)(2,1)}, u32[]{:S(2)}, u32[]{:S(2)}) collective-permute-start(bf16[3088,512]{1,0:T(8,128)(2,1)S(1)} %shard_map.83.refs_8_.refs_2_.refs_0_), channel_id=1, source_target_pairs={{0,8},{2,4},{4,2},{6,30},{8,16},{10,12},{12,10},{14,6},{16,24},{18... | collective-permute-start | bytes 9486344 | tf_op jit(solution)/shard_map/ppermute | solution.py:609
  139.4 14.4 %shard_map.84 = (f32[3072,512]{1,0:T(8,128)}, bf16[3088,512]{1,0:T(8,128)(2,1)}) custom-call(bf16[3088,512]{1,0:T(8,128)(2,1)} %get-tuple-element.38.refs_0_.refs_2_, bf16[3088,512]{1,0:T(8,128)(2,1)} %collective-permute-done.5.refs_1_.refs_3_, bf16[3088,512]{1,0:T(8,128)(2,1)} %get-tuple-element.40.refs_0_.refs_2_, bf16[3088,512]{1,0:T(8,128)(2,1)} %copy-done.20, ...), custom_call_target="tpu_custom_call" | custom-call | flops 6442450944 | bytes 20971520 | tf_op jit(solution)/shard_map/pallas_call | solution.py:576
  154.1 1.2 copy-done.14
  155.3 14.0 %shard_map.85.refs_4_.refs_3_.refs_5_.refs_6_.refs_7_ = bf16[5,512,512]{2,1,0:T(8,128)(2,1)} custom-call(f32[12,3]{1,0:T(8,128)S(1)} %copy.44.scalars, bf16[1536,512]{1,0:T(8,128)(2,1)S(1)} %collective-permute-done.10.refs_0_, bf16[1552,512]{1,0:T(8,128)(2,1)} %copy-done.14, bf16[3088,512]{1,0:T(8,128)(2,1)} %copy-done.2, ...), custom_call_target="tpu_custom_call" | custom-call | flops 8053063680 | bytes 18350080 | tf_op jit(solution)/shard_map/pallas_call | solution.py:255
  169.4 1.1 copy-done.16
  170.5 2.8 %collective-permute-done.9.refs_0_.refs_2_.refs_4_ = bf16[3088,512]{1,0:T(8,128)(2,1)} collective-permute-done((bf16[3088,512]{1,0:T(8,128)(2,1)S(1)}, bf16[3088,512]{1,0:T(8,128)(2,1)}, u32[]{:S(2)}, u32[]{:S(2)}) %collective-permute-start.9) | collective-permute-done | bytes 3162144 | tf_op jit(solution)/shard_map/ppermute | solution.py:609
  173.3 4.8 %shard_map.86.refs_5_.refs_6_ = bf16[1,512,512]{2,1,0:T(8,128)(2,1)S(1)} custom-call(f32[12,3]{1,0:T(8,128)S(1)} %copy.44.scalars, bf16[3088,512]{1,0:T(8,128)(2,1)} %collective-permute-done.9.refs_0_.refs_2_.refs_4_, bf16[512,3072]{1,0:T(8,128)(2,1)} %copy-done, bf16[512,1536]{1,0:T(8,128)(2,1)S(1)} %shard_map.78.refs_1_.refs_7_.refs_5_.refs_2_, ...), custom_call_target="tpu_custom_call" | custom-call | flops 1610612736 | bytes 9961472 | tf_op jit(solution)/shard_map/pallas_call | solution.py:255
  178.1 7.0 %shard_map.87 = (bf16[1536,512]{1,0:T(8,128)(2,1)S(1)}, bf16[3088,512]{1,0:T(8,128)(2,1)}) custom-call(bf16[3088,512]{1,0:T(8,128)(2,1)} %copy-done.2, bf16[3088,512]{1,0:T(8,128)(2,1)} %collective-permute-done.8.refs_3_.refs_1_, bf16[3088,512]{1,0:T(8,128)(2,1)} %collective-permute-done.9.refs_0_.refs_2_.refs_4_, ...), custom_call_target="tpu_custom_call" | custom-call | flops 2415919104 | bytes 11010048 | tf_op jit(solution)/shard_map/pallas_call | solution.py:576
  185.1 3.9 %collective-permute-start.12 = (bf16[3088,512]{1,0:T(8,128)(2,1)}, bf16[3088,512]{1,0:T(8,128)(2,1)}, u32[]{:S(2)}, u32[]{:S(2)}) collective-permute-start(bf16[3088,512]{1,0:T(8,128)(2,1)} %get-tuple-element.42), channel_id=1, source_target_pairs={{0,8},{2,4},{4,2},{6,30},{8,16},{10,12},{12,10},{14,6},{16,24},{18... | collective-permute-start | bytes 9486344 | tf_op jit(solution)/shard_map/ppermute | solution.py:609
  189.0 1.2 collective-permute-start.17
  190.2 7.7 %shard_map.88.refs_2_ = bf16[1536,512]{1,0:T(8,128)(2,1)} custom-call(bf16[3088,512]{1,0:T(8,128)(2,1)} %copy-done.2, bf16[3088,512]{1,0:T(8,128)(2,1)} %collective-permute-done.8.refs_3_.refs_1_, bf16[3088,512]{1,0:T(8,128)(2,1)} %collective-permute-done.9.refs_0_.refs_2_.refs_4_, bf16[5,512,512]{2,1,0:T(8,128)(2,1)} %shard_map.85.refs_4_.refs_3_.refs_5_.refs_6_.refs_7_, ...), custom_call_target="tpu_custom_call" | custom-call | flops 2415919104 | bytes 11010048 | tf_op jit(solution)/shard_map/pallas_call | solution.py:576
  198.0 5.0 %shard_map.89.refs_8_.refs_9_ = bf16[1,512,512]{2,1,0:T(8,128)(2,1)S(1)} custom-call(f32[12,3]{1,0:T(8,128)S(1)} %copy.44.scalars, bf16[3088,512]{1,0:T(8,128)(2,1)} %collective-permute-done.9.refs_0_.refs_2_.refs_4_, bf16[512,3072]{1,0:T(8,128)(2,1)S(1)} %copy-done.1, bf16[1536,512]{1,0:T(8,128)(2,1)} %shard_map.88.refs_2_, f32[2,512,1]{2,1,0:T(8,128)S(1)} %copy-done.4, ...), custom_call_target="tpu_custom_call" | custom-call | flops 1610612736 | bytes 6815744 | tf_op jit(solution)/shard_map/pallas_call | solution.py:255
  203.0 13.5 %shard_map.90.refs_0_.refs_9_ = f32[3072,512]{1,0:T(8,128)} custom-call(bf16[1536,512]{1,0:T(8,128)(2,1)S(1)} %copy-done.17, bf16[1552,512]{1,0:T(8,128)(2,1)S(1)} %copy-done.15, bf16[3088,512]{1,0:T(8,128)(2,1)} %copy-done.2, bf16[3088,512]{1,0:T(8,128)(2,1)} %collective-permute-done.8.refs_3_.refs_1_, ...), custom_call_target="tpu_custom_call" | custom-call | flops 6442450944 | bytes 27262976 | tf_op jit(solution)/shard_map/pallas_call | solution.py:576
  216.5 3.2 %shard_map.91 = (bf16[1024,512]{1,0:T(8,128)(2,1)S(1)}, bf16[1024,512]{1,0:T(8,128)(2,1)}, bf16[1040,512]{1,0:T(8,128)(2,1)S(1)}) custom-call(s32[1]{0:T(128)} %dynamic_slice.12.flag_ref, bf16[3088,512]{1,0:T(8,128)(2,1)} %collective-permute-done.13.a_ref.b_ref, bf16[3088,512]{1,0:T(8,128)(2,1)} %collective-permute-done.13.a_ref.b_ref, ...), custom_call_target="tpu_custom_call" | custom-call | bytes 6324224 | tf_op jit(solution)/shard_map/pallas_call | solution.py:413
  220.4 1.3 collective-permute-done.17.refs_0_.refs_10_
  221.7 1.1 copy-done.22
  222.8 1.2 collective-permute-start.21
  224.0 4.1 %shard_map.92.refs_1_.refs_6_ = bf16[1,512,512]{2,1,0:T(8,128)(2,1)S(1)} custom-call(f32[12,3]{1,0:T(8,128)S(1)} %copy.44.scalars, bf16[1024,512]{1,0:T(8,128)(2,1)S(1)} %get-tuple-element.45.refs_0_.refs_4_, bf16[1024,512]{1,0:T(8,128)(2,1)} %get-tuple-element.46.refs_1_.refs_5_, bf16[1040,512]{1,0:T(8,128)(2,1)S(1)} %get-tuple-element.47.refs_2_.refs_6_, ...), custom_call_target="tpu_custom_call" | custom-call | flops 1610612736 | bytes 6815744 | tf_op jit(solution)/shard_map/pallas_call | solution.py:255
  230.3 5.7 %shard_map.94.refs_7_.refs_8_ = bf16[1,512,512]{2,1,0:T(8,128)(2,1)S(1)} custom-call(f32[12,3]{1,0:T(8,128)S(1)} %copy.44.scalars, bf16[1024,512]{1,0:T(8,128)(2,1)} %collective-permute-done.14.refs_0_.refs_3_, bf16[1024,512]{1,0:T(8,128)(2,1)} %collective-permute-done.15.refs_1_.refs_4_, bf16[1040,512]{1,0:T(8,128)(2,1)} %collective-permute-done.16.refs_2_.refs_5_, ...), custom_call_target="tpu_custom_call" | custom-call | flops 1610612736 | bytes 6815744 | tf_op jit(solution)/shard_map/pallas_call | solution.py:255
  236.0 11.2 %shard_map.95.refs_0_.refs_9_ = f32[3072,512]{1,0:T(8,128)} custom-call(bf16[1024,512]{1,0:T(8,128)(2,1)S(1)} %get-tuple-element.45.refs_0_.refs_4_, bf16[1024,512]{1,0:T(8,128)(2,1)} %get-tuple-element.46.refs_1_.refs_5_, bf16[1040,512]{1,0:T(8,128)(2,1)} %copy-done.8, bf16[1024,512]{1,0:T(8,128)(2,1)} %collective-permute-done.14.refs_0_.refs_3_, ...), custom_call_target="tpu_custom_call" | custom-call | flops 3221225472 | bytes 19922944 | tf_op jit(solution)/shard_map/pallas_call | solution.py:576
  247.3 3.1 %shard_map.96 = (bf16[1024,512]{1,0:T(8,128)(2,1)S(1)}, bf16[1024,512]{1,0:T(8,128)(2,1)}, bf16[1040,512]{1,0:T(8,128)(2,1)S(1)}) custom-call(s32[1]{0:T(128)} %dynamic_slice.12.flag_ref, bf16[3088,512]{1,0:T(8,128)(2,1)} %collective-permute-done.12.a_ref.b_ref, bf16[3088,512]{1,0:T(8,128)(2,1)} %collective-permute-done.12.a_ref.b_ref, ...), custom_call_target="tpu_custom_call" | custom-call | bytes 6324224 | tf_op jit(solution)/shard_map/pallas_call | solution.py:413
  251.1 4.1 %shard_map.97.refs_1_.refs_6_ = bf16[1,512,512]{2,1,0:T(8,128)(2,1)S(1)} custom-call(f32[12,3]{1,0:T(8,128)S(1)} %copy.44.scalars, bf16[1024,512]{1,0:T(8,128)(2,1)S(1)} %get-tuple-element.48.refs_0_.refs_4_, bf16[1024,512]{1,0:T(8,128)(2,1)} %get-tuple-element.49.refs_1_.refs_5_, bf16[1040,512]{1,0:T(8,128)(2,1)S(1)} %get-tuple-element.50.refs_2_.refs_6_, ...), custom_call_target="tpu_custom_call" | custom-call | flops 1610612736 | bytes 6815744 | tf_op jit(solution)/shard_map/pallas_call | solution.py:255
  256.0 2.9 %collective-permute-done.21.refs_0_.refs_11_ = bf16[1536,512]{1,0:T(8,128)(2,1)} collective-permute-done((bf16[1536,512]{1,0:T(8,128)(2,1)}, bf16[1536,512]{1,0:T(8,128)(2,1)}, u32[]{:S(2)}, u32[]{:S(2)}) %collective-permute-start.21) | collective-permute-done | bytes 1572896 | tf_op jit(solution)/shard_map/ppermute | solution.py:621
  260.2 5.7 %shard_map.99.refs_7_.refs_8_ = bf16[1,512,512]{2,1,0:T(8,128)(2,1)S(1)} custom-call(f32[12,3]{1,0:T(8,128)S(1)} %copy.44.scalars, bf16[1024,512]{1,0:T(8,128)(2,1)} %collective-permute-done.18.refs_0_.refs_3_, bf16[1024,512]{1,0:T(8,128)(2,1)} %collective-permute-done.19.refs_1_.refs_4_, bf16[1040,512]{1,0:T(8,128)(2,1)} %collective-permute-done.20.refs_2_.refs_5_, ...), custom_call_target="tpu_custom_call" | custom-call | flops 1610612736 | bytes 6815744 | tf_op jit(solution)/shard_map/pallas_call | solution.py:255
  265.9 11.9 %shard_map.100 = f32[3072,512]{1,0:T(8,128)} custom-call(bf16[1024,512]{1,0:T(8,128)(2,1)S(1)} %get-tuple-element.48.refs_0_.refs_4_, bf16[1024,512]{1,0:T(8,128)(2,1)} %get-tuple-element.49.refs_1_.refs_5_, bf16[1040,512]{1,0:T(8,128)(2,1)} %copy-done.9, bf16[1024,512]{1,0:T(8,128)(2,1)} %collective-permute-done.18.refs_0_.refs_3_, ...), custom_call_target="tpu_custom_call" | custom-call | flops 3221225472 | bytes 26214400 | tf_op jit(solution)/shard_map/pallas_call | solution.py:576
  (94 shorter events, 13.4 us)
Async XLA Ops:
  3.8 13.6 %collective-permute-start.2 = (bf16[3088,512]{1,0:T(8,128)(2,1)}, bf16[3088,512]{1,0:T(8,128)(2,1)}, u32[]{:S(2)}, u32[]{:S(2)}) collective-permute-start(bf16[3088,512]{1,0:T(8,128)(2,1)} %get-tuple-element.34.refs_0_.b_ref.refs_9_), channel_id=1, source_target_pairs={{0,2},{2,0},{4,6},{6,4},{8,10},{10,8},{12,14},{14,12},{16,18},{18,... | collective-permute-start | bytes 9486344 | tf_op jit(solution)/shard_map/ppermute | solution.py:609
  4.5 37.5 %collective-permute-start = (bf16[3088,512]{1,0:T(8,128)(2,1)}, bf16[3088,512]{1,0:T(8,128)(2,1)}, u32[]{:S(2)}, u32[]{:S(2)}) collective-permute-start(bf16[3088,512]{1,0:T(8,128)(2,1)} %get-tuple-element.34.refs_0_.b_ref.refs_9_), channel_id=1, source_target_pairs={{0,6},{2,26},{4,12},{6,0},{8,14},{10,2},{12,20},{14,8},{16,22},{18... | collective-permute-start | bytes 9486344 | tf_op jit(solution)/shard_map/ppermute | solution.py:609
  4.5 34.4 %collective-permute-start.1 = (bf16[1536,512]{1,0:T(8,128)(2,1)S(1)}, bf16[1536,512]{1,0:T(8,128)(2,1)}, u32[]{:S(2)}, u32[]{:S(2)}) collective-permute-start(bf16[1536,512]{1,0:T(8,128)(2,1)S(1)} %get-tuple-element.35), channel_id=1, source_target_pairs={{0,1},{1,0},{2,3},{3,2},{4,5},{5,4},{6,7},{7,6},{8,9},{9,8},{10,11... | collective-permute-start | bytes 4718600 | tf_op jit(solution)/shard_map/ppermute | solution.py:621
  6.0 6.3 %copy-start.24 = (f32[16]{0:T(128)S(1)}, f32[16]{0:T(128)}, u32[]{:S(2)}) copy-start(f32[16]{0:T(128)} %param.11) | copy-start | bytes 196
  6.0 6.3 %copy-start.25 = (s32[16]{0:T(128)S(1)}, s32[16]{0:T(128)}, u32[]{:S(2)}) copy-start(s32[16]{0:T(128)} %param.10) | copy-start | bytes 196
  6.0 6.9 %copy-start.23 = (f32[1024]{0:T(1024)S(1)}, f32[1024]{0:T(1024)}, u32[]{:S(2)}) copy-start(f32[1024]{0:T(1024)} %param.12) | copy-start | bytes 12292
  6.0 8.0 %copy-start.26 = (s32[16]{0:T(128)S(1)}, s32[16]{0:T(128)}, u32[]{:S(2)}) copy-start(s32[16]{0:T(128)} %constant.53.clone) | copy-start | bytes 196
  14.0 3.4 %copy-start.4 = (f32[2,512,1]{2,1,0:T(8,128)S(1)}, f32[2,512,1]{2,1,0:T(8,128)}, u32[]{:S(2)}) copy-start(f32[2,512,1]{2,1,0:T(8,128)} %copy.45.refs_3_.refs_4_.refs_9_.refs_8_.refs_5_.refs_7_) | copy-start | bytes 12292
  17.4 36.4 %copy-start = (bf16[512,3072]{1,0:T(8,128)(2,1)}, bf16[512,3072]{1,0:T(8,128)(2,1)S(1)}, u32[]{:S(2)}) copy-start(bf16[512,3072]{1,0:T(8,128)(2,1)S(1)} %slice_bitcast_fusion.refs_2_.refs_6_.refs_4_.refs_1_.refs_3_) | copy-start | bytes 9437188
  47.5 6.3 %collective-permute-start.5 = (bf16[3088,512]{1,0:T(8,128)(2,1)}, bf16[3088,512]{1,0:T(8,128)(2,1)}, u32[]{:S(2)}, u32[]{:S(2)}) collective-permute-start(bf16[3088,512]{1,0:T(8,128)(2,1)} %get-tuple-element.38.refs_0_.refs_2_), channel_id=1, source_target_pairs={{0,2},{2,0},{4,6},{6,4},{8,10},{10,8},{12,14},{14,12},{16,18},{18,... | collective-permute-start | bytes 9486344 | tf_op jit(solution)/shard_map/ppermute | solution.py:609
  48.2 38.4 %collective-permute-start.3 = (bf16[3088,512]{1,0:T(8,128)(2,1)}, bf16[3088,512]{1,0:T(8,128)(2,1)}, u32[]{:S(2)}, u32[]{:S(2)}) collective-permute-start(bf16[3088,512]{1,0:T(8,128)(2,1)} %get-tuple-element.36.refs_3_), channel_id=1, source_target_pairs={{0,24},{2,4},{4,2},{6,14},{8,0},{10,12},{12,10},{14,22},{16,8},{18... | collective-permute-start | bytes 9486344 | tf_op jit(solution)/shard_map/ppermute | solution.py:609
  48.9 11.7 %copy-start.3 = (bf16[3088,512]{1,0:T(8,128)(2,1)S(1)}, bf16[3088,512]{1,0:T(8,128)(2,1)}, u32[]{:S(2)}) copy-start(bf16[3088,512]{1,0:T(8,128)(2,1)} %get-tuple-element.34.refs_0_.b_ref.refs_9_) | copy-start | bytes 9486340
  48.9 36.7 %collective-permute-start.4 = (bf16[1552,512]{1,0:T(8,128)(2,1)S(1)}, bf16[1552,512]{1,0:T(8,128)(2,1)S(1)}, u32[]{:S(2)}, u32[]{:S(2)}) collective-permute-start(bf16[1552,512]{1,0:T(8,128)(2,1)S(1)} %get-tuple-element.37), channel_id=1, source_target_pairs={{0,1},{1,0},{2,3},{3,2},{4,5},{5,4},{6,7},{7,6},{8,9},{9,8},{10,11... | collective-permute-start | bytes 4767752 | tf_op jit(solution)/shard_map/ppermute | solution.py:621
  85.7 6.6 %copy-start.6 = (bf16[1552,512]{1,0:T(8,128)(2,1)}, bf16[1552,512]{1,0:T(8,128)(2,1)S(1)}, u32[]{:S(2)}) copy-start(bf16[1552,512]{1,0:T(8,128)(2,1)S(1)} %collective-permute-done.4.refs_0_.array_ref.refs_5_.refs_1_.refs_8_) | copy-start | bytes 4767748
  91.2 6.6 %collective-permute-start.7 = (bf16[3088,512]{1,0:T(8,128)(2,1)}, bf16[3088,512]{1,0:T(8,128)(2,1)S(1)}, u32[]{:S(2)}, u32[]{:S(2)}) collective-permute-start(bf16[3088,512]{1,0:T(8,128)(2,1)} %get-tuple-element.40.refs_0_.refs_2_), channel_id=1, source_target_pairs={{0,2},{2,0},{4,6},{6,4},{8,10},{10,8},{12,14},{14,12},{16,18},{18,... | collective-permute-start | bytes 9486344 | tf_op jit(solution)/shard_map/ppermute | solution.py:609
  92.3 38.3 %collective-permute-start.6 = (bf16[3088,512]{1,0:T(8,128)(2,1)}, bf16[3088,512]{1,0:T(8,128)(2,1)S(1)}, u32[]{:S(2)}, u32[]{:S(2)}) collective-permute-start(bf16[3088,512]{1,0:T(8,128)(2,1)} %get-tuple-element.39.refs_0_), channel_id=1, source_target_pairs={{0,6},{2,10},{4,28},{6,0},{8,14},{10,18},{12,4},{14,8},{16,22},{18... | collective-permute-start | bytes 9486344 | tf_op jit(solution)/shard_map/ppermute | solution.py:609
  93.0 25.1 %copy-start.7 = (bf16[1552,512]{1,0:T(8,128)(2,1)S(1)}, bf16[1552,512]{1,0:T(8,128)(2,1)}, u32[]{:S(2)}) copy-start(bf16[1552,512]{1,0:T(8,128)(2,1)} %copy-done.6) | copy-start | bytes 4767748
  97.8 1.7 copy-start.20
  130.6 1.7 copy-start.21
  134.9 4.5 %copy-start.2 = (bf16[3088,512]{1,0:T(8,128)(2,1)}, bf16[3088,512]{1,0:T(8,128)(2,1)S(1)}, u32[]{:S(2)}) copy-start(bf16[3088,512]{1,0:T(8,128)(2,1)S(1)} %shard_map.83.refs_8_.refs_2_.refs_0_) | copy-start | bytes 9486340
  134.9 19.2 %collective-permute-start.8 = (bf16[3088,512]{1,0:T(8,128)(2,1)S(1)}, bf16[3088,512]{1,0:T(8,128)(2,1)}, u32[]{:S(2)}, u32[]{:S(2)}) collective-permute-start(bf16[3088,512]{1,0:T(8,128)(2,1)S(1)} %shard_map.83.refs_8_.refs_2_.refs_0_), channel_id=1, source_target_pairs={{0,2},{2,0},{4,6},{6,4},{8,10},{10,8},{12,14},{14,12},{16,18},{18,... | collective-permute-start | bytes 9486344 | tf_op jit(solution)/shard_map/ppermute | solution.py:609
  135.4 37.9 %collective-permute-start.9 = (bf16[3088,512]{1,0:T(8,128)(2,1)S(1)}, bf16[3088,512]{1,0:T(8,128)(2,1)}, u32[]{:S(2)}, u32[]{:S(2)}) collective-permute-start(bf16[3088,512]{1,0:T(8,128)(2,1)S(1)} %shard_map.83.refs_8_.refs_2_.refs_0_), channel_id=1, source_target_pairs={{0,8},{2,4},{4,2},{6,30},{8,16},{10,12},{12,10},{14,6},{16,24},{18... | collective-permute-start | bytes 9486344 | tf_op jit(solution)/shard_map/ppermute | solution.py:609
  138.9 15.2 %collective-permute-start.11 = (bf16[1552,512]{1,0:T(8,128)(2,1)S(1)}, bf16[1552,512]{1,0:T(8,128)(2,1)S(1)}, u32[]{:S(2)}, u32[]{:S(2)}) collective-permute-start(bf16[1552,512]{1,0:T(8,128)(2,1)S(1)} %copy-done.7), channel_id=1, source_target_pairs={{0,2},{2,0},{4,6},{6,4},{8,10},{10,8},{12,14},{14,12},{16,18},{18,... | collective-permute-start | bytes 4767752 | tf_op jit(solution)/shard_map/ppermute | solution.py:609
  138.9 15.2 %collective-permute-start.10 = (bf16[1536,512]{1,0:T(8,128)(2,1)}, bf16[1536,512]{1,0:T(8,128)(2,1)S(1)}, u32[]{:S(2)}, u32[]{:S(2)}) collective-permute-start(bf16[1536,512]{1,0:T(8,128)(2,1)} %collective-permute-done.1.refs_0_.array_ref.refs_4_.refs_7_), channel_id=1, source_target_pairs={{0,2},{2,0},{4,6},{6,4},{8,10},{10,8},{12,14},{14,12},{16,18},{18,... | collective-permute-start | bytes 4718600 | tf_op jit(solution)/shard_map/ppermute | solution.py:609
  153.8 62.7 %collective-permute-start.13 = (bf16[3088,512]{1,0:T(8,128)(2,1)}, bf16[3088,512]{1,0:T(8,128)(2,1)}, u32[]{:S(2)}, u32[]{:S(2)}) collective-permute-start(bf16[3088,512]{1,0:T(8,128)(2,1)} %get-tuple-element.43), channel_id=1, source_target_pairs={{0,8},{2,4},{4,2},{6,30},{8,16},{10,12},{12,10},{14,6},{16,24},{18... | collective-permute-start | bytes 9486344 | tf_op jit(solution)/shard_map/ppermute | solution.py:609
  154.1 1.2 copy-start.14
  169.3 1.1 copy-start.16
  185.1 62.1 %collective-permute-start.12 = (bf16[3088,512]{1,0:T(8,128)(2,1)}, bf16[3088,512]{1,0:T(8,128)(2,1)}, u32[]{:S(2)}, u32[]{:S(2)}) collective-permute-start(bf16[3088,512]{1,0:T(8,128)(2,1)} %get-tuple-element.42), channel_id=1, source_target_pairs={{0,8},{2,4},{4,2},{6,30},{8,16},{10,12},{12,10},{14,6},{16,24},{18... | collective-permute-start | bytes 9486344 | tf_op jit(solution)/shard_map/ppermute | solution.py:609
  189.0 8.9 %copy-start.1 = (bf16[512,3072]{1,0:T(8,128)(2,1)S(1)}, bf16[512,3072]{1,0:T(8,128)(2,1)}, u32[]{:S(2)}) copy-start(bf16[512,3072]{1,0:T(8,128)(2,1)} %copy-done) | copy-start | bytes 9437188
  189.0 32.7 %collective-permute-start.17 = (bf16[1536,512]{1,0:T(8,128)(2,1)S(1)}, bf16[1536,512]{1,0:T(8,128)(2,1)S(1)}, u32[]{:S(2)}, u32[]{:S(2)}) collective-permute-start(bf16[1536,512]{1,0:T(8,128)(2,1)S(1)} %get-tuple-element.44.refs_6_), channel_id=1, source_target_pairs={{0,1},{1,0},{2,3},{3,2},{4,5},{5,4},{6,7},{7,6},{8,9},{9,8},{10,11... | collective-permute-start | bytes 4718600 | tf_op jit(solution)/shard_map/ppermute | solution.py:621
  198.0 5.0 %copy-start.15 = (bf16[1552,512]{1,0:T(8,128)(2,1)S(1)}, bf16[1552,512]{1,0:T(8,128)(2,1)}, u32[]{:S(2)}) copy-start(bf16[1552,512]{1,0:T(8,128)(2,1)} %copy-done.14) | copy-start | bytes 4767748
  198.0 5.0 %copy-start.17 = (bf16[1536,512]{1,0:T(8,128)(2,1)S(1)}, bf16[1536,512]{1,0:T(8,128)(2,1)}, u32[]{:S(2)}) copy-start(bf16[1536,512]{1,0:T(8,128)(2,1)} %copy-done.16) | copy-start | bytes 4718596
  219.7 8.4 %copy-start.8 = (bf16[1040,512]{1,0:T(8,128)(2,1)}, bf16[1040,512]{1,0:T(8,128)(2,1)S(1)}, u32[]{:S(2)}) copy-start(bf16[1040,512]{1,0:T(8,128)(2,1)S(1)} %get-tuple-element.47.refs_2_.refs_6_) | copy-start | bytes 3194884
  219.7 9.9 %collective-permute-start.16 = (bf16[1040,512]{1,0:T(8,128)(2,1)S(1)}, bf16[1040,512]{1,0:T(8,128)(2,1)}, u32[]{:S(2)}, u32[]{:S(2)}) collective-permute-start(bf16[1040,512]{1,0:T(8,128)(2,1)S(1)} %get-tuple-element.47.refs_2_.refs_6_), channel_id=1, source_target_pairs={{0,2},{2,0},{4,6},{6,4},{8,10},{10,8},{12,14},{14,12},{16,18},{18,... | collective-permute-start | bytes 3194888 | tf_op jit(solution)/shard_map/ppermute | solution.py:609
  219.8 9.8 %collective-permute-start.14 = (bf16[1024,512]{1,0:T(8,128)(2,1)S(1)}, bf16[1024,512]{1,0:T(8,128)(2,1)}, u32[]{:S(2)}, u32[]{:S(2)}) collective-permute-start(bf16[1024,512]{1,0:T(8,128)(2,1)S(1)} %get-tuple-element.45.refs_0_.refs_4_), channel_id=1, source_target_pairs={{0,2},{2,0},{4,6},{6,4},{8,10},{10,8},{12,14},{14,12},{16,18},{18,... | collective-permute-start | bytes 3145736 | tf_op jit(solution)/shard_map/ppermute | solution.py:609
  220.3 9.3 %copy-start.5 = (f32[2,512,1]{2,1,0:T(8,128)S(1)}, f32[2,512,1]{2,1,0:T(8,128)}, u32[]{:S(2)}) copy-start(f32[2,512,1]{2,1,0:T(8,128)} %copy.45.refs_3_.refs_4_.refs_9_.refs_8_.refs_5_.refs_7_) | copy-start | bytes 12292
  220.3 9.3 %collective-permute-start.15 = (bf16[1024,512]{1,0:T(8,128)(2,1)}, bf16[1024,512]{1,0:T(8,128)(2,1)}, u32[]{:S(2)}, u32[]{:S(2)}) collective-permute-start(bf16[1024,512]{1,0:T(8,128)(2,1)} %get-tuple-element.46.refs_1_.refs_5_), channel_id=1, source_target_pairs={{0,2},{2,0},{4,6},{6,4},{8,10},{10,8},{12,14},{14,12},{16,18},{18,... | collective-permute-start | bytes 3145736 | tf_op jit(solution)/shard_map/ppermute | solution.py:609
  221.7 1.1 copy-start.22
  222.8 36.1 %collective-permute-start.21 = (bf16[1536,512]{1,0:T(8,128)(2,1)}, bf16[1536,512]{1,0:T(8,128)(2,1)}, u32[]{:S(2)}, u32[]{:S(2)}) collective-permute-start(bf16[1536,512]{1,0:T(8,128)(2,1)} %shard_map.88.refs_2_), channel_id=1, source_target_pairs={{0,1},{1,0},{2,3},{3,2},{4,5},{5,4},{6,7},{7,6},{8,9},{9,8},{10,11... | collective-permute-start | bytes 4718600 | tf_op jit(solution)/shard_map/ppermute | solution.py:621
  228.2 0.8 copy-start.12
  229.6 6.5 %copy-start.13 = (bf16[1,512,512]{2,1,0:T(8,128)(2,1)S(1)}, bf16[1,512,512]{2,1,0:T(8,128)(2,1)}, u32[]{:S(2)}) copy-start(bf16[1,512,512]{2,1,0:T(8,128)(2,1)} %copy-done.12) | copy-start | bytes 1572868
  229.6 0.7 copy-start.19
  250.4 4.8 %copy-start.9 = (bf16[1040,512]{1,0:T(8,128)(2,1)}, bf16[1040,512]{1,0:T(8,128)(2,1)S(1)}, u32[]{:S(2)}) copy-start(bf16[1040,512]{1,0:T(8,128)(2,1)S(1)} %get-tuple-element.50.refs_2_.refs_6_) | copy-start | bytes 3194884
  250.4 9.1 %collective-permute-start.20 = (bf16[1040,512]{1,0:T(8,128)(2,1)S(1)}, bf16[1040,512]{1,0:T(8,128)(2,1)}, u32[]{:S(2)}, u32[]{:S(2)}) collective-permute-start(bf16[1040,512]{1,0:T(8,128)(2,1)S(1)} %get-tuple-element.50.refs_2_.refs_6_), channel_id=1, source_target_pairs={{0,2},{2,0},{4,6},{6,4},{8,10},{10,8},{12,14},{14,12},{16,18},{18,... | collective-permute-start | bytes 3194888 | tf_op jit(solution)/shard_map/ppermute | solution.py:609
  250.5 9.0 %collective-permute-start.18 = (bf16[1024,512]{1,0:T(8,128)(2,1)S(1)}, bf16[1024,512]{1,0:T(8,128)(2,1)}, u32[]{:S(2)}, u32[]{:S(2)}) collective-permute-start(bf16[1024,512]{1,0:T(8,128)(2,1)S(1)} %get-tuple-element.48.refs_0_.refs_4_), channel_id=1, source_target_pairs={{0,2},{2,0},{4,6},{6,4},{8,10},{10,8},{12,14},{14,12},{16,18},{18,... | collective-permute-start | bytes 3145736 | tf_op jit(solution)/shard_map/ppermute | solution.py:609
  251.0 8.5 %collective-permute-start.19 = (bf16[1024,512]{1,0:T(8,128)(2,1)}, bf16[1024,512]{1,0:T(8,128)(2,1)}, u32[]{:S(2)}, u32[]{:S(2)}) collective-permute-start(bf16[1024,512]{1,0:T(8,128)(2,1)} %get-tuple-element.49.refs_1_.refs_5_), channel_id=1, source_target_pairs={{0,2},{2,0},{4,6},{6,4},{8,10},{10,8},{12,14},{14,12},{16,18},{18,... | collective-permute-start | bytes 3145736 | tf_op jit(solution)/shard_map/ppermute | solution.py:609
  255.2 0.8 copy-start.10
  259.5 6.4 %copy-start.11 = (bf16[1,512,512]{2,1,0:T(8,128)(2,1)S(1)}, bf16[1,512,512]{2,1,0:T(8,128)(2,1)}, u32[]{:S(2)}) copy-start(bf16[1,512,512]{2,1,0:T(8,128)(2,1)} %copy-done.10) | copy-start | bytes 1572868
  (1 other events, 0.7 us)
where the time goes:
time: 280 us; the launch traced here: 278 us
  Pallas kernels  192 us (69%)
  waiting for transfers between devices  44.9 us (16%)
  local copies, waits for them, and re-layouts  19.4 us (7%)
  starting transfers between devices  18.3 us (7%)
    pallas_call x8, Pallas kernels, density_call(): pl.pallas_call(kernel, grid=(steps,), in_specs=[pl.BlockSpec(memory_space...  89.6 us
    pallas_call x10, Pallas kernels, amplitude_call(): pl.pallas_call(kernel, grid=(len(jobs),), in_specs=[pl.BlockSpec(memory_s...  75.9 us
    ppermute x4, waiting for transfers between devices, sibling(): return lax.ppermute(array, 'narrow', [(0, 1), (1, 0)])  29.6 us
    pallas_call x5, Pallas kernels, choice_call(): pl.pallas_call(kernel, in_specs=[pl.BlockSpec(memory_space=pltpu.SMEM)] +...  19.1 us
    ppermute x18, waiting for transfers between devices, moved(): sent = [lax.ppermute(piece, 'wide', pairs) for piece in slab.pieces]  15.3 us
    ppermute x18, starting transfers between devices, moved(): sent = [lax.ppermute(piece, 'wide', pairs) for piece in slab.pieces]  13.1 us
    unnamed x54, local copies, waits for them, and re-layouts  9.89 us
  transfers between devices with their start and end apart: 22, of which 9 were waited for; matrix products, arithmetic and copies ran while one was open for 4% of the time, Pallas kernels for 57%

commit v1 on v0

--- a/solution.py
+++ b/solution.py
@@ -705,16 +705,15 @@
     mate_far = swapped(own_far)
     rows_far.append(turn_call(parts[1], aux - cut, [sent3.array]))
     jobs = [(r2, near), (r2, far), (s2, far), (s2, near), (r1, far), (s1, far)]
-    jobs += [(own_far, near)]
     done = amps(jobs, [rows_near, rows_far])
-    part = density([own_far, r2, s2], near, [[part]], f32, done)
+    part = density([r2, s2], near, [[part]], f32, done)
 
     r3 = Slab(copied(r3.array, part), r3.ids)
     r4 = moved(r3, routes.rounds[3])
     s3 = swapped(r3)
     out_part, again = density([r1, s1, r2, s2], far, [], f32, r3.array, copied=own.pieces)
     r5 = moved(Slab(again, own.ids), routes.rounds[4])
-    jobs = [(mate_far, near), (r3, near), (r3, far), (s3, far), (s3, near)]
+    jobs = [(own_far, near), (mate_far, near), (r3, near), (r3, far), (s3, far), (s3, near)]
     done = amps(jobs, [rows_near, rows_far], out_part)
 
     done = amps([(r4, far)], [rows_near, rows_far], done)
@@ -727,19 +726,17 @@
     sent1 = density(slabs, far, [[out_part]], bf16, sent0, rows=(half, half))
     incoming = [sibling(sent0), sibling(sent1)]
     done = amps([(r4, near)], [rows_near], sent1)
-    part = density([mate_far, r3, s3, r4], near, [[part]], f32, done)
 
     thirds = [aux // 3, aux // 3 * 2]
-    r5 = Slab(copied(r5.array, part, cuts=thirds), r5.ids)
+    r5 = Slab(copied(r5.array, done, cuts=thirds), r5.ids)
     s5 = swapped(r5)
     done = amps([(r5, near)], [rows_near], *r5.pieces)
     done = join_call([incoming[0], done])
     done = amps([(s5, near)], [rows_near], done)
-    part = density([r5, s5], near, [[part]], f32, done)
+    part = density([own_far, mate_far, r3, s3, r4, r5, s5], near, [[part]], f32, done)
     r6 = Slab(copied(r6.array, part, cuts=thirds), r6.ids, 1)
     s6 = swapped(r6)
     done = amps([(r6, near)], [rows_near], *r6.pieces)
-    done = join_call([incoming[1], done])
     done = amps([(s6, near)], [rows_near], done)
     return density([r6, s6], near, [[part], incoming], f32, done)[None]
 

time: 280 us -> 277 us (0.989)
  Pallas kernels: 192 us -> 180 us
  waiting for transfers between devices: 44.9 us -> 51.8 us
    pallas_call x8 -> x7, Pallas kernels: 89.6 us -> 80 us  [density_call(): pl.pallas_call(kernel, grid=(steps,), in_specs=[pl.BlockSpec(memory_space...]
    ppermute x18, waiting for transfers between devices: 15.3 us -> 19.2 us  [moved(): sent = [lax.ppermute(piece, 'wide', pairs) for piece in slab.pieces]]
    ppermute x4, waiting for transfers between devices: 29.6 us -> 32.7 us  [sibling(): return lax.ppermute(array, 'narrow', [(0, 1), (1, 0)])]
    unnamed x54 -> x68, local copies, waits for them, and re-layouts: 9.89 us -> 10.9 us
  transfers between devices with their start and end apart: 22 -> 22, of which waited for: 9 -> 11; matrix products, arithmetic and copies ran while one was open for 4% -> 4% of each run, Pallas kernels for 57% -> 56%
where the time goes in v1:
time: 277 us; the launch traced here: 275 us
  Pallas kernels  180 us (65%)
  waiting for transfers between devices  51.8 us (19%)
  local copies, waits for them, and re-layouts  20.5 us (7%)
  starting transfers between devices  18.7 us (7%)
    pallas_call x7, Pallas kernels, density_call(): pl.pallas_call(kernel, grid=(steps,), in_specs=[pl.BlockSpec(memory_space...  80 us
    pallas_call x10, Pallas kernels, amplitude_call(): pl.pallas_call(kernel, grid=(len(jobs),), in_specs=[pl.BlockSpec(memory_s...  74.6 us
    ppermute x4, waiting for transfers between devices, sibling(): return lax.ppermute(array, 'narrow', [(0, 1), (1, 0)])  32.7 us
    ppermute x18, waiting for transfers between devices, moved(): sent = [lax.ppermute(piece, 'wide', pairs) for piece in slab.pieces]  19.2 us
    pallas_call x5, Pallas kernels, choice_call(): pl.pallas_call(kernel, in_specs=[pl.BlockSpec(memory_space=pltpu.SMEM)] +...  19.1 us
    ppermute x18, starting transfers between devices, moved(): sent = [lax.ppermute(piece, 'wide', pairs) for piece in slab.pieces]  13.6 us
    unnamed x68, local copies, waits for them, and re-layouts  10.9 us
    pallas_call x1, local copies, waits for them, and re-layouts, append_call(): pl.pallas_call(kernel, in_specs=[pl.BlockSpec(memory_space=pl.ANY)] * 2,...  5.6 us
  transfers between devices with their start and end apart: 22, of which 11 were waited for; matrix products, arithmetic and copies ran while one was open for 4% of the time, Pallas kernels for 56%

profile of v1, /device:TPU:3, one launch (start us, length us, event | category | flops | bytes accessed | tf_op | source)
XLA Modules:
  0.0 274.9 jit_solution(17513040104280846967)
XLA Ops:
  0.7 3.0 %shard_map.73 = (bf16[3088,512]{1,0:T(8,128)(2,1)}, bf16[1536,512]{1,0:T(8,128)(2,1)S(1)}, bf16[1552,512]{1,0:T(8,128)(2,1)S(1)}) custom-call(bf16[3072,512]{1,0:T(8,128)(2,1)} %bitcast.20, bf16[16,512]{1,0:T(8,128)(2,1)S(1)} %scatter.4.tail_ref), custom_call_target="tpu_custom_call" | custom-call | tf_op jit(solution)/shard_map/pallas_call | solution.py:355
  4.5 1.4 collective-permute-start.1
  5.9 5.6 %copy.43 = bf16[3088,512]{0,1:T(8,128)(2,1)} copy(bf16[3088,512]{1,0:T(8,128)(2,1)} %get-tuple-element.34.refs_0_.b_ref.refs_9_) | data formatting | bytes 6324224 | tf_op jit(solution)/shard_map/pallas_call | solution.py:355
  12.9 1.0 copy.45.refs_3_.refs_4_.refs_7_.refs_10_.refs_5_
  15.3 2.1 slice_bitcast_fusion.refs_2_.refs_4_.refs_6_.refs_1_.refs_3_
  17.4 7.1 %shard_map.74.refs_1_.refs_4_.refs_5_ = bf16[2,512,512]{2,1,0:T(8,128)(2,1)S(1)} custom-call(f32[12,3]{1,0:T(8,128)S(1)} %copy.44.scalars, bf16[3088,512]{1,0:T(8,128)(2,1)} %get-tuple-element.34.refs_0_.b_ref.refs_9_, bf16[3088,512]{1,0:T(8,128)(2,1)} %collective-permute-done.2.refs_1_, ...), custom_call_target="tpu_custom_call" | custom-call | flops 3221225472 | bytes 10485760 | tf_op jit(solution)/shard_map/pallas_call | solution.py:255
  24.5 14.3 %collective-permute-done.1.refs_0_.array_ref.refs_7_ = bf16[1536,512]{1,0:T(8,128)(2,1)} collective-permute-done((bf16[1536,512]{1,0:T(8,128)(2,1)S(1)}, bf16[1536,512]{1,0:T(8,128)(2,1)}, u32[]{:S(2)}, u32[]{:S(2)}) %collective-permute-start.1) | collective-permute-done | bytes 1572896 | tf_op jit(solution)/shard_map/ppermute | solution.py:621
  38.8 3.1 %collective-permute-done.a_ref = bf16[3088,512]{1,0:T(8,128)(2,1)} collective-permute-done((bf16[3088,512]{1,0:T(8,128)(2,1)}, bf16[3088,512]{1,0:T(8,128)(2,1)}, u32[]{:S(2)}, u32[]{:S(2)}) %collective-permute-start) | collective-permute-done | bytes 3162144 | tf_op jit(solution)/shard_map/ppermute | solution.py:609
  41.9 5.5 %shard_map.75 = (bf16[3088,512]{1,0:T(8,128)(2,1)}, bf16[3088,512]{1,0:T(8,128)(2,1)}) custom-call(s32[1]{0:T(128)S(6)} %sub.6.flag_ref, bf16[3088,512]{1,0:T(8,128)(2,1)} %collective-permute-done.a_ref, bf16[3088,512]{1,0:T(8,128)(2,1)} %get-tuple-element.34.refs_0_.b_ref.refs_9_, bf16[1536,512]{1,0:T(8,128)(2,1)} %collective-permute-done.1.refs_0_.array_ref.refs_7_, ...), custom_call_target="tpu_custom_call" | custom-call | bytes 6324224 | tf_op jit(solution)/shard_map/pallas_call | solution.py:413
  48.8 1.2 collective-permute-start.4
  50.1 3.7 %collective-permute-done.5.refs_1_.refs_3_ = bf16[3088,512]{1,0:T(8,128)(2,1)} collective-permute-done((bf16[3088,512]{1,0:T(8,128)(2,1)}, bf16[3088,512]{1,0:T(8,128)(2,1)}, u32[]{:S(2)}, u32[]{:S(2)}) %collective-permute-start.5) | collective-permute-done | bytes 3162144 | tf_op jit(solution)/shard_map/ppermute | solution.py:609
  53.8 6.8 %shard_map.76.refs_6_.refs_7_.refs_8_ = bf16[2,512,512]{2,1,0:T(8,128)(2,1)S(1)} custom-call(f32[12,3]{1,0:T(8,128)S(1)} %copy.44.scalars, bf16[3088,512]{1,0:T(8,128)(2,1)} %get-tuple-element.38.refs_0_.refs_2_, bf16[3088,512]{1,0:T(8,128)(2,1)} %collective-permute-done.5.refs_1_.refs_3_, ...), custom_call_target="tpu_custom_call" | custom-call | flops 3221225472 | bytes 10485760 | tf_op jit(solution)/shard_map/pallas_call | solution.py:255
  60.6 11.4 %shard_map.77.refs_0_.refs_5_ = f32[3072,512]{1,0:T(8,128)} custom-call(bf16[3088,512]{1,0:T(8,128)(2,1)S(1)} %copy-done.5, bf16[3088,512]{1,0:T(8,128)(2,1)} %collective-permute-done.2.refs_1_, bf16[3088,512]{1,0:T(8,128)(2,1)} %get-tuple-element.38.refs_0_.refs_2_, bf16[3088,512]{1,0:T(8,128)(2,1)} %collective-permute-done.5.refs_1_.refs_3_, ...), custom_call_target="tpu_custom_call" | custom-call | flops 6442450944 | bytes 20971520 | tf_op jit(solution)/shard_map/pallas_call | solution.py:576
  72.0 2.6 shard_map.78.refs_1_.refs_5_.refs_7_.refs_2_
  74.5 11.1 %collective-permute-done.4.refs_0_.array_ref.refs_1_.refs_8_ = bf16[1552,512]{1,0:T(8,128)(2,1)S(1)} collective-permute-done((bf16[1552,512]{1,0:T(8,128)(2,1)S(1)}, bf16[1552,512]{1,0:T(8,128)(2,1)S(1)}, u32[]{:S(2)}, u32[]{:S(2)}) %collective-permute-start.4) | collective-permute-done | bytes 1589280 | tf_op jit(solution)/shard_map/ppermute | solution.py:621
  86.5 4.6 %shard_map.79 = (bf16[3088,512]{1,0:T(8,128)(2,1)}, bf16[3088,512]{1,0:T(8,128)(2,1)}) custom-call(s32[1]{0:T(128)} %dynamic_slice.12.flag_ref, bf16[3088,512]{1,0:T(8,128)(2,1)} %collective-permute-done.3.a_ref, bf16[3088,512]{1,0:T(8,128)(2,1)} %get-tuple-element.34.refs_0_.b_ref.refs_9_, ...), custom_call_target="tpu_custom_call" | custom-call | bytes 6324224 | tf_op jit(solution)/shard_map/pallas_call | solution.py:413
  91.2 1.0 collective-permute-start.7
  92.9 4.8 %collective-permute-done.7.refs_1_.refs_3_ = bf16[3088,512]{1,0:T(8,128)(2,1)S(1)} collective-permute-done((bf16[3088,512]{1,0:T(8,128)(2,1)}, bf16[3088,512]{1,0:T(8,128)(2,1)S(1)}, u32[]{:S(2)}, u32[]{:S(2)}) %collective-permute-start.7) | collective-permute-done | bytes 3162144 | tf_op jit(solution)/shard_map/ppermute | solution.py:609
  97.7 1.6 copy-done.26
  99.4 16.5 %shard_map.81.refs_2_.refs_3_.refs_4_.refs_5_.refs_6_.refs_7_ = bf16[6,512,512]{2,1,0:T(8,128)(2,1)} custom-call(f32[12,3]{1,0:T(8,128)S(1)} %copy.44.scalars, bf16[3088,512]{1,0:T(8,128)(2,1)} %get-tuple-element.40.refs_0_.refs_2_, bf16[3088,512]{1,0:T(8,128)(2,1)} %copy-done.26, bf16[3088,512]{1,0:T(8,128)(2,1)} %get-tuple-element.38.refs_0_.refs_2_, ...), custom_call_target="tpu_custom_call" | custom-call | flops 9663676416 | bytes 22020096 | tf_op jit(solution)/shard_map/pallas_call | solution.py:255
  115.9 1.9 copy-done.2
  117.8 11.2 %shard_map.82.refs_0_.refs_21_ = f32[3072,512]{1,0:T(8,128)} custom-call(bf16[3088,512]{1,0:T(8,128)(2,1)} %get-tuple-element.40.refs_0_.refs_2_, bf16[3088,512]{1,0:T(8,128)(2,1)} %copy-done.26, bf16[6,512,512]{2,1,0:T(8,128)(2,1)S(1)} %copy-done.2, bf16[6,512,512]{2,1,0:T(8,128)(2,1)S(1)} %copy-done.2, bf16[6,512,512]{2,1,0:T(8,128)(2,1)S(1)} %copy-done.2, ...), custom_call_target="tpu_custom_call" | custom-call | flops 3221225472 | bytes 19922944 | tf_op jit(solution)/shard_map/pallas_call | solution.py:576
  129.6 1.7 copy-done.27
  131.3 3.1 %shard_map.83.refs_8_.refs_4_.refs_0_ = bf16[3088,512]{1,0:T(8,128)(2,1)S(1)} custom-call(s32[1]{0:T(128)} %dynamic_slice.12.flag_ref, bf16[3088,512]{1,0:T(8,128)(2,1)} %copy-done.27, bf16[3088,512]{1,0:T(8,128)(2,1)} %copy-done.27, f32[3072,512]{1,0:T(8,128)} %shard_map.82.refs_0_.refs_21_), custom_call_target="tpu_custom_call" | custom-call | bytes 6324224 | tf_op jit(solution)/shard_map/pallas_call | solution.py:413
  135.0 3.9 %collective-permute-start.9 = (bf16[3088,512]{1,0:T(8,128)(2,1)S(1)}, bf16[3088,512]{1,0:T(8,128)(2,1)S(1)}, u32[]{:S(2)}, u32[]{:S(2)}) collective-permute-start(bf16[3088,512]{1,0:T(8,128)(2,1)S(1)} %shard_map.83.refs_8_.refs_4_.refs_0_), channel_id=1, source_target_pairs={{0,8},{2,4},{4,2},{6,30},{8,16},{10,12},{12,10},{14,6},{16,24},{18... | collective-permute-start | bytes 9486344 | tf_op jit(solution)/shard_map/ppermute | solution.py:609
  139.5 13.5 %shard_map.84 = (f32[3072,512]{1,0:T(8,128)}, bf16[3088,512]{1,0:T(8,128)(2,1)}) custom-call(bf16[3088,512]{1,0:T(8,128)(2,1)} %get-tuple-element.38.refs_0_.refs_2_, bf16[3088,512]{1,0:T(8,128)(2,1)} %collective-permute-done.5.refs_1_.refs_3_, bf16[3088,512]{1,0:T(8,128)(2,1)} %get-tuple-element.40.refs_0_.refs_2_, bf16[3088,512]{1,0:T(8,128)(2,1)} %copy-done.26, ...), custom_call_target="tpu_custom_call" | custom-call | flops 6442450944 | bytes 20971520 | tf_op jit(solution)/shard_map/pallas_call | solution.py:576
  153.3 1.2 copy-done.29
  154.5 16.6 %shard_map.85.refs_4_.refs_3_.refs_13_.refs_14_.refs_15_.refs_16_ = bf16[6,512,512]{2,1,0:T(8,128)(2,1)} custom-call(f32[12,3]{1,0:T(8,128)S(1)} %copy.44.scalars, bf16[1536,512]{1,0:T(8,128)(2,1)} %collective-permute-done.1.refs_0_.array_ref.refs_7_, bf16[1552,512]{1,0:T(8,128)(2,1)} %copy-done.9, bf16[1536,512]{1,0:T(8,128)(2,1)S(1)} %collective-permute-done.10.refs_2_, ...), custom_call_target="tpu_custom_call" | custom-call | flops 9663676416 | bytes 22020096 | tf_op jit(solution)/shard_map/pallas_call | solution.py:255
  171.1 2.3 collective-permute-done.9.refs_0_.refs_2_.refs_6_
  173.3 1.7 copy-done.25
  175.1 4.8 %shard_map.86.refs_5_.refs_6_ = bf16[1,512,512]{2,1,0:T(8,128)(2,1)S(1)} custom-call(f32[12,3]{1,0:T(8,128)S(1)} %copy.44.scalars, bf16[3088,512]{1,0:T(8,128)(2,1)} %copy-done.25, bf16[512,3072]{1,0:T(8,128)(2,1)} %copy-done, bf16[512,1536]{1,0:T(8,128)(2,1)S(1)} %shard_map.78.refs_1_.refs_5_.refs_7_.refs_2_, bf16[512,1536]{1,0:T(8,128)(2,1)S(1)} %copy-done.17, ...), custom_call_target="tpu_custom_call" | custom-call | flops 1610612736 | bytes 9961472 | tf_op jit(solution)/shard_map/pallas_call | solution.py:255
  179.9 7.0 %shard_map.87 = (bf16[1536,512]{1,0:T(8,128)(2,1)S(1)}, bf16[3088,512]{1,0:T(8,128)(2,1)}) custom-call(bf16[3088,512]{1,0:T(8,128)(2,1)} %copy-done.4, bf16[3088,512]{1,0:T(8,128)(2,1)} %collective-permute-done.8.refs_5_.refs_1_, bf16[3088,512]{1,0:T(8,128)(2,1)} %copy-done.25, ...), custom_call_target="tpu_custom_call" | custom-call | flops 2415919104 | bytes 11010048 | tf_op jit(solution)/shard_map/pallas_call | solution.py:576
  187.0 3.8 %collective-permute-start.12 = (bf16[3088,512]{1,0:T(8,128)(2,1)}, bf16[3088,512]{1,0:T(8,128)(2,1)}, u32[]{:S(2)}, u32[]{:S(2)}) collective-permute-start(bf16[3088,512]{1,0:T(8,128)(2,1)} %get-tuple-element.42), channel_id=1, source_target_pairs={{0,8},{2,4},{4,2},{6,30},{8,16},{10,12},{12,10},{14,6},{16,24},{18... | collective-permute-start | bytes 9486344 | tf_op jit(solution)/shard_map/ppermute | solution.py:609
  190.7 1.2 collective-permute-start.17
  192.0 7.7 %shard_map.88.refs_2_ = bf16[1536,512]{1,0:T(8,128)(2,1)} custom-call(bf16[3088,512]{1,0:T(8,128)(2,1)} %copy-done.4, bf16[3088,512]{1,0:T(8,128)(2,1)} %collective-permute-done.8.refs_5_.refs_1_, bf16[3088,512]{1,0:T(8,128)(2,1)} %copy-done.25, bf16[6,512,512]{2,1,0:T(8,128)(2,1)} %shard_map.85.refs_4_.refs_3_.refs_13_.refs_14_.refs_15_.refs_16_, ...), custom_call_target="tpu_custom_call" | custom-call | flops 2415919104 | bytes 11010048 | tf_op jit(solution)/shard_map/pallas_call | solution.py:576
  199.7 4.8 %shard_map.89.refs_0_.refs_17_ = bf16[1,512,512]{2,1,0:T(8,128)(2,1)S(1)} custom-call(f32[12,3]{1,0:T(8,128)S(1)} %copy.44.scalars, bf16[3088,512]{1,0:T(8,128)(2,1)} %copy-done.25, bf16[512,3072]{1,0:T(8,128)(2,1)S(1)} %copy-done.1, bf16[1536,512]{1,0:T(8,128)(2,1)} %shard_map.88.refs_2_, f32[2,512,1]{2,1,0:T(8,128)S(1)} %copy-done.7, ...), custom_call_target="tpu_custom_call" | custom-call | flops 1610612736 | bytes 6815744 | tf_op jit(solution)/shard_map/pallas_call | solution.py:255
  204.5 2.8 %collective-permute-done.13.a_ref.b_ref = bf16[3088,512]{1,0:T(8,128)(2,1)} collective-permute-done((bf16[3088,512]{1,0:T(8,128)(2,1)}, bf16[3088,512]{1,0:T(8,128)(2,1)}, u32[]{:S(2)}, u32[]{:S(2)}) %collective-permute-start.13) | collective-permute-done | bytes 3162144 | tf_op jit(solution)/shard_map/ppermute | solution.py:609
  207.3 3.2 %shard_map.90 = (bf16[1024,512]{1,0:T(8,128)(2,1)S(1)}, bf16[1024,512]{1,0:T(8,128)(2,1)}, bf16[1040,512]{1,0:T(8,128)(2,1)S(1)}) custom-call(s32[1]{0:T(128)} %dynamic_slice.12.flag_ref, bf16[3088,512]{1,0:T(8,128)(2,1)} %collective-permute-done.13.a_ref.b_ref, bf16[3088,512]{1,0:T(8,128)(2,1)} %collective-permute-done.13.a_ref.b_ref, ...), custom_call_target="tpu_custom_call" | custom-call | bytes 6324224 | tf_op jit(solution)/shard_map/pallas_call | solution.py:413
  211.2 4.1 %shard_map.91.refs_1_.refs_18_ = bf16[1,512,512]{2,1,0:T(8,128)(2,1)S(1)} custom-call(f32[12,3]{1,0:T(8,128)S(1)} %copy.44.scalars, bf16[1024,512]{1,0:T(8,128)(2,1)S(1)} %get-tuple-element.45.refs_0_.refs_4_.refs_7_, bf16[1024,512]{1,0:T(8,128)(2,1)} %get-tuple-element.46.refs_1_.refs_5_.refs_8_, ...), custom_call_target="tpu_custom_call" | custom-call | flops 1610612736 | bytes 6815744 | tf_op jit(solution)/shard_map/pallas_call | solution.py:255
  216.1 7.3 %collective-permute-done.17.refs_0_.refs_10_ = bf16[1536,512]{1,0:T(8,128)(2,1)S(1)} collective-permute-done((bf16[1536,512]{1,0:T(8,128)(2,1)S(1)}, bf16[1536,512]{1,0:T(8,128)(2,1)S(1)}, u32[]{:S(2)}, u32[]{:S(2)}) %collective-permute-start.17) | collective-permute-done | bytes 1572896 | tf_op jit(solution)/shard_map/ppermute | solution.py:621
  223.5 1.1 copy-done.28
  224.6 1.2 collective-permute-start.21
  227.2 5.7 %shard_map.93.refs_19_.refs_20_ = bf16[1,512,512]{2,1,0:T(8,128)(2,1)S(1)} custom-call(f32[12,3]{1,0:T(8,128)S(1)} %copy.44.scalars, bf16[1024,512]{1,0:T(8,128)(2,1)} %collective-permute-done.14.refs_0_.refs_10_, bf16[1024,512]{1,0:T(8,128)(2,1)} %collective-permute-done.15.refs_1_.refs_11_, bf16[1040,512]{1,0:T(8,128)(2,1)} %collective-permute-done.16.refs_2_.refs_12_, ...), custom_call_target="tpu_custom_call" | custom-call | flops 1610612736 | bytes 6815744 | tf_op jit(solution)/shard_map/pallas_call | solution.py:255
  232.9 18.5 %shard_map.94.refs_0_.refs_9_ = f32[3072,512]{1,0:T(8,128)} custom-call(bf16[1536,512]{1,0:T(8,128)(2,1)} %collective-permute-done.1.refs_0_.array_ref.refs_7_, bf16[1552,512]{1,0:T(8,128)(2,1)} %copy-done.9, bf16[1536,512]{1,0:T(8,128)(2,1)} %copy-done.23, bf16[1552,512]{1,0:T(8,128)(2,1)} %copy-done.29, bf16[3088,512]{1,0:T(8,128)(2,1)} %copy-done.4, ...), custom_call_target="tpu_custom_call" | custom-call | flops 11274289152 | bytes 38273024 | tf_op jit(solution)/shard_map/pallas_call | solution.py:576
  251.4 2.7 shard_map.95
  254.8 4.1 %shard_map.96.refs_4_.refs_6_ = bf16[1,512,512]{2,1,0:T(8,128)(2,1)S(1)} custom-call(f32[12,3]{1,0:T(8,128)S(1)} %copy.44.scalars, bf16[1024,512]{1,0:T(8,128)(2,1)S(1)} %get-tuple-element.48.refs_0_.refs_4_, bf16[1024,512]{1,0:T(8,128)(2,1)S(1)} %get-tuple-element.49.refs_1_.refs_5_, bf16[1040,512]{1,0:T(8,128)(2,1)S(1)} %get-tuple-element.50.refs_2_.refs_6_, ...), custom_call_target="tpu_custom_call" | custom-call | flops 1610612736 | bytes 6815744 | tf_op jit(solution)/shard_map/pallas_call | solution.py:255
  259.9 4.1 %shard_map.97.refs_7_.refs_8_ = bf16[1,512,512]{2,1,0:T(8,128)(2,1)S(1)} custom-call(f32[12,3]{1,0:T(8,128)S(1)} %copy.44.scalars, bf16[1024,512]{1,0:T(8,128)(2,1)S(1)} %collective-permute-done.18.refs_0_.refs_3_, bf16[1024,512]{1,0:T(8,128)(2,1)S(1)} %collective-permute-done.19.refs_1_.refs_4_, ...), custom_call_target="tpu_custom_call" | custom-call | flops 1610612736 | bytes 6815744 | tf_op jit(solution)/shard_map/pallas_call | solution.py:255
  264.1 10.6 %shard_map.98 = f32[3072,512]{1,0:T(8,128)} custom-call(bf16[1024,512]{1,0:T(8,128)(2,1)S(1)} %get-tuple-element.48.refs_0_.refs_4_, bf16[1024,512]{1,0:T(8,128)(2,1)S(1)} %get-tuple-element.49.refs_1_.refs_5_, bf16[1040,512]{1,0:T(8,128)(2,1)} %copy-done.13, bf16[1024,512]{1,0:T(8,128)(2,1)S(1)} %collective-permute-done.18.refs_0_.refs_3_, ...), custom_call_target="tpu_custom_call" | custom-call | flops 3221225472 | bytes 26214400 | tf_op jit(solution)/shard_map/pallas_call | solution.py:576
  (106 shorter events, 13.0 us)
Async XLA Ops:
  3.7 13.7 %collective-permute-start.2 = (bf16[3088,512]{1,0:T(8,128)(2,1)}, bf16[3088,512]{1,0:T(8,128)(2,1)}, u32[]{:S(2)}, u32[]{:S(2)}) collective-permute-start(bf16[3088,512]{1,0:T(8,128)(2,1)} %get-tuple-element.34.refs_0_.b_ref.refs_9_), channel_id=1, source_target_pairs={{0,2},{2,0},{4,6},{6,4},{8,10},{10,8},{12,14},{14,12},{16,18},{18,... | collective-permute-start | bytes 9486344 | tf_op jit(solution)/shard_map/ppermute | solution.py:609
  4.5 37.5 %collective-permute-start = (bf16[3088,512]{1,0:T(8,128)(2,1)}, bf16[3088,512]{1,0:T(8,128)(2,1)}, u32[]{:S(2)}, u32[]{:S(2)}) collective-permute-start(bf16[3088,512]{1,0:T(8,128)(2,1)} %get-tuple-element.34.refs_0_.b_ref.refs_9_), channel_id=1, source_target_pairs={{0,6},{2,26},{4,12},{6,0},{8,14},{10,2},{12,20},{14,8},{16,22},{18... | collective-permute-start | bytes 9486344 | tf_op jit(solution)/shard_map/ppermute | solution.py:609
  4.5 34.4 %collective-permute-start.1 = (bf16[1536,512]{1,0:T(8,128)(2,1)S(1)}, bf16[1536,512]{1,0:T(8,128)(2,1)}, u32[]{:S(2)}, u32[]{:S(2)}) collective-permute-start(bf16[1536,512]{1,0:T(8,128)(2,1)S(1)} %get-tuple-element.35), channel_id=1, source_target_pairs={{0,1},{1,0},{2,3},{3,2},{4,5},{5,4},{6,7},{7,6},{8,9},{9,8},{10,11... | collective-permute-start | bytes 4718600 | tf_op jit(solution)/shard_map/ppermute | solution.py:621
  5.9 6.3 %copy-start.31 = (f32[16]{0:T(128)S(1)}, f32[16]{0:T(128)}, u32[]{:S(2)}) copy-start(f32[16]{0:T(128)} %param.11) | copy-start | bytes 196
  5.9 6.3 %copy-start.32 = (s32[16]{0:T(128)S(1)}, s32[16]{0:T(128)}, u32[]{:S(2)}) copy-start(s32[16]{0:T(128)} %param.10) | copy-start | bytes 196
  5.9 6.9 %copy-start.30 = (f32[1024]{0:T(1024)S(1)}, f32[1024]{0:T(1024)}, u32[]{:S(2)}) copy-start(f32[1024]{0:T(1024)} %param.12) | copy-start | bytes 12292
  5.9 8.0 %copy-start.33 = (s32[16]{0:T(128)S(1)}, s32[16]{0:T(128)}, u32[]{:S(2)}) copy-start(s32[16]{0:T(128)} %constant.53.clone) | copy-start | bytes 196
  13.9 3.5 %copy-start.6 = (f32[2,512,1]{2,1,0:T(8,128)S(1)}, f32[2,512,1]{2,1,0:T(8,128)}, u32[]{:S(2)}) copy-start(f32[2,512,1]{2,1,0:T(8,128)} %copy.45.refs_3_.refs_4_.refs_7_.refs_10_.refs_5_) | copy-start | bytes 12292
  17.4 36.4 %copy-start = (bf16[512,3072]{1,0:T(8,128)(2,1)}, bf16[512,3072]{1,0:T(8,128)(2,1)S(1)}, u32[]{:S(2)}) copy-start(bf16[512,3072]{1,0:T(8,128)(2,1)S(1)} %slice_bitcast_fusion.refs_2_.refs_4_.refs_6_.refs_1_.refs_3_) | copy-start | bytes 9437188
  24.5 22.9 %copy-start.14 = (bf16[2,512,512]{2,1,0:T(8,128)(2,1)}, bf16[2,512,512]{2,1,0:T(8,128)(2,1)S(1)}, u32[]{:S(2)}) copy-start(bf16[2,512,512]{2,1,0:T(8,128)(2,1)S(1)} %shard_map.74.refs_1_.refs_4_.refs_5_) | copy-start | bytes 3145732
  47.5 6.3 %collective-permute-start.5 = (bf16[3088,512]{1,0:T(8,128)(2,1)}, bf16[3088,512]{1,0:T(8,128)(2,1)}, u32[]{:S(2)}, u32[]{:S(2)}) collective-permute-start(bf16[3088,512]{1,0:T(8,128)(2,1)} %get-tuple-element.38.refs_0_.refs_2_), channel_id=1, source_target_pairs={{0,2},{2,0},{4,6},{6,4},{8,10},{10,8},{12,14},{14,12},{16,18},{18,... | collective-permute-start | bytes 9486344 | tf_op jit(solution)/shard_map/ppermute | solution.py:609
  48.1 38.4 %collective-permute-start.3 = (bf16[3088,512]{1,0:T(8,128)(2,1)}, bf16[3088,512]{1,0:T(8,128)(2,1)}, u32[]{:S(2)}, u32[]{:S(2)}) collective-permute-start(bf16[3088,512]{1,0:T(8,128)(2,1)} %get-tuple-element.36.refs_3_), channel_id=1, source_target_pairs={{0,24},{2,4},{4,2},{6,14},{8,0},{10,12},{12,10},{14,22},{16,8},{18... | collective-permute-start | bytes 9486344 | tf_op jit(solution)/shard_map/ppermute | solution.py:609
  48.8 11.7 %copy-start.5 = (bf16[3088,512]{1,0:T(8,128)(2,1)S(1)}, bf16[3088,512]{1,0:T(8,128)(2,1)}, u32[]{:S(2)}) copy-start(bf16[3088,512]{1,0:T(8,128)(2,1)} %get-tuple-element.34.refs_0_.b_ref.refs_9_) | copy-start | bytes 9486340
  48.8 11.7 %copy-start.15 = (bf16[2,512,512]{2,1,0:T(8,128)(2,1)S(1)}, bf16[2,512,512]{2,1,0:T(8,128)(2,1)}, u32[]{:S(2)}) copy-start(bf16[2,512,512]{2,1,0:T(8,128)(2,1)} %copy-done.14) | copy-start | bytes 3145732
  48.8 36.7 %collective-permute-start.4 = (bf16[1552,512]{1,0:T(8,128)(2,1)S(1)}, bf16[1552,512]{1,0:T(8,128)(2,1)S(1)}, u32[]{:S(2)}, u32[]{:S(2)}) collective-permute-start(bf16[1552,512]{1,0:T(8,128)(2,1)S(1)} %get-tuple-element.37), channel_id=1, source_target_pairs={{0,1},{1,0},{2,3},{3,2},{4,5},{5,4},{6,7},{7,6},{8,9},{9,8},{10,11... | collective-permute-start | bytes 4767752 | tf_op jit(solution)/shard_map/ppermute | solution.py:621
  85.6 6.6 %copy-start.9 = (bf16[1552,512]{1,0:T(8,128)(2,1)}, bf16[1552,512]{1,0:T(8,128)(2,1)S(1)}, u32[]{:S(2)}) copy-start(bf16[1552,512]{1,0:T(8,128)(2,1)S(1)} %collective-permute-done.4.refs_0_.array_ref.refs_1_.refs_8_) | copy-start | bytes 4767748
  91.2 6.6 %collective-permute-start.7 = (bf16[3088,512]{1,0:T(8,128)(2,1)}, bf16[3088,512]{1,0:T(8,128)(2,1)S(1)}, u32[]{:S(2)}, u32[]{:S(2)}) collective-permute-start(bf16[3088,512]{1,0:T(8,128)(2,1)} %get-tuple-element.40.refs_0_.refs_2_), channel_id=1, source_target_pairs={{0,2},{2,0},{4,6},{6,4},{8,10},{10,8},{12,14},{14,12},{16,18},{18,... | collective-permute-start | bytes 9486344 | tf_op jit(solution)/shard_map/ppermute | solution.py:609
  92.2 37.4 %collective-permute-start.6 = (bf16[3088,512]{1,0:T(8,128)(2,1)}, bf16[3088,512]{1,0:T(8,128)(2,1)S(1)}, u32[]{:S(2)}, u32[]{:S(2)}) collective-permute-start(bf16[3088,512]{1,0:T(8,128)(2,1)} %get-tuple-element.39.refs_0_), channel_id=1, source_target_pairs={{0,6},{2,10},{4,28},{6,0},{8,14},{10,18},{12,4},{14,8},{16,22},{18... | collective-permute-start | bytes 9486344 | tf_op jit(solution)/shard_map/ppermute | solution.py:609
  92.9 23.0 %copy-start.16 = (bf16[512,1536]{1,0:T(8,128)(2,1)}, bf16[512,1536]{1,0:T(8,128)(2,1)S(1)}, u32[]{:S(2)}) copy-start(bf16[512,1536]{1,0:T(8,128)(2,1)S(1)} %shard_map.80.refs_6_.refs_8_.refs_3_) | copy-start | bytes 4718596
  129.1 9.9 %copy-start.10 = (bf16[1552,512]{1,0:T(8,128)(2,1)S(1)}, bf16[1552,512]{1,0:T(8,128)(2,1)}, u32[]{:S(2)}) copy-start(bf16[1552,512]{1,0:T(8,128)(2,1)} %copy-done.9) | copy-start | bytes 4767748
  129.1 10.4 %copy-start.3 = (bf16[6,512,512]{2,1,0:T(8,128)(2,1)S(1)}, bf16[6,512,512]{2,1,0:T(8,128)(2,1)}, u32[]{:S(2)}) copy-start(bf16[6,512,512]{2,1,0:T(8,128)(2,1)} %shard_map.81.refs_2_.refs_3_.refs_4_.refs_5_.refs_6_.refs_7_) | copy-start | bytes 9437188
  134.4 5.1 %copy-start.4 = (bf16[3088,512]{1,0:T(8,128)(2,1)}, bf16[3088,512]{1,0:T(8,128)(2,1)S(1)}, u32[]{:S(2)}) copy-start(bf16[3088,512]{1,0:T(8,128)(2,1)S(1)} %shard_map.83.refs_8_.refs_4_.refs_0_) | copy-start | bytes 9486340
  134.4 20.1 %copy-start.7 = (f32[2,512,1]{2,1,0:T(8,128)S(1)}, f32[2,512,1]{2,1,0:T(8,128)}, u32[]{:S(2)}) copy-start(f32[2,512,1]{2,1,0:T(8,128)} %copy.45.refs_3_.refs_4_.refs_7_.refs_10_.refs_5_) | copy-start | bytes 12292
  134.4 18.9 %collective-permute-start.8 = (bf16[3088,512]{1,0:T(8,128)(2,1)S(1)}, bf16[3088,512]{1,0:T(8,128)(2,1)}, u32[]{:S(2)}, u32[]{:S(2)}) collective-permute-start(bf16[3088,512]{1,0:T(8,128)(2,1)S(1)} %shard_map.83.refs_8_.refs_4_.refs_0_), channel_id=1, source_target_pairs={{0,2},{2,0},{4,6},{6,4},{8,10},{10,8},{12,14},{14,12},{16,18},{18,... | collective-permute-start | bytes 9486344 | tf_op jit(solution)/shard_map/ppermute | solution.py:609
  135.0 38.3 %collective-permute-start.9 = (bf16[3088,512]{1,0:T(8,128)(2,1)S(1)}, bf16[3088,512]{1,0:T(8,128)(2,1)S(1)}, u32[]{:S(2)}, u32[]{:S(2)}) collective-permute-start(bf16[3088,512]{1,0:T(8,128)(2,1)S(1)} %shard_map.83.refs_8_.refs_4_.refs_0_), channel_id=1, source_target_pairs={{0,8},{2,4},{4,2},{6,30},{8,16},{10,12},{12,10},{14,6},{16,24},{18... | collective-permute-start | bytes 9486344 | tf_op jit(solution)/shard_map/ppermute | solution.py:609
  138.9 14.3 %collective-permute-start.10 = (bf16[1536,512]{1,0:T(8,128)(2,1)}, bf16[1536,512]{1,0:T(8,128)(2,1)S(1)}, u32[]{:S(2)}, u32[]{:S(2)}) collective-permute-start(bf16[1536,512]{1,0:T(8,128)(2,1)} %collective-permute-done.1.refs_0_.array_ref.refs_7_), channel_id=1, source_target_pairs={{0,2},{2,0},{4,6},{6,4},{8,10},{10,8},{12,14},{14,12},{16,18},{18,... | collective-permute-start | bytes 4718600 | tf_op jit(solution)/shard_map/ppermute | solution.py:609
  138.9 14.3 %collective-permute-start.11 = (bf16[1552,512]{1,0:T(8,128)(2,1)S(1)}, bf16[1552,512]{1,0:T(8,128)(2,1)S(1)}, u32[]{:S(2)}, u32[]{:S(2)}) collective-permute-start(bf16[1552,512]{1,0:T(8,128)(2,1)S(1)} %copy-done.10), channel_id=1, source_target_pairs={{0,2},{2,0},{4,6},{6,4},{8,10},{10,8},{12,14},{14,12},{16,18},{18,... | collective-permute-start | bytes 4767752 | tf_op jit(solution)/shard_map/ppermute | solution.py:609
  152.9 54.4 %collective-permute-start.13 = (bf16[3088,512]{1,0:T(8,128)(2,1)}, bf16[3088,512]{1,0:T(8,128)(2,1)}, u32[]{:S(2)}, u32[]{:S(2)}) collective-permute-start(bf16[3088,512]{1,0:T(8,128)(2,1)} %get-tuple-element.43), channel_id=1, source_target_pairs={{0,8},{2,4},{4,2},{6,30},{8,16},{10,12},{12,10},{14,6},{16,24},{18... | collective-permute-start | bytes 9486344 | tf_op jit(solution)/shard_map/ppermute | solution.py:609
  153.2 17.8 %copy-start.23 = (bf16[1536,512]{1,0:T(8,128)(2,1)}, bf16[1536,512]{1,0:T(8,128)(2,1)S(1)}, u32[]{:S(2)}) copy-start(bf16[1536,512]{1,0:T(8,128)(2,1)S(1)} %collective-permute-done.10.refs_2_) | copy-start | bytes 4718596
  154.5 20.6 %copy-start.17 = (bf16[512,1536]{1,0:T(8,128)(2,1)S(1)}, bf16[512,1536]{1,0:T(8,128)(2,1)}, u32[]{:S(2)}) copy-start(bf16[512,1536]{1,0:T(8,128)(2,1)} %copy-done.16) | copy-start | bytes 4718596
  171.0 8.9 %copy-start.11 = (bf16[1552,512]{1,0:T(8,128)(2,1)S(1)}, bf16[1552,512]{1,0:T(8,128)(2,1)}, u32[]{:S(2)}) copy-start(bf16[1552,512]{1,0:T(8,128)(2,1)} %copy-done.9) | copy-start | bytes 4767748
  187.0 64.5 %collective-permute-start.12 = (bf16[3088,512]{1,0:T(8,128)(2,1)}, bf16[3088,512]{1,0:T(8,128)(2,1)}, u32[]{:S(2)}, u32[]{:S(2)}) collective-permute-start(bf16[3088,512]{1,0:T(8,128)(2,1)} %get-tuple-element.42), channel_id=1, source_target_pairs={{0,8},{2,4},{4,2},{6,30},{8,16},{10,12},{12,10},{14,6},{16,24},{18... | collective-permute-start | bytes 9486344 | tf_op jit(solution)/shard_map/ppermute | solution.py:609
  190.7 9.0 %copy-start.1 = (bf16[512,3072]{1,0:T(8,128)(2,1)S(1)}, bf16[512,3072]{1,0:T(8,128)(2,1)}, u32[]{:S(2)}) copy-start(bf16[512,3072]{1,0:T(8,128)(2,1)} %copy-done) | copy-start | bytes 9437188
  190.7 32.7 %collective-permute-start.17 = (bf16[1536,512]{1,0:T(8,128)(2,1)S(1)}, bf16[1536,512]{1,0:T(8,128)(2,1)S(1)}, u32[]{:S(2)}, u32[]{:S(2)}) collective-permute-start(bf16[1536,512]{1,0:T(8,128)(2,1)S(1)} %get-tuple-element.44.refs_6_), channel_id=1, source_target_pairs={{0,1},{1,0},{2,3},{3,2},{4,5},{5,4},{6,7},{7,6},{8,9},{9,8},{10,11... | collective-permute-start | bytes 4718600 | tf_op jit(solution)/shard_map/ppermute | solution.py:621
  204.5 6.0 %copy-start.20 = (bf16[1,512,512]{2,1,0:T(8,128)(2,1)}, bf16[1,512,512]{2,1,0:T(8,128)(2,1)S(1)}, u32[]{:S(2)}) copy-start(bf16[1,512,512]{2,1,0:T(8,128)(2,1)S(1)} %shard_map.89.refs_0_.refs_17_) | copy-start | bytes 1572868
  210.5 4.8 %copy-start.12 = (bf16[1040,512]{1,0:T(8,128)(2,1)}, bf16[1040,512]{1,0:T(8,128)(2,1)S(1)}, u32[]{:S(2)}) copy-start(bf16[1040,512]{1,0:T(8,128)(2,1)S(1)} %get-tuple-element.47.refs_2_.refs_6_.refs_9_) | copy-start | bytes 3194884
  210.5 15.9 %collective-permute-start.16 = (bf16[1040,512]{1,0:T(8,128)(2,1)S(1)}, bf16[1040,512]{1,0:T(8,128)(2,1)}, u32[]{:S(2)}, u32[]{:S(2)}) collective-permute-start(bf16[1040,512]{1,0:T(8,128)(2,1)S(1)} %get-tuple-element.47.refs_2_.refs_6_.refs_9_), channel_id=1, source_target_pairs={{0,2},{2,0},{4,6},{6,4},{8,10},{10,8},{12,14},{14,12},{16,18},{18,... | collective-permute-start | bytes 3194888 | tf_op jit(solution)/shard_map/ppermute | solution.py:609
  210.6 15.8 %collective-permute-start.14 = (bf16[1024,512]{1,0:T(8,128)(2,1)S(1)}, bf16[1024,512]{1,0:T(8,128)(2,1)}, u32[]{:S(2)}, u32[]{:S(2)}) collective-permute-start(bf16[1024,512]{1,0:T(8,128)(2,1)S(1)} %get-tuple-element.45.refs_0_.refs_4_.refs_7_), channel_id=1, source_target_pairs={{0,2},{2,0},{4,6},{6,4},{8,10},{10,8},{12,14},{14,12},{16,18},{18,... | collective-permute-start | bytes 3145736 | tf_op jit(solution)/shard_map/ppermute | solution.py:609
  211.1 15.4 %copy-start.8 = (f32[2,512,1]{2,1,0:T(8,128)S(1)}, f32[2,512,1]{2,1,0:T(8,128)}, u32[]{:S(2)}) copy-start(f32[2,512,1]{2,1,0:T(8,128)} %copy.45.refs_3_.refs_4_.refs_7_.refs_10_.refs_5_) | copy-start | bytes 12292
  211.1 15.3 %collective-permute-start.15 = (bf16[1024,512]{1,0:T(8,128)(2,1)}, bf16[1024,512]{1,0:T(8,128)(2,1)}, u32[]{:S(2)}, u32[]{:S(2)}) collective-permute-start(bf16[1024,512]{1,0:T(8,128)(2,1)} %get-tuple-element.46.refs_1_.refs_5_.refs_8_), channel_id=1, source_target_pairs={{0,2},{2,0},{4,6},{6,4},{8,10},{10,8},{12,14},{14,12},{16,18},{18,... | collective-permute-start | bytes 3145736 | tf_op jit(solution)/shard_map/ppermute | solution.py:609
  224.6 39.4 %collective-permute-start.21 = (bf16[1536,512]{1,0:T(8,128)(2,1)}, bf16[1536,512]{1,0:T(8,128)(2,1)}, u32[]{:S(2)}, u32[]{:S(2)}) collective-permute-start(bf16[1536,512]{1,0:T(8,128)(2,1)} %shard_map.88.refs_2_), channel_id=1, source_target_pairs={{0,1},{1,0},{2,3},{3,2},{4,5},{5,4},{6,7},{7,6},{8,9},{9,8},{10,11... | collective-permute-start | bytes 4718600 | tf_op jit(solution)/shard_map/ppermute | solution.py:621
  226.4 6.5 %copy-start.19 = (bf16[1,512,512]{2,1,0:T(8,128)(2,1)S(1)}, bf16[1,512,512]{2,1,0:T(8,128)(2,1)}, u32[]{:S(2)}) copy-start(bf16[1,512,512]{2,1,0:T(8,128)(2,1)} %copy-done.18) | copy-start | bytes 1572868
  226.4 6.5 %copy-start.21 = (bf16[1,512,512]{2,1,0:T(8,128)(2,1)S(1)}, bf16[1,512,512]{2,1,0:T(8,128)(2,1)}, u32[]{:S(2)}) copy-start(bf16[1,512,512]{2,1,0:T(8,128)(2,1)} %copy-done.20) | copy-start | bytes 1572868
  254.1 4.8 %copy-start.13 = (bf16[1040,512]{1,0:T(8,128)(2,1)}, bf16[1040,512]{1,0:T(8,128)(2,1)S(1)}, u32[]{:S(2)}) copy-start(bf16[1040,512]{1,0:T(8,128)(2,1)S(1)} %get-tuple-element.50.refs_2_.refs_6_) | copy-start | bytes 3194884
  254.2 5.8 %collective-permute-start.20 = (bf16[1040,512]{1,0:T(8,128)(2,1)S(1)}, bf16[1040,512]{1,0:T(8,128)(2,1)S(1)}, u32[]{:S(2)}, u32[]{:S(2)}) collective-permute-start(bf16[1040,512]{1,0:T(8,128)(2,1)S(1)} %get-tuple-element.50.refs_2_.refs_6_), channel_id=1, source_target_pairs={{0,2},{2,0},{4,6},{6,4},{8,10},{10,8},{12,14},{14,12},{16,18},{18,... | collective-permute-start | bytes 3194888 | tf_op jit(solution)/shard_map/ppermute | solution.py:609
  254.2 4.7 %collective-permute-start.18 = (bf16[1024,512]{1,0:T(8,128)(2,1)S(1)}, bf16[1024,512]{1,0:T(8,128)(2,1)S(1)}, u32[]{:S(2)}, u32[]{:S(2)}) collective-permute-start(bf16[1024,512]{1,0:T(8,128)(2,1)S(1)} %get-tuple-element.48.refs_0_.refs_4_), channel_id=1, source_target_pairs={{0,2},{2,0},{4,6},{6,4},{8,10},{10,8},{12,14},{14,12},{16,18},{18,... | collective-permute-start | bytes 3145736 | tf_op jit(solution)/shard_map/ppermute | solution.py:609
  254.7 5.2 %collective-permute-start.19 = (bf16[1024,512]{1,0:T(8,128)(2,1)S(1)}, bf16[1024,512]{1,0:T(8,128)(2,1)S(1)}, u32[]{:S(2)}, u32[]{:S(2)}) collective-permute-start(bf16[1024,512]{1,0:T(8,128)(2,1)S(1)} %get-tuple-element.49.refs_1_.refs_5_), channel_id=1, source_target_pairs={{0,2},{2,0},{4,6},{6,4},{8,10},{10,8},{12,14},{14,12},{16,18},{18,... | collective-permute-start | bytes 3145736 | tf_op jit(solution)/shard_map/ppermute | solution.py:609
  259.9 4.1 %copy-start.22 = (bf16[1040,512]{1,0:T(8,128)(2,1)}, bf16[1040,512]{1,0:T(8,128)(2,1)S(1)}, u32[]{:S(2)}) copy-start(bf16[1040,512]{1,0:T(8,128)(2,1)S(1)} %collective-permute-done.20.refs_2_.refs_5_) | copy-start | bytes 3194884
  (8 other events, 10.8 us)

commit v2 on v1

--- a/solution.py
+++ b/solution.py
@@ -726,14 +726,15 @@
     sent1 = density(slabs, far, [[out_part]], bf16, sent0, rows=(half, half))
     incoming = [sibling(sent0), sibling(sent1)]
     done = amps([(r4, near)], [rows_near], sent1)
+    part = density([own_far, mate_far, r3, s3, r4], near, [[part]], f32, done)
 
     thirds = [aux // 3, aux // 3 * 2]
-    r5 = Slab(copied(r5.array, done, cuts=thirds), r5.ids)
+    r5 = Slab(copied(r5.array, part, cuts=thirds), r5.ids)
     s5 = swapped(r5)
     done = amps([(r5, near)], [rows_near], *r5.pieces)
     done = join_call([incoming[0], done])
     done = amps([(s5, near)], [rows_near], done)
-    part = density([own_far, mate_far, r3, s3, r4, r5, s5], near, [[part]], f32, done)
+    part = density([r5, s5], near, [[part]], f32, done)
     r6 = Slab(copied(r6.array, part, cuts=thirds), r6.ids, 1)
     s6 = swapped(r6)
     done = amps([(r6, near)], [rows_near], *r6.pieces)

time: 277 us -> 278 us (level)
  Pallas kernels: 180 us -> 188 us
  waiting for transfers between devices: 51.8 us -> 45.8 us
    pallas_call x7 -> x8, Pallas kernels: 80 us -> 87.6 us  [density_call(): pl.pallas_call(kernel, grid=(steps,), in_specs=[pl.BlockSpec(memory_space...]
    ppermute x4, waiting for transfers between devices: 32.7 us -> 29.5 us  [sibling(): return lax.ppermute(array, 'narrow', [(0, 1), (1, 0)])]
    ppermute x18, waiting for transfers between devices: 19.2 us -> 16.3 us  [moved(): sent = [lax.ppermute(piece, 'wide', pairs) for piece in slab.pieces]]
    unnamed x68 -> x66, local copies, waits for them, and re-layouts: 10.9 us -> 10.8 us
  transfers between devices with their start and end apart: 22 -> 22, of which waited for: 11 -> 10; matrix products, arithmetic and copies ran while one was open for 4% -> 4% of each run, Pallas kernels for 56% -> 58%
where the time goes in v2:
time: 278 us; the launch traced here: 276 us
  Pallas kernels  188 us (68%)
  waiting for transfers between devices  45.8 us (16%)
  local copies, waits for them, and re-layouts  20.3 us (7%)
  starting transfers between devices  18.6 us (7%)
    pallas_call x8, Pallas kernels, density_call(): pl.pallas_call(kernel, grid=(steps,), in_specs=[pl.BlockSpec(memory_space...  87.6 us
    pallas_call x10, Pallas kernels, amplitude_call(): pl.pallas_call(kernel, grid=(len(jobs),), in_specs=[pl.BlockSpec(memory_s...  74.6 us
    ppermute x4, waiting for transfers between devices, sibling(): return lax.ppermute(array, 'narrow', [(0, 1), (1, 0)])  29.5 us
    pallas_call x5, Pallas kernels, choice_call(): pl.pallas_call(kernel, in_specs=[pl.BlockSpec(memory_space=pltpu.SMEM)] +...  18.9 us
    ppermute x18, waiting for transfers between devices, moved(): sent = [lax.ppermute(piece, 'wide', pairs) for piece in slab.pieces]  16.3 us
    ppermute x18, starting transfers between devices, moved(): sent = [lax.ppermute(piece, 'wide', pairs) for piece in slab.pieces]  14.3 us
    unnamed x66, local copies, waits for them, and re-layouts  10.8 us
    pallas_call x1, local copies, waits for them, and re-layouts, append_call(): pl.pallas_call(kernel, in_specs=[pl.BlockSpec(memory_space=pl.ANY)] * 2,...  5.6 us
  transfers between devices with their start and end apart: 22, of which 10 were waited for; matrix products, arithmetic and copies ran while one was open for 4% of the time, Pallas kernels for 58%

profile of v2, /device:TPU:3, one launch (start us, length us, event | category | flops | bytes accessed | tf_op | source)
XLA Modules:
  0.0 276.0 jit_solution(2610494315288091512)
XLA Ops:
  0.7 3.0 %shard_map.73 = (bf16[3088,512]{1,0:T(8,128)(2,1)}, bf16[1536,512]{1,0:T(8,128)(2,1)S(1)}, bf16[1552,512]{1,0:T(8,128)(2,1)S(1)}) custom-call(bf16[3072,512]{1,0:T(8,128)(2,1)} %bitcast.20, bf16[16,512]{1,0:T(8,128)(2,1)S(1)} %scatter.4.tail_ref), custom_call_target="tpu_custom_call" | custom-call | tf_op jit(solution)/shard_map/pallas_call | solution.py:355
  4.5 1.4 collective-permute-start.1
  5.9 5.6 %copy.43 = bf16[3088,512]{0,1:T(8,128)(2,1)} copy(bf16[3088,512]{1,0:T(8,128)(2,1)} %get-tuple-element.34.refs_0_.b_ref.refs_9_) | data formatting | bytes 6324224 | tf_op jit(solution)/shard_map/pallas_call | solution.py:355
  12.9 1.0 copy.45.refs_3_.refs_4_.refs_7_.refs_10_.refs_5_
  15.2 2.1 slice_bitcast_fusion.refs_2_.refs_4_.refs_6_.refs_1_.refs_3_
  17.3 7.1 %shard_map.74.refs_1_.refs_4_.refs_5_ = bf16[2,512,512]{2,1,0:T(8,128)(2,1)S(1)} custom-call(f32[12,3]{1,0:T(8,128)S(1)} %copy.44.scalars, bf16[3088,512]{1,0:T(8,128)(2,1)} %get-tuple-element.34.refs_0_.b_ref.refs_9_, bf16[3088,512]{1,0:T(8,128)(2,1)} %collective-permute-done.2.refs_1_, ...), custom_call_target="tpu_custom_call" | custom-call | flops 3221225472 | bytes 10485760 | tf_op jit(solution)/shard_map/pallas_call | solution.py:255
  24.5 14.4 %collective-permute-done.1.refs_0_.array_ref.refs_7_ = bf16[1536,512]{1,0:T(8,128)(2,1)} collective-permute-done((bf16[1536,512]{1,0:T(8,128)(2,1)S(1)}, bf16[1536,512]{1,0:T(8,128)(2,1)}, u32[]{:S(2)}, u32[]{:S(2)}) %collective-permute-start.1) | collective-permute-done | bytes 1572896 | tf_op jit(solution)/shard_map/ppermute | solution.py:621
  38.8 3.1 %collective-permute-done.a_ref = bf16[3088,512]{1,0:T(8,128)(2,1)} collective-permute-done((bf16[3088,512]{1,0:T(8,128)(2,1)}, bf16[3088,512]{1,0:T(8,128)(2,1)}, u32[]{:S(2)}, u32[]{:S(2)}) %collective-permute-start) | collective-permute-done | bytes 3162144 | tf_op jit(solution)/shard_map/ppermute | solution.py:609
  41.9 5.5 %shard_map.75 = (bf16[3088,512]{1,0:T(8,128)(2,1)}, bf16[3088,512]{1,0:T(8,128)(2,1)}) custom-call(s32[1]{0:T(128)S(6)} %sub.6.flag_ref, bf16[3088,512]{1,0:T(8,128)(2,1)} %collective-permute-done.a_ref, bf16[3088,512]{1,0:T(8,128)(2,1)} %get-tuple-element.34.refs_0_.b_ref.refs_9_, bf16[1536,512]{1,0:T(8,128)(2,1)} %collective-permute-done.1.refs_0_.array_ref.refs_7_, ...), custom_call_target="tpu_custom_call" | custom-call | bytes 6324224 | tf_op jit(solution)/shard_map/pallas_call | solution.py:413
  48.9 1.2 collective-permute-start.4
  50.1 3.8 %collective-permute-done.5.refs_1_.refs_3_ = bf16[3088,512]{1,0:T(8,128)(2,1)} collective-permute-done((bf16[3088,512]{1,0:T(8,128)(2,1)}, bf16[3088,512]{1,0:T(8,128)(2,1)}, u32[]{:S(2)}, u32[]{:S(2)}) %collective-permute-start.5) | collective-permute-done | bytes 3162144 | tf_op jit(solution)/shard_map/ppermute | solution.py:609
  54.0 6.8 %shard_map.76.refs_6_.refs_7_.refs_8_ = bf16[2,512,512]{2,1,0:T(8,128)(2,1)S(1)} custom-call(f32[12,3]{1,0:T(8,128)S(1)} %copy.44.scalars, bf16[3088,512]{1,0:T(8,128)(2,1)} %get-tuple-element.38.refs_0_.refs_2_, bf16[3088,512]{1,0:T(8,128)(2,1)} %collective-permute-done.5.refs_1_.refs_3_, ...), custom_call_target="tpu_custom_call" | custom-call | flops 3221225472 | bytes 10485760 | tf_op jit(solution)/shard_map/pallas_call | solution.py:255
  60.8 11.4 %shard_map.77.refs_0_.refs_5_ = f32[3072,512]{1,0:T(8,128)} custom-call(bf16[3088,512]{1,0:T(8,128)(2,1)S(1)} %copy-done.5, bf16[3088,512]{1,0:T(8,128)(2,1)} %collective-permute-done.2.refs_1_, bf16[3088,512]{1,0:T(8,128)(2,1)} %get-tuple-element.38.refs_0_.refs_2_, bf16[3088,512]{1,0:T(8,128)(2,1)} %collective-permute-done.5.refs_1_.refs_3_, ...), custom_call_target="tpu_custom_call" | custom-call | flops 6442450944 | bytes 20971520 | tf_op jit(solution)/shard_map/pallas_call | solution.py:576
  72.2 2.6 shard_map.78.refs_1_.refs_5_.refs_7_.refs_2_
  74.8 10.9 %collective-permute-done.4.refs_0_.array_ref.refs_1_.refs_8_ = bf16[1552,512]{1,0:T(8,128)(2,1)S(1)} collective-permute-done((bf16[1552,512]{1,0:T(8,128)(2,1)S(1)}, bf16[1552,512]{1,0:T(8,128)(2,1)S(1)}, u32[]{:S(2)}, u32[]{:S(2)}) %collective-permute-start.4) | collective-permute-done | bytes 1589280 | tf_op jit(solution)/shard_map/ppermute | solution.py:621
  85.6 1.1 collective-permute-done.3.a_ref
  86.7 4.5 %shard_map.79 = (bf16[3088,512]{1,0:T(8,128)(2,1)}, bf16[3088,512]{1,0:T(8,128)(2,1)}) custom-call(s32[1]{0:T(128)} %dynamic_slice.12.flag_ref, bf16[3088,512]{1,0:T(8,128)(2,1)} %collective-permute-done.3.a_ref, bf16[3088,512]{1,0:T(8,128)(2,1)} %get-tuple-element.34.refs_0_.b_ref.refs_9_, ...), custom_call_target="tpu_custom_call" | custom-call | bytes 6324224 | tf_op jit(solution)/shard_map/pallas_call | solution.py:413
  91.2 1.0 collective-permute-start.7
  93.0 4.8 %collective-permute-done.7.refs_1_.refs_3_ = bf16[3088,512]{1,0:T(8,128)(2,1)S(1)} collective-permute-done((bf16[3088,512]{1,0:T(8,128)(2,1)}, bf16[3088,512]{1,0:T(8,128)(2,1)S(1)}, u32[]{:S(2)}, u32[]{:S(2)}) %collective-permute-start.7) | collective-permute-done | bytes 3162144 | tf_op jit(solution)/shard_map/ppermute | solution.py:609
  97.8 1.7 copy-done.25
  99.4 16.5 %shard_map.81.refs_2_.refs_3_.refs_4_.refs_5_.refs_6_.refs_7_ = bf16[6,512,512]{2,1,0:T(8,128)(2,1)} custom-call(f32[12,3]{1,0:T(8,128)S(1)} %copy.44.scalars, bf16[3088,512]{1,0:T(8,128)(2,1)} %get-tuple-element.40.refs_0_.refs_2_, bf16[3088,512]{1,0:T(8,128)(2,1)} %copy-done.25, bf16[3088,512]{1,0:T(8,128)(2,1)} %get-tuple-element.38.refs_0_.refs_2_, ...), custom_call_target="tpu_custom_call" | custom-call | flops 9663676416 | bytes 22020096 | tf_op jit(solution)/shard_map/pallas_call | solution.py:255
  116.0 1.9 copy-done.2
  117.9 11.2 %shard_map.82.refs_0_.refs_13_ = f32[3072,512]{1,0:T(8,128)} custom-call(bf16[3088,512]{1,0:T(8,128)(2,1)} %get-tuple-element.40.refs_0_.refs_2_, bf16[3088,512]{1,0:T(8,128)(2,1)} %copy-done.25, bf16[6,512,512]{2,1,0:T(8,128)(2,1)S(1)} %copy-done.2, bf16[6,512,512]{2,1,0:T(8,128)(2,1)S(1)} %copy-done.2, bf16[6,512,512]{2,1,0:T(8,128)(2,1)S(1)} %copy-done.2, ...), custom_call_target="tpu_custom_call" | custom-call | flops 3221225472 | bytes 19922944 | tf_op jit(solution)/shard_map/pallas_call | solution.py:576
  129.6 1.7 copy-done.26
  131.3 3.1 %shard_map.83.refs_8_.refs_4_.refs_0_ = bf16[3088,512]{1,0:T(8,128)(2,1)S(1)} custom-call(s32[1]{0:T(128)} %dynamic_slice.12.flag_ref, bf16[3088,512]{1,0:T(8,128)(2,1)} %copy-done.26, bf16[3088,512]{1,0:T(8,128)(2,1)} %copy-done.26, f32[3072,512]{1,0:T(8,128)} %shard_map.82.refs_0_.refs_13_), custom_call_target="tpu_custom_call" | custom-call | bytes 6324224 | tf_op jit(solution)/shard_map/pallas_call | solution.py:413
  135.1 3.9 %collective-permute-start.9 = (bf16[3088,512]{1,0:T(8,128)(2,1)S(1)}, bf16[3088,512]{1,0:T(8,128)(2,1)S(1)}, u32[]{:S(2)}, u32[]{:S(2)}) collective-permute-start(bf16[3088,512]{1,0:T(8,128)(2,1)S(1)} %shard_map.83.refs_8_.refs_4_.refs_0_), channel_id=1, source_target_pairs={{0,8},{2,4},{4,2},{6,30},{8,16},{10,12},{12,10},{14,6},{16,24},{18... | collective-permute-start | bytes 9486344 | tf_op jit(solution)/shard_map/ppermute | solution.py:609
  139.6 13.5 %shard_map.84 = (f32[3072,512]{1,0:T(8,128)}, bf16[3088,512]{1,0:T(8,128)(2,1)}) custom-call(bf16[3088,512]{1,0:T(8,128)(2,1)} %get-tuple-element.38.refs_0_.refs_2_, bf16[3088,512]{1,0:T(8,128)(2,1)} %collective-permute-done.5.refs_1_.refs_3_, bf16[3088,512]{1,0:T(8,128)(2,1)} %get-tuple-element.40.refs_0_.refs_2_, bf16[3088,512]{1,0:T(8,128)(2,1)} %copy-done.25, ...), custom_call_target="tpu_custom_call" | custom-call | flops 6442450944 | bytes 20971520 | tf_op jit(solution)/shard_map/pallas_call | solution.py:576
  153.4 1.1 copy-done.28
  154.5 16.6 %shard_map.85.refs_4_.refs_3_.refs_7_.refs_8_.refs_9_.refs_10_ = bf16[6,512,512]{2,1,0:T(8,128)(2,1)} custom-call(f32[12,3]{1,0:T(8,128)S(1)} %copy.44.scalars, bf16[1536,512]{1,0:T(8,128)(2,1)} %collective-permute-done.1.refs_0_.array_ref.refs_7_, bf16[1552,512]{1,0:T(8,128)(2,1)} %copy-done.9, bf16[1536,512]{1,0:T(8,128)(2,1)S(1)} %collective-permute-done.10.refs_2_, ...), custom_call_target="tpu_custom_call" | custom-call | flops 9663676416 | bytes 22020096 | tf_op jit(solution)/shard_map/pallas_call | solution.py:255
  171.1 2.3 collective-permute-done.9.refs_0_.refs_2_.refs_6_
  173.4 1.6 copy-done.24
  175.1 4.8 %shard_map.86.refs_5_.refs_6_ = bf16[1,512,512]{2,1,0:T(8,128)(2,1)S(1)} custom-call(f32[12,3]{1,0:T(8,128)S(1)} %copy.44.scalars, bf16[3088,512]{1,0:T(8,128)(2,1)} %copy-done.24, bf16[512,3072]{1,0:T(8,128)(2,1)} %copy-done, bf16[512,1536]{1,0:T(8,128)(2,1)S(1)} %shard_map.78.refs_1_.refs_5_.refs_7_.refs_2_, bf16[512,1536]{1,0:T(8,128)(2,1)S(1)} %copy-done.17, ...), custom_call_target="tpu_custom_call" | custom-call | flops 1610612736 | bytes 9961472 | tf_op jit(solution)/shard_map/pallas_call | solution.py:255
  179.9 7.0 %shard_map.87 = (bf16[1536,512]{1,0:T(8,128)(2,1)S(1)}, bf16[3088,512]{1,0:T(8,128)(2,1)}) custom-call(bf16[3088,512]{1,0:T(8,128)(2,1)} %copy-done.4, bf16[3088,512]{1,0:T(8,128)(2,1)} %collective-permute-done.8.refs_5_.refs_1_, bf16[3088,512]{1,0:T(8,128)(2,1)} %copy-done.24, ...), custom_call_target="tpu_custom_call" | custom-call | flops 2415919104 | bytes 11010048 | tf_op jit(solution)/shard_map/pallas_call | solution.py:576
  186.9 3.8 %collective-permute-start.12 = (bf16[3088,512]{1,0:T(8,128)(2,1)}, bf16[3088,512]{1,0:T(8,128)(2,1)}, u32[]{:S(2)}, u32[]{:S(2)}) collective-permute-start(bf16[3088,512]{1,0:T(8,128)(2,1)} %get-tuple-element.42), channel_id=1, source_target_pairs={{0,8},{2,4},{4,2},{6,30},{8,16},{10,12},{12,10},{14,6},{16,24},{18... | collective-permute-start | bytes 9486344 | tf_op jit(solution)/shard_map/ppermute | solution.py:609
  190.7 1.2 collective-permute-start.17
  191.9 7.7 %shard_map.88.refs_2_ = bf16[1536,512]{1,0:T(8,128)(2,1)} custom-call(bf16[3088,512]{1,0:T(8,128)(2,1)} %copy-done.4, bf16[3088,512]{1,0:T(8,128)(2,1)} %collective-permute-done.8.refs_5_.refs_1_, bf16[3088,512]{1,0:T(8,128)(2,1)} %copy-done.24, bf16[6,512,512]{2,1,0:T(8,128)(2,1)} %shard_map.85.refs_4_.refs_3_.refs_7_.refs_8_.refs_9_.refs_10_, ...), custom_call_target="tpu_custom_call" | custom-call | flops 2415919104 | bytes 11010048 | tf_op jit(solution)/shard_map/pallas_call | solution.py:576
  199.6 4.8 %shard_map.89.refs_11_.refs_12_ = bf16[1,512,512]{2,1,0:T(8,128)(2,1)S(1)} custom-call(f32[12,3]{1,0:T(8,128)S(1)} %copy.44.scalars, bf16[3088,512]{1,0:T(8,128)(2,1)} %copy-done.24, bf16[512,3072]{1,0:T(8,128)(2,1)S(1)} %copy-done.1, bf16[1536,512]{1,0:T(8,128)(2,1)} %shard_map.88.refs_2_, f32[2,512,1]{2,1,0:T(8,128)S(1)} %copy-done.7, ...), custom_call_target="tpu_custom_call" | custom-call | flops 1610612736 | bytes 6815744 | tf_op jit(solution)/shard_map/pallas_call | solution.py:255
  204.4 15.0 %shard_map.90.refs_0_.refs_9_ = f32[3072,512]{1,0:T(8,128)} custom-call(bf16[1536,512]{1,0:T(8,128)(2,1)} %collective-permute-done.1.refs_0_.array_ref.refs_7_, bf16[1552,512]{1,0:T(8,128)(2,1)S(1)} %copy-done.11, bf16[1536,512]{1,0:T(8,128)(2,1)S(1)} %copy-done.22, bf16[1552,512]{1,0:T(8,128)(2,1)} %copy-done.28, bf16[3088,512]{1,0:T(8,128)(2,1)} %copy-done.4, ...), custom_call_target="tpu_custom_call" | custom-call | flops 8053063680 | bytes 30932992 | tf_op jit(solution)/shard_map/pallas_call | solution.py:576
  219.5 3.1 %shard_map.91 = (bf16[1024,512]{1,0:T(8,128)(2,1)S(1)}, bf16[1024,512]{1,0:T(8,128)(2,1)}, bf16[1040,512]{1,0:T(8,128)(2,1)S(1)}) custom-call(s32[1]{0:T(128)} %dynamic_slice.12.flag_ref, bf16[3088,512]{1,0:T(8,128)(2,1)} %collective-permute-done.13.a_ref.b_ref, bf16[3088,512]{1,0:T(8,128)(2,1)} %collective-permute-done.13.a_ref.b_ref, ...), custom_call_target="tpu_custom_call" | custom-call | bytes 6324224 | tf_op jit(solution)/shard_map/pallas_call | solution.py:413
  223.3 4.1 %shard_map.92.refs_1_.refs_6_ = bf16[1,512,512]{2,1,0:T(8,128)(2,1)S(1)} custom-call(f32[12,3]{1,0:T(8,128)S(1)} %copy.44.scalars, bf16[1024,512]{1,0:T(8,128)(2,1)S(1)} %get-tuple-element.45.refs_0_.refs_4_, bf16[1024,512]{1,0:T(8,128)(2,1)} %get-tuple-element.46.refs_1_.refs_5_, bf16[1040,512]{1,0:T(8,128)(2,1)S(1)} %get-tuple-element.47.refs_2_.refs_6_, ...), custom_call_target="tpu_custom_call" | custom-call | flops 1610612736 | bytes 6815744 | tf_op jit(solution)/shard_map/pallas_call | solution.py:255
  228.2 1.1 copy-done.27
  231.1 5.7 %shard_map.94.refs_7_.refs_8_ = bf16[1,512,512]{2,1,0:T(8,128)(2,1)S(1)} custom-call(f32[12,3]{1,0:T(8,128)S(1)} %copy.44.scalars, bf16[1024,512]{1,0:T(8,128)(2,1)} %collective-permute-done.14.refs_0_.refs_3_, bf16[1024,512]{1,0:T(8,128)(2,1)} %collective-permute-done.15.refs_1_.refs_4_, bf16[1040,512]{1,0:T(8,128)(2,1)} %collective-permute-done.16.refs_2_.refs_5_, ...), custom_call_target="tpu_custom_call" | custom-call | flops 1610612736 | bytes 6815744 | tf_op jit(solution)/shard_map/pallas_call | solution.py:255
  236.8 11.2 %shard_map.95.refs_0_.refs_9_ = f32[3072,512]{1,0:T(8,128)} custom-call(bf16[1024,512]{1,0:T(8,128)(2,1)S(1)} %get-tuple-element.45.refs_0_.refs_4_, bf16[1024,512]{1,0:T(8,128)(2,1)} %get-tuple-element.46.refs_1_.refs_5_, bf16[1040,512]{1,0:T(8,128)(2,1)} %copy-done.12, bf16[1024,512]{1,0:T(8,128)(2,1)} %collective-permute-done.14.refs_0_.refs_3_, ...), custom_call_target="tpu_custom_call" | custom-call | flops 3221225472 | bytes 19922944 | tf_op jit(solution)/shard_map/pallas_call | solution.py:576
  248.0 2.7 shard_map.96
  252.0 4.1 %shard_map.97.refs_4_.refs_6_ = bf16[1,512,512]{2,1,0:T(8,128)(2,1)S(1)} custom-call(f32[12,3]{1,0:T(8,128)S(1)} %copy.44.scalars, bf16[1024,512]{1,0:T(8,128)(2,1)S(1)} %get-tuple-element.48.refs_0_.refs_4_, bf16[1024,512]{1,0:T(8,128)(2,1)S(1)} %get-tuple-element.49.refs_1_.refs_5_, bf16[1040,512]{1,0:T(8,128)(2,1)S(1)} %get-tuple-element.50.refs_2_.refs_6_, ...), custom_call_target="tpu_custom_call" | custom-call | flops 1610612736 | bytes 6815744 | tf_op jit(solution)/shard_map/pallas_call | solution.py:255
  256.8 4.1 %shard_map.98.refs_7_.refs_8_ = bf16[1,512,512]{2,1,0:T(8,128)(2,1)S(1)} custom-call(f32[12,3]{1,0:T(8,128)S(1)} %copy.44.scalars, bf16[1024,512]{1,0:T(8,128)(2,1)S(1)} %collective-permute-done.18.refs_0_.refs_3_, bf16[1024,512]{1,0:T(8,128)(2,1)S(1)} %collective-permute-done.19.refs_1_.refs_4_, ...), custom_call_target="tpu_custom_call" | custom-call | flops 1610612736 | bytes 6815744 | tf_op jit(solution)/shard_map/pallas_call | solution.py:255
  260.9 4.3 %collective-permute-done.21.refs_11_ = bf16[1536,512]{1,0:T(8,128)(2,1)} collective-permute-done((bf16[1536,512]{1,0:T(8,128)(2,1)}, bf16[1536,512]{1,0:T(8,128)(2,1)}, u32[]{:S(2)}, u32[]{:S(2)}) %collective-permute-start.21) | collective-permute-done | bytes 1572896 | tf_op jit(solution)/shard_map/ppermute | solution.py:621
  265.2 10.6 %shard_map.99 = f32[3072,512]{1,0:T(8,128)} custom-call(bf16[1024,512]{1,0:T(8,128)(2,1)S(1)} %get-tuple-element.48.refs_0_.refs_4_, bf16[1024,512]{1,0:T(8,128)(2,1)S(1)} %get-tuple-element.49.refs_1_.refs_5_, bf16[1040,512]{1,0:T(8,128)(2,1)} %copy-done.13, bf16[1024,512]{1,0:T(8,128)(2,1)S(1)} %collective-permute-done.18.refs_0_.refs_3_, ...), custom_call_target="tpu_custom_call" | custom-call | flops 3221225472 | bytes 26214400 | tf_op jit(solution)/shard_map/pallas_call | solution.py:576
  (105 shorter events, 12.9 us)
Async XLA Ops:
  3.7 13.6 %collective-permute-start.2 = (bf16[3088,512]{1,0:T(8,128)(2,1)}, bf16[3088,512]{1,0:T(8,128)(2,1)}, u32[]{:S(2)}, u32[]{:S(2)}) collective-permute-start(bf16[3088,512]{1,0:T(8,128)(2,1)} %get-tuple-element.34.refs_0_.b_ref.refs_9_), channel_id=1, source_target_pairs={{0,2},{2,0},{4,6},{6,4},{8,10},{10,8},{12,14},{14,12},{16,18},{18,... | collective-permute-start | bytes 9486344 | tf_op jit(solution)/shard_map/ppermute | solution.py:609
  4.5 37.5 %collective-permute-start = (bf16[3088,512]{1,0:T(8,128)(2,1)}, bf16[3088,512]{1,0:T(8,128)(2,1)}, u32[]{:S(2)}, u32[]{:S(2)}) collective-permute-start(bf16[3088,512]{1,0:T(8,128)(2,1)} %get-tuple-element.34.refs_0_.b_ref.refs_9_), channel_id=1, source_target_pairs={{0,6},{2,26},{4,12},{6,0},{8,14},{10,2},{12,20},{14,8},{16,22},{18... | collective-permute-start | bytes 9486344 | tf_op jit(solution)/shard_map/ppermute | solution.py:609
  4.5 34.4 %collective-permute-start.1 = (bf16[1536,512]{1,0:T(8,128)(2,1)S(1)}, bf16[1536,512]{1,0:T(8,128)(2,1)}, u32[]{:S(2)}, u32[]{:S(2)}) collective-permute-start(bf16[1536,512]{1,0:T(8,128)(2,1)S(1)} %get-tuple-element.35), channel_id=1, source_target_pairs={{0,1},{1,0},{2,3},{3,2},{4,5},{5,4},{6,7},{7,6},{8,9},{9,8},{10,11... | collective-permute-start | bytes 4718600 | tf_op jit(solution)/shard_map/ppermute | solution.py:621
  5.9 6.3 %copy-start.30 = (f32[16]{0:T(128)S(1)}, f32[16]{0:T(128)}, u32[]{:S(2)}) copy-start(f32[16]{0:T(128)} %param.11) | copy-start | bytes 196
  5.9 6.3 %copy-start.31 = (s32[16]{0:T(128)S(1)}, s32[16]{0:T(128)}, u32[]{:S(2)}) copy-start(s32[16]{0:T(128)} %param.10) | copy-start | bytes 196
  5.9 6.9 %copy-start.29 = (f32[1024]{0:T(1024)S(1)}, f32[1024]{0:T(1024)}, u32[]{:S(2)}) copy-start(f32[1024]{0:T(1024)} %param.12) | copy-start | bytes 12292
  5.9 8.0 %copy-start.32 = (s32[16]{0:T(128)S(1)}, s32[16]{0:T(128)}, u32[]{:S(2)}) copy-start(s32[16]{0:T(128)} %constant.53.clone) | copy-start | bytes 196
  13.9 3.4 %copy-start.6 = (f32[2,512,1]{2,1,0:T(8,128)S(1)}, f32[2,512,1]{2,1,0:T(8,128)}, u32[]{:S(2)}) copy-start(f32[2,512,1]{2,1,0:T(8,128)} %copy.45.refs_3_.refs_4_.refs_7_.refs_10_.refs_5_) | copy-start | bytes 12292
  17.3 36.6 %copy-start = (bf16[512,3072]{1,0:T(8,128)(2,1)}, bf16[512,3072]{1,0:T(8,128)(2,1)S(1)}, u32[]{:S(2)}) copy-start(bf16[512,3072]{1,0:T(8,128)(2,1)S(1)} %slice_bitcast_fusion.refs_2_.refs_4_.refs_6_.refs_1_.refs_3_) | copy-start | bytes 9437188
  24.4 23.1 %copy-start.14 = (bf16[2,512,512]{2,1,0:T(8,128)(2,1)}, bf16[2,512,512]{2,1,0:T(8,128)(2,1)S(1)}, u32[]{:S(2)}) copy-start(bf16[2,512,512]{2,1,0:T(8,128)(2,1)S(1)} %shard_map.74.refs_1_.refs_4_.refs_5_) | copy-start | bytes 3145732
  47.5 6.4 %collective-permute-start.5 = (bf16[3088,512]{1,0:T(8,128)(2,1)}, bf16[3088,512]{1,0:T(8,128)(2,1)}, u32[]{:S(2)}, u32[]{:S(2)}) collective-permute-start(bf16[3088,512]{1,0:T(8,128)(2,1)} %get-tuple-element.38.refs_0_.refs_2_), channel_id=1, source_target_pairs={{0,2},{2,0},{4,6},{6,4},{8,10},{10,8},{12,14},{14,12},{16,18},{18,... | collective-permute-start | bytes 9486344 | tf_op jit(solution)/shard_map/ppermute | solution.py:609
  48.3 38.4 %collective-permute-start.3 = (bf16[3088,512]{1,0:T(8,128)(2,1)}, bf16[3088,512]{1,0:T(8,128)(2,1)}, u32[]{:S(2)}, u32[]{:S(2)}) collective-permute-start(bf16[3088,512]{1,0:T(8,128)(2,1)} %get-tuple-element.36.refs_3_), channel_id=1, source_target_pairs={{0,24},{2,4},{4,2},{6,14},{8,0},{10,12},{12,10},{14,22},{16,8},{18... | collective-permute-start | bytes 9486344 | tf_op jit(solution)/shard_map/ppermute | solution.py:609
  48.9 11.9 %copy-start.5 = (bf16[3088,512]{1,0:T(8,128)(2,1)S(1)}, bf16[3088,512]{1,0:T(8,128)(2,1)}, u32[]{:S(2)}) copy-start(bf16[3088,512]{1,0:T(8,128)(2,1)} %get-tuple-element.34.refs_0_.b_ref.refs_9_) | copy-start | bytes 9486340
  48.9 11.9 %copy-start.15 = (bf16[2,512,512]{2,1,0:T(8,128)(2,1)S(1)}, bf16[2,512,512]{2,1,0:T(8,128)(2,1)}, u32[]{:S(2)}) copy-start(bf16[2,512,512]{2,1,0:T(8,128)(2,1)} %copy-done.14) | copy-start | bytes 3145732
  48.9 36.7 %collective-permute-start.4 = (bf16[1552,512]{1,0:T(8,128)(2,1)S(1)}, bf16[1552,512]{1,0:T(8,128)(2,1)S(1)}, u32[]{:S(2)}, u32[]{:S(2)}) collective-permute-start(bf16[1552,512]{1,0:T(8,128)(2,1)S(1)} %get-tuple-element.37), channel_id=1, source_target_pairs={{0,1},{1,0},{2,3},{3,2},{4,5},{5,4},{6,7},{7,6},{8,9},{9,8},{10,11... | collective-permute-start | bytes 4767752 | tf_op jit(solution)/shard_map/ppermute | solution.py:621
  85.6 6.6 %copy-start.9 = (bf16[1552,512]{1,0:T(8,128)(2,1)}, bf16[1552,512]{1,0:T(8,128)(2,1)S(1)}, u32[]{:S(2)}) copy-start(bf16[1552,512]{1,0:T(8,128)(2,1)S(1)} %collective-permute-done.4.refs_0_.array_ref.refs_1_.refs_8_) | copy-start | bytes 4767748
  91.2 6.5 %collective-permute-start.7 = (bf16[3088,512]{1,0:T(8,128)(2,1)}, bf16[3088,512]{1,0:T(8,128)(2,1)S(1)}, u32[]{:S(2)}, u32[]{:S(2)}) collective-permute-start(bf16[3088,512]{1,0:T(8,128)(2,1)} %get-tuple-element.40.refs_0_.refs_2_), channel_id=1, source_target_pairs={{0,2},{2,0},{4,6},{6,4},{8,10},{10,8},{12,14},{14,12},{16,18},{18,... | collective-permute-start | bytes 9486344 | tf_op jit(solution)/shard_map/ppermute | solution.py:609
  92.2 37.4 %collective-permute-start.6 = (bf16[3088,512]{1,0:T(8,128)(2,1)}, bf16[3088,512]{1,0:T(8,128)(2,1)S(1)}, u32[]{:S(2)}, u32[]{:S(2)}) collective-permute-start(bf16[3088,512]{1,0:T(8,128)(2,1)} %get-tuple-element.39.refs_0_), channel_id=1, source_target_pairs={{0,6},{2,10},{4,28},{6,0},{8,14},{10,18},{12,4},{14,8},{16,22},{18... | collective-permute-start | bytes 9486344 | tf_op jit(solution)/shard_map/ppermute | solution.py:609
  92.9 23.0 %copy-start.16 = (bf16[512,1536]{1,0:T(8,128)(2,1)}, bf16[512,1536]{1,0:T(8,128)(2,1)S(1)}, u32[]{:S(2)}) copy-start(bf16[512,1536]{1,0:T(8,128)(2,1)S(1)} %shard_map.80.refs_6_.refs_8_.refs_3_) | copy-start | bytes 4718596
  116.0 1.9 copy-start.2
  129.1 9.9 %copy-start.10 = (bf16[1552,512]{1,0:T(8,128)(2,1)S(1)}, bf16[1552,512]{1,0:T(8,128)(2,1)}, u32[]{:S(2)}) copy-start(bf16[1552,512]{1,0:T(8,128)(2,1)} %copy-done.9) | copy-start | bytes 4767748
  129.1 10.4 %copy-start.3 = (bf16[6,512,512]{2,1,0:T(8,128)(2,1)S(1)}, bf16[6,512,512]{2,1,0:T(8,128)(2,1)}, u32[]{:S(2)}) copy-start(bf16[6,512,512]{2,1,0:T(8,128)(2,1)} %shard_map.81.refs_2_.refs_3_.refs_4_.refs_5_.refs_6_.refs_7_) | copy-start | bytes 9437188
  134.3 5.2 %copy-start.4 = (bf16[3088,512]{1,0:T(8,128)(2,1)}, bf16[3088,512]{1,0:T(8,128)(2,1)S(1)}, u32[]{:S(2)}) copy-start(bf16[3088,512]{1,0:T(8,128)(2,1)S(1)} %shard_map.83.refs_8_.refs_4_.refs_0_) | copy-start | bytes 9486340
  134.4 20.2 %copy-start.7 = (f32[2,512,1]{2,1,0:T(8,128)S(1)}, f32[2,512,1]{2,1,0:T(8,128)}, u32[]{:S(2)}) copy-start(f32[2,512,1]{2,1,0:T(8,128)} %copy.45.refs_3_.refs_4_.refs_7_.refs_10_.refs_5_) | copy-start | bytes 12292
  134.4 19.0 %collective-permute-start.8 = (bf16[3088,512]{1,0:T(8,128)(2,1)S(1)}, bf16[3088,512]{1,0:T(8,128)(2,1)}, u32[]{:S(2)}, u32[]{:S(2)}) collective-permute-start(bf16[3088,512]{1,0:T(8,128)(2,1)S(1)} %shard_map.83.refs_8_.refs_4_.refs_0_), channel_id=1, source_target_pairs={{0,2},{2,0},{4,6},{6,4},{8,10},{10,8},{12,14},{14,12},{16,18},{18,... | collective-permute-start | bytes 9486344 | tf_op jit(solution)/shard_map/ppermute | solution.py:609
  135.1 38.3 %collective-permute-start.9 = (bf16[3088,512]{1,0:T(8,128)(2,1)S(1)}, bf16[3088,512]{1,0:T(8,128)(2,1)S(1)}, u32[]{:S(2)}, u32[]{:S(2)}) collective-permute-start(bf16[3088,512]{1,0:T(8,128)(2,1)S(1)} %shard_map.83.refs_8_.refs_4_.refs_0_), channel_id=1, source_target_pairs={{0,8},{2,4},{4,2},{6,30},{8,16},{10,12},{12,10},{14,6},{16,24},{18... | collective-permute-start | bytes 9486344 | tf_op jit(solution)/shard_map/ppermute | solution.py:609
  139.0 14.3 %collective-permute-start.11 = (bf16[1552,512]{1,0:T(8,128)(2,1)S(1)}, bf16[1552,512]{1,0:T(8,128)(2,1)S(1)}, u32[]{:S(2)}, u32[]{:S(2)}) collective-permute-start(bf16[1552,512]{1,0:T(8,128)(2,1)S(1)} %copy-done.10), channel_id=1, source_target_pairs={{0,2},{2,0},{4,6},{6,4},{8,10},{10,8},{12,14},{14,12},{16,18},{18,... | collective-permute-start | bytes 4767752 | tf_op jit(solution)/shard_map/ppermute | solution.py:609
  139.0 14.3 %collective-permute-start.10 = (bf16[1536,512]{1,0:T(8,128)(2,1)}, bf16[1536,512]{1,0:T(8,128)(2,1)S(1)}, u32[]{:S(2)}, u32[]{:S(2)}) collective-permute-start(bf16[1536,512]{1,0:T(8,128)(2,1)} %collective-permute-done.1.refs_0_.array_ref.refs_7_), channel_id=1, source_target_pairs={{0,2},{2,0},{4,6},{6,4},{8,10},{10,8},{12,14},{14,12},{16,18},{18,... | collective-permute-start | bytes 4718600 | tf_op jit(solution)/shard_map/ppermute | solution.py:609
  153.1 66.4 %collective-permute-start.13 = (bf16[3088,512]{1,0:T(8,128)(2,1)}, bf16[3088,512]{1,0:T(8,128)(2,1)}, u32[]{:S(2)}, u32[]{:S(2)}) collective-permute-start(bf16[3088,512]{1,0:T(8,128)(2,1)} %get-tuple-element.43), channel_id=1, source_target_pairs={{0,8},{2,4},{4,2},{6,30},{8,16},{10,12},{12,10},{14,6},{16,24},{18... | collective-permute-start | bytes 9486344 | tf_op jit(solution)/shard_map/ppermute | solution.py:609
  153.4 17.8 %copy-start.21 = (bf16[1536,512]{1,0:T(8,128)(2,1)}, bf16[1536,512]{1,0:T(8,128)(2,1)S(1)}, u32[]{:S(2)}) copy-start(bf16[1536,512]{1,0:T(8,128)(2,1)S(1)} %collective-permute-done.10.refs_2_) | copy-start | bytes 4718596
  154.5 20.5 %copy-start.17 = (bf16[512,1536]{1,0:T(8,128)(2,1)S(1)}, bf16[512,1536]{1,0:T(8,128)(2,1)}, u32[]{:S(2)}) copy-start(bf16[512,1536]{1,0:T(8,128)(2,1)} %copy-done.16) | copy-start | bytes 4718596
  171.1 8.8 %copy-start.11 = (bf16[1552,512]{1,0:T(8,128)(2,1)S(1)}, bf16[1552,512]{1,0:T(8,128)(2,1)}, u32[]{:S(2)}) copy-start(bf16[1552,512]{1,0:T(8,128)(2,1)} %copy-done.9) | copy-start | bytes 4767748
  186.9 61.1 %collective-permute-start.12 = (bf16[3088,512]{1,0:T(8,128)(2,1)}, bf16[3088,512]{1,0:T(8,128)(2,1)}, u32[]{:S(2)}, u32[]{:S(2)}) collective-permute-start(bf16[3088,512]{1,0:T(8,128)(2,1)} %get-tuple-element.42), channel_id=1, source_target_pairs={{0,8},{2,4},{4,2},{6,30},{8,16},{10,12},{12,10},{14,6},{16,24},{18... | collective-permute-start | bytes 9486344 | tf_op jit(solution)/shard_map/ppermute | solution.py:609
  190.7 8.9 %copy-start.1 = (bf16[512,3072]{1,0:T(8,128)(2,1)S(1)}, bf16[512,3072]{1,0:T(8,128)(2,1)}, u32[]{:S(2)}) copy-start(bf16[512,3072]{1,0:T(8,128)(2,1)} %copy-done) | copy-start | bytes 9437188
  190.7 37.5 %collective-permute-start.17 = (bf16[1536,512]{1,0:T(8,128)(2,1)S(1)}, bf16[1536,512]{1,0:T(8,128)(2,1)S(1)}, u32[]{:S(2)}, u32[]{:S(2)}) collective-permute-start(bf16[1536,512]{1,0:T(8,128)(2,1)S(1)} %get-tuple-element.44.refs_6_), channel_id=1, source_target_pairs={{0,1},{1,0},{2,3},{3,2},{4,5},{5,4},{6,7},{7,6},{8,9},{9,8},{10,11... | collective-permute-start | bytes 4718600 | tf_op jit(solution)/shard_map/ppermute | solution.py:621
  199.6 4.8 %copy-start.22 = (bf16[1536,512]{1,0:T(8,128)(2,1)S(1)}, bf16[1536,512]{1,0:T(8,128)(2,1)}, u32[]{:S(2)}) copy-start(bf16[1536,512]{1,0:T(8,128)(2,1)} %copy-done.21) | copy-start | bytes 4718596
  222.6 4.8 %copy-start.12 = (bf16[1040,512]{1,0:T(8,128)(2,1)}, bf16[1040,512]{1,0:T(8,128)(2,1)S(1)}, u32[]{:S(2)}) copy-start(bf16[1040,512]{1,0:T(8,128)(2,1)S(1)} %get-tuple-element.47.refs_2_.refs_6_) | copy-start | bytes 3194884
  222.6 7.7 %collective-permute-start.16 = (bf16[1040,512]{1,0:T(8,128)(2,1)S(1)}, bf16[1040,512]{1,0:T(8,128)(2,1)}, u32[]{:S(2)}, u32[]{:S(2)}) collective-permute-start(bf16[1040,512]{1,0:T(8,128)(2,1)S(1)} %get-tuple-element.47.refs_2_.refs_6_), channel_id=1, source_target_pairs={{0,2},{2,0},{4,6},{6,4},{8,10},{10,8},{12,14},{14,12},{16,18},{18,... | collective-permute-start | bytes 3194888 | tf_op jit(solution)/shard_map/ppermute | solution.py:609
  222.7 7.6 %collective-permute-start.14 = (bf16[1024,512]{1,0:T(8,128)(2,1)S(1)}, bf16[1024,512]{1,0:T(8,128)(2,1)}, u32[]{:S(2)}, u32[]{:S(2)}) collective-permute-start(bf16[1024,512]{1,0:T(8,128)(2,1)S(1)} %get-tuple-element.45.refs_0_.refs_4_), channel_id=1, source_target_pairs={{0,2},{2,0},{4,6},{6,4},{8,10},{10,8},{12,14},{14,12},{16,18},{18,... | collective-permute-start | bytes 3145736 | tf_op jit(solution)/shard_map/ppermute | solution.py:609
  223.2 7.2 %copy-start.8 = (f32[2,512,1]{2,1,0:T(8,128)S(1)}, f32[2,512,1]{2,1,0:T(8,128)}, u32[]{:S(2)}) copy-start(f32[2,512,1]{2,1,0:T(8,128)} %copy.45.refs_3_.refs_4_.refs_7_.refs_10_.refs_5_) | copy-start | bytes 12292
  223.2 7.1 %collective-permute-start.15 = (bf16[1024,512]{1,0:T(8,128)(2,1)}, bf16[1024,512]{1,0:T(8,128)(2,1)}, u32[]{:S(2)}, u32[]{:S(2)}) collective-permute-start(bf16[1024,512]{1,0:T(8,128)(2,1)} %get-tuple-element.46.refs_1_.refs_5_), channel_id=1, source_target_pairs={{0,2},{2,0},{4,6},{6,4},{8,10},{10,8},{12,14},{14,12},{16,18},{18,... | collective-permute-start | bytes 3145736 | tf_op jit(solution)/shard_map/ppermute | solution.py:609
  229.3 35.9 %collective-permute-start.21 = (bf16[1536,512]{1,0:T(8,128)(2,1)}, bf16[1536,512]{1,0:T(8,128)(2,1)}, u32[]{:S(2)}, u32[]{:S(2)}) collective-permute-start(bf16[1536,512]{1,0:T(8,128)(2,1)} %shard_map.88.refs_2_), channel_id=1, source_target_pairs={{0,1},{1,0},{2,3},{3,2},{4,5},{5,4},{6,7},{7,6},{8,9},{9,8},{10,11... | collective-permute-start | bytes 4718600 | tf_op jit(solution)/shard_map/ppermute | solution.py:621
  230.3 6.4 %copy-start.19 = (bf16[1,512,512]{2,1,0:T(8,128)(2,1)S(1)}, bf16[1,512,512]{2,1,0:T(8,128)(2,1)}, u32[]{:S(2)}) copy-start(bf16[1,512,512]{2,1,0:T(8,128)(2,1)} %copy-done.18) | copy-start | bytes 1572868
  250.7 5.4 %copy-start.13 = (bf16[1040,512]{1,0:T(8,128)(2,1)}, bf16[1040,512]{1,0:T(8,128)(2,1)S(1)}, u32[]{:S(2)}) copy-start(bf16[1040,512]{1,0:T(8,128)(2,1)S(1)} %get-tuple-element.50.refs_2_.refs_6_) | copy-start | bytes 3194884
  250.7 6.1 %collective-permute-start.20 = (bf16[1040,512]{1,0:T(8,128)(2,1)S(1)}, bf16[1040,512]{1,0:T(8,128)(2,1)S(1)}, u32[]{:S(2)}, u32[]{:S(2)}) collective-permute-start(bf16[1040,512]{1,0:T(8,128)(2,1)S(1)} %get-tuple-element.50.refs_2_.refs_6_), channel_id=1, source_target_pairs={{0,2},{2,0},{4,6},{6,4},{8,10},{10,8},{12,14},{14,12},{16,18},{18,... | collective-permute-start | bytes 3194888 | tf_op jit(solution)/shard_map/ppermute | solution.py:609
  251.5 4.6 %collective-permute-start.18 = (bf16[1024,512]{1,0:T(8,128)(2,1)S(1)}, bf16[1024,512]{1,0:T(8,128)(2,1)S(1)}, u32[]{:S(2)}, u32[]{:S(2)}) collective-permute-start(bf16[1024,512]{1,0:T(8,128)(2,1)S(1)} %get-tuple-element.48.refs_0_.refs_4_), channel_id=1, source_target_pairs={{0,2},{2,0},{4,6},{6,4},{8,10},{10,8},{12,14},{14,12},{16,18},{18,... | collective-permute-start | bytes 3145736 | tf_op jit(solution)/shard_map/ppermute | solution.py:609
  251.6 5.2 %collective-permute-start.19 = (bf16[1024,512]{1,0:T(8,128)(2,1)S(1)}, bf16[1024,512]{1,0:T(8,128)(2,1)S(1)}, u32[]{:S(2)}, u32[]{:S(2)}) collective-permute-start(bf16[1024,512]{1,0:T(8,128)(2,1)S(1)} %get-tuple-element.49.refs_1_.refs_5_), channel_id=1, source_target_pairs={{0,2},{2,0},{4,6},{6,4},{8,10},{10,8},{12,14},{14,12},{16,18},{18,... | collective-permute-start | bytes 3145736 | tf_op jit(solution)/shard_map/ppermute | solution.py:609
  256.8 4.1 %copy-start.20 = (bf16[1040,512]{1,0:T(8,128)(2,1)}, bf16[1040,512]{1,0:T(8,128)(2,1)S(1)}, u32[]{:S(2)}) copy-start(bf16[1040,512]{1,0:T(8,128)(2,1)S(1)} %collective-permute-done.20.refs_2_.refs_5_) | copy-start | bytes 3194884
  (7 other events, 8.8 us)

commit v3 on v2

--- a/solution.py
+++ b/solution.py
@@ -9,7 +9,7 @@
 ROUNDS = 5
 TAIL = 16
 CHUNK = 512
-VMEM = 48 * 1024 * 1024
+VMEM = 52 * 1024 * 1024
 
 
 def passed_along(array, axis, by):

time: 278 us -> 290 us (1.043)
  Pallas kernels: 188 us -> 204 us
  waiting for transfers between devices: 45.8 us -> 32.7 us
  local copies, waits for them, and re-layouts: 20.3 us -> 29.1 us
    ppermute x4, waiting for transfers between devices: 29.5 us -> 20.6 us  [sibling(): return lax.ppermute(array, 'narrow', [(0, 1), (1, 0)])]
    unnamed x66 -> x54, local copies, waits for them, and re-layouts: 10.8 us -> 18.7 us
    pallas_call x10, Pallas kernels: 74.6 us -> 82.1 us  [amplitude_call(): pl.pallas_call(kernel, grid=(len(jobs),), in_specs=[pl.BlockSpec(memory_s...]
    pallas_call x8, Pallas kernels: 87.6 us -> 92.6 us  [density_call(): pl.pallas_call(kernel, grid=(steps,), in_specs=[pl.BlockSpec(memory_space...]
    ppermute x18, waiting for transfers between devices: 16.3 us -> 12.1 us  [moved(): sent = [lax.ppermute(piece, 'wide', pairs) for piece in slab.pieces]]
  transfers between devices with their start and end apart: 22 -> 22, of which waited for: 10 -> 8; matrix products, arithmetic and copies ran while one was open for 4% -> 4% of each run, Pallas kernels for 58% -> 61%
where the time goes in v3:
time: 290 us; the launch traced here: 289 us
  Pallas kernels  204 us (70%)
  waiting for transfers between devices  32.7 us (11%)
  local copies, waits for them, and re-layouts  29.1 us (10%)
  starting transfers between devices  19.1 us (7%)
    pallas_call x8, Pallas kernels, density_call(): pl.pallas_call(kernel, grid=(steps,), in_specs=[pl.BlockSpec(memory_space...  92.6 us
    pallas_call x10, Pallas kernels, amplitude_call(): pl.pallas_call(kernel, grid=(len(jobs),), in_specs=[pl.BlockSpec(memory_s...  82.1 us
    ppermute x4, waiting for transfers between devices, sibling(): return lax.ppermute(array, 'narrow', [(0, 1), (1, 0)])  20.6 us
    pallas_call x5, Pallas kernels, choice_call(): pl.pallas_call(kernel, in_specs=[pl.BlockSpec(memory_space=pltpu.SMEM)] +...  20.5 us
    unnamed x54, local copies, waits for them, and re-layouts  18.7 us
    ppermute x18, starting transfers between devices, moved(): sent = [lax.ppermute(piece, 'wide', pairs) for piece in slab.pieces]  14.9 us
    ppermute x18, waiting for transfers between devices, moved(): sent = [lax.ppermute(piece, 'wide', pairs) for piece in slab.pieces]  12.1 us
  transfers between devices with their start and end apart: 22, of which 8 were waited for; matrix products, arithmetic and copies ran while one was open for 4% of the time, Pallas kernels for 61%

profile of v3, /device:TPU:3, one launch (start us, length us, event | category | flops | bytes accessed | tf_op | source)
XLA Modules:
  0.0 288.5 jit_solution(6904871083650087345)
XLA Ops:
  0.7 3.6 %shard_map.73 = (bf16[3088,512]{1,0:T(8,128)(2,1)}, bf16[1536,512]{1,0:T(8,128)(2,1)S(1)}, bf16[1552,512]{1,0:T(8,128)(2,1)}) custom-call(bf16[3072,512]{1,0:T(8,128)(2,1)} %bitcast.20, bf16[16,512]{1,0:T(8,128)(2,1)S(1)} %scatter.4.tail_ref), custom_call_target="tpu_custom_call" | custom-call | tf_op jit(solution)/shard_map/pallas_call | solution.py:355
  5.0 1.4 collective-permute-start.1
  6.5 5.6 %copy.43 = bf16[3088,512]{0,1:T(8,128)(2,1)} copy(bf16[3088,512]{1,0:T(8,128)(2,1)} %get-tuple-element.34.refs_0_.b_ref.refs_9_) | data formatting | bytes 6324224 | tf_op jit(solution)/shard_map/pallas_call | solution.py:355
  15.0 3.8 %slice_bitcast_fusion.refs_2_.refs_4_.refs_6_.refs_1_.refs_3_ = bf16[512,3072]{1,0:T(8,128)(2,1)} fusion(bf16[3088,512]{0,1:T(8,128)(2,1)} %copy.43), kind=kLoop, calls=%fused_computation | loop fusion | bytes 6291456 | tf_op jit(solution)/shard_map/transpose | solution.py:671
  18.8 7.3 %shard_map.74.refs_1_.refs_4_.refs_5_ = bf16[2,512,512]{2,1,0:T(8,128)(2,1)S(1)} custom-call(f32[12,3]{1,0:T(8,128)S(1)} %copy.44.scalars, bf16[3088,512]{1,0:T(8,128)(2,1)} %get-tuple-element.34.refs_0_.b_ref.refs_9_, bf16[3088,512]{1,0:T(8,128)(2,1)} %collective-permute-done.2.refs_1_, ...), custom_call_target="tpu_custom_call" | custom-call | flops 3221225472 | bytes 10485760 | tf_op jit(solution)/shard_map/pallas_call | solution.py:255
  26.1 13.3 %collective-permute-done.1.refs_0_.array_ref.refs_7_ = bf16[1536,512]{1,0:T(8,128)(2,1)} collective-permute-done((bf16[1536,512]{1,0:T(8,128)(2,1)S(1)}, bf16[1536,512]{1,0:T(8,128)(2,1)}, u32[]{:S(2)}, u32[]{:S(2)}) %collective-permute-start.1) | collective-permute-done | bytes 1572896 | tf_op jit(solution)/shard_map/ppermute | solution.py:621
  39.4 3.1 %collective-permute-done.a_ref = bf16[3088,512]{1,0:T(8,128)(2,1)} collective-permute-done((bf16[3088,512]{1,0:T(8,128)(2,1)}, bf16[3088,512]{1,0:T(8,128)(2,1)}, u32[]{:S(2)}, u32[]{:S(2)}) %collective-permute-start) | collective-permute-done | bytes 3162144 | tf_op jit(solution)/shard_map/ppermute | solution.py:609
  42.5 5.4 %shard_map.75 = (bf16[3088,512]{1,0:T(8,128)(2,1)}, bf16[3088,512]{1,0:T(8,128)(2,1)}) custom-call(s32[1]{0:T(128)S(6)} %sub.6.flag_ref, bf16[3088,512]{1,0:T(8,128)(2,1)} %collective-permute-done.a_ref, bf16[3088,512]{1,0:T(8,128)(2,1)} %get-tuple-element.34.refs_0_.b_ref.refs_9_, bf16[1536,512]{1,0:T(8,128)(2,1)} %collective-permute-done.1.refs_0_.array_ref.refs_7_, ...), custom_call_target="tpu_custom_call" | custom-call | bytes 6324224 | tf_op jit(solution)/shard_map/pallas_call | solution.py:413
  49.4 1.2 collective-permute-start.4
  50.6 3.6 %collective-permute-done.5.refs_1_.refs_3_ = bf16[3088,512]{1,0:T(8,128)(2,1)S(1)} collective-permute-done((bf16[3088,512]{1,0:T(8,128)(2,1)}, bf16[3088,512]{1,0:T(8,128)(2,1)S(1)}, u32[]{:S(2)}, u32[]{:S(2)}) %collective-permute-start.5) | collective-permute-done | bytes 3162144 | tf_op jit(solution)/shard_map/ppermute | solution.py:609
  54.2 1.7 copy-done.10
  55.9 7.4 %shard_map.76.refs_6_.refs_7_.refs_8_ = bf16[2,512,512]{2,1,0:T(8,128)(2,1)S(1)} custom-call(f32[12,3]{1,0:T(8,128)S(1)} %copy.44.scalars, bf16[3088,512]{1,0:T(8,128)(2,1)} %get-tuple-element.38.refs_0_.refs_2_, bf16[3088,512]{1,0:T(8,128)(2,1)} %copy-done.10, bf16[512,3072]{1,0:T(8,128)(2,1)} %slice_bitcast_fusion.refs_2_.refs_4_.refs_6_.refs_1_.refs_3_, ...), custom_call_target="tpu_custom_call" | custom-call | flops 3221225472 | bytes 10485760 | tf_op jit(solution)/shard_map/pallas_call | solution.py:255
  64.3 11.8 %shard_map.77.refs_0_.refs_5_ = f32[3072,512]{1,0:T(8,128)} custom-call(bf16[3088,512]{1,0:T(8,128)(2,1)} %get-tuple-element.34.refs_0_.b_ref.refs_9_, bf16[3088,512]{1,0:T(8,128)(2,1)} %collective-permute-done.2.refs_1_, bf16[3088,512]{1,0:T(8,128)(2,1)} %get-tuple-element.38.refs_0_.refs_2_, bf16[3088,512]{1,0:T(8,128)(2,1)} %copy-done.10, ...), custom_call_target="tpu_custom_call" | custom-call | flops 6442450944 | bytes 20971520 | tf_op jit(solution)/shard_map/pallas_call | solution.py:576
  76.1 2.6 shard_map.78.refs_1_.refs_5_.refs_7_.refs_2_
  78.6 7.3 %collective-permute-done.4.refs_0_.array_ref.refs_1_.refs_8_ = bf16[1552,512]{1,0:T(8,128)(2,1)S(1)} collective-permute-done((bf16[1552,512]{1,0:T(8,128)(2,1)S(1)}, bf16[1552,512]{1,0:T(8,128)(2,1)S(1)}, u32[]{:S(2)}, u32[]{:S(2)}) %collective-permute-start.4) | collective-permute-done | bytes 1589280 | tf_op jit(solution)/shard_map/ppermute | solution.py:621
  87.1 1.7 copy-done.19
  88.8 4.7 %shard_map.79 = (bf16[3088,512]{1,0:T(8,128)(2,1)}, bf16[3088,512]{1,0:T(8,128)(2,1)}) custom-call(s32[1]{0:T(128)} %dynamic_slice.12.flag_ref, bf16[3088,512]{1,0:T(8,128)(2,1)} %copy-done.19, bf16[3088,512]{1,0:T(8,128)(2,1)} %get-tuple-element.34.refs_0_.b_ref.refs_9_, bf16[1552,512]{1,0:T(8,128)(2,1)} %copy-done.11, ...), custom_call_target="tpu_custom_call" | custom-call | bytes 6324224 | tf_op jit(solution)/shard_map/pallas_call | solution.py:413
  93.5 2.0 collective-permute-start.7
  95.5 2.6 shard_map.80.refs_6_.refs_8_.refs_3_
  98.1 1.2 copy-done.4
  99.3 1.8 collective-permute-done.7.refs_1_.refs_3_
  101.1 1.6 copy-done.13
  102.7 16.6 %shard_map.81.refs_2_.refs_3_.refs_4_.refs_5_.refs_6_.refs_7_ = bf16[6,512,512]{2,1,0:T(8,128)(2,1)} custom-call(f32[12,3]{1,0:T(8,128)S(1)} %copy.44.scalars, bf16[3088,512]{1,0:T(8,128)(2,1)} %get-tuple-element.40.refs_0_.refs_2_, bf16[3088,512]{1,0:T(8,128)(2,1)} %copy-done.13, bf16[3088,512]{1,0:T(8,128)(2,1)} %get-tuple-element.38.refs_0_.refs_2_, ...), custom_call_target="tpu_custom_call" | custom-call | flops 9663676416 | bytes 22020096 | tf_op jit(solution)/shard_map/pallas_call | solution.py:255
  119.3 11.5 %shard_map.82.refs_0_.refs_13_ = f32[3072,512]{1,0:T(8,128)} custom-call(bf16[3088,512]{1,0:T(8,128)(2,1)} %get-tuple-element.40.refs_0_.refs_2_, bf16[3088,512]{1,0:T(8,128)(2,1)} %copy-done.13, bf16[6,512,512]{2,1,0:T(8,128)(2,1)} %shard_map.81.refs_2_.refs_3_.refs_4_.refs_5_.refs_6_.refs_7_, ...), custom_call_target="tpu_custom_call" | custom-call | flops 3221225472 | bytes 19922944 | tf_op jit(solution)/shard_map/pallas_call | solution.py:576
  130.8 2.1 collective-permute-done.6.a_ref.b_ref
  132.9 1.7 copy-done.14
  134.6 3.5 %shard_map.83.refs_8_.refs_4_.refs_0_ = bf16[3088,512]{1,0:T(8,128)(2,1)} custom-call(s32[1]{0:T(128)} %dynamic_slice.12.flag_ref, bf16[3088,512]{1,0:T(8,128)(2,1)} %copy-done.14, bf16[3088,512]{1,0:T(8,128)(2,1)} %copy-done.14, f32[3072,512]{1,0:T(8,128)} %shard_map.82.refs_0_.refs_13_), custom_call_target="tpu_custom_call" | custom-call | bytes 6324224 | tf_op jit(solution)/shard_map/pallas_call | solution.py:413
  138.1 1.1 collective-permute-start.8
  139.3 3.9 %collective-permute-start.9 = (bf16[3088,512]{1,0:T(8,128)(2,1)}, bf16[3088,512]{1,0:T(8,128)(2,1)S(1)}, u32[]{:S(2)}, u32[]{:S(2)}) collective-permute-start(bf16[3088,512]{1,0:T(8,128)(2,1)} %shard_map.83.refs_8_.refs_4_.refs_0_), channel_id=1, source_target_pairs={{0,8},{2,4},{4,2},{6,30},{8,16},{10,12},{12,10},{14,6},{16,24},{18... | collective-permute-start | bytes 9486344 | tf_op jit(solution)/shard_map/ppermute | solution.py:609
  143.7 14.4 %shard_map.84 = (f32[3072,512]{1,0:T(8,128)}, bf16[3088,512]{1,0:T(8,128)(2,1)}) custom-call(bf16[3088,512]{1,0:T(8,128)(2,1)} %get-tuple-element.38.refs_0_.refs_2_, bf16[3088,512]{1,0:T(8,128)(2,1)} %copy-done.10, bf16[3088,512]{1,0:T(8,128)(2,1)} %get-tuple-element.40.refs_0_.refs_2_, bf16[3088,512]{1,0:T(8,128)(2,1)} %copy-done.13, ...), custom_call_target="tpu_custom_call" | custom-call | flops 6442450944 | bytes 20971520 | tf_op jit(solution)/shard_map/pallas_call | solution.py:576
  158.2 1.1 copy-done.21
  160.9 16.6 %shard_map.85.refs_4_.refs_3_.refs_7_.refs_8_.refs_9_.refs_10_ = bf16[6,512,512]{2,1,0:T(8,128)(2,1)} custom-call(f32[12,3]{1,0:T(8,128)S(1)} %copy.44.scalars, bf16[1536,512]{1,0:T(8,128)(2,1)} %collective-permute-done.1.refs_0_.array_ref.refs_7_, bf16[1552,512]{1,0:T(8,128)(2,1)} %copy-done.11, bf16[1536,512]{1,0:T(8,128)(2,1)} %copy-done.21, ...), custom_call_target="tpu_custom_call" | custom-call | flops 9663676416 | bytes 22020096 | tf_op jit(solution)/shard_map/pallas_call | solution.py:255
  177.9 1.6 copy-done.8
  179.5 5.7 %shard_map.86.refs_5_.refs_6_ = bf16[1,512,512]{2,1,0:T(8,128)(2,1)S(1)} custom-call(f32[12,3]{1,0:T(8,128)S(1)} %copy.44.scalars, bf16[3088,512]{1,0:T(8,128)(2,1)} %copy-done.8, bf16[512,3072]{1,0:T(8,128)(2,1)} %slice_bitcast_fusion.refs_2_.refs_4_.refs_6_.refs_1_.refs_3_, bf16[512,1536]{1,0:T(8,128)(2,1)} %copy-done.1, bf16[512,1536]{1,0:T(8,128)(2,1)} %copy-done.4, ...), custom_call_target="tpu_custom_call" | custom-call | flops 1610612736 | bytes 9961472 | tf_op jit(solution)/shard_map/pallas_call | solution.py:255
  185.2 8.4 %shard_map.87 = (bf16[1536,512]{1,0:T(8,128)(2,1)}, bf16[3088,512]{1,0:T(8,128)(2,1)}) custom-call(bf16[3088,512]{1,0:T(8,128)(2,1)} %shard_map.83.refs_8_.refs_4_.refs_0_, bf16[3088,512]{1,0:T(8,128)(2,1)} %copy-done.9, bf16[3088,512]{1,0:T(8,128)(2,1)} %copy-done.8, bf16[6,512,512]{2,1,0:T(8,128)(2,1)} %shard_map.85.refs_4_.refs_3_.refs_7_.refs_8_.refs_9_.refs_10_, ...), custom_call_target="tpu_custom_call" | custom-call | flops 2415919104 | bytes 11010048 | tf_op jit(solution)/shard_map/pallas_call | solution.py:576
  193.6 3.9 %collective-permute-start.12 = (bf16[3088,512]{1,0:T(8,128)(2,1)}, bf16[3088,512]{1,0:T(8,128)(2,1)}, u32[]{:S(2)}, u32[]{:S(2)}) collective-permute-start(bf16[3088,512]{1,0:T(8,128)(2,1)} %get-tuple-element.42), channel_id=1, source_target_pairs={{0,8},{2,4},{4,2},{6,30},{8,16},{10,12},{12,10},{14,6},{16,24},{18... | collective-permute-start | bytes 9486344 | tf_op jit(solution)/shard_map/ppermute | solution.py:609
  197.4 1.2 collective-permute-start.17
  198.7 7.7 %shard_map.88.refs_2_ = bf16[1536,512]{1,0:T(8,128)(2,1)} custom-call(bf16[3088,512]{1,0:T(8,128)(2,1)} %shard_map.83.refs_8_.refs_4_.refs_0_, bf16[3088,512]{1,0:T(8,128)(2,1)} %copy-done.9, bf16[3088,512]{1,0:T(8,128)(2,1)} %copy-done.8, bf16[6,512,512]{2,1,0:T(8,128)(2,1)} %shard_map.85.refs_4_.refs_3_.refs_7_.refs_8_.refs_9_.refs_10_, ...), custom_call_target="tpu_custom_call" | custom-call | flops 2415919104 | bytes 11010048 | tf_op jit(solution)/shard_map/pallas_call | solution.py:576
  206.4 5.7 %shard_map.89.refs_11_.refs_12_ = bf16[1,512,512]{2,1,0:T(8,128)(2,1)S(1)} custom-call(f32[12,3]{1,0:T(8,128)S(1)} %copy.44.scalars, bf16[3088,512]{1,0:T(8,128)(2,1)} %copy-done.8, bf16[512,3072]{1,0:T(8,128)(2,1)} %slice_bitcast_fusion.refs_2_.refs_4_.refs_6_.refs_1_.refs_3_, bf16[1536,512]{1,0:T(8,128)(2,1)} %shard_map.88.refs_2_, ...), custom_call_target="tpu_custom_call" | custom-call | flops 1610612736 | bytes 6815744 | tf_op jit(solution)/shard_map/pallas_call | solution.py:255
  212.1 15.6 %shard_map.90.refs_0_.refs_9_ = f32[3072,512]{1,0:T(8,128)} custom-call(bf16[1536,512]{1,0:T(8,128)(2,1)} %collective-permute-done.1.refs_0_.array_ref.refs_7_, bf16[1552,512]{1,0:T(8,128)(2,1)} %copy-done.11, bf16[1536,512]{1,0:T(8,128)(2,1)} %copy-done.21, bf16[1552,512]{1,0:T(8,128)(2,1)} %copy-done.20, ...), custom_call_target="tpu_custom_call" | custom-call | flops 8053063680 | bytes 30932992 | tf_op jit(solution)/shard_map/pallas_call | solution.py:576
  227.7 3.4 %shard_map.91 = (bf16[1024,512]{1,0:T(8,128)(2,1)S(1)}, bf16[1024,512]{1,0:T(8,128)(2,1)}, bf16[1040,512]{1,0:T(8,128)(2,1)}) custom-call(s32[1]{0:T(128)} %dynamic_slice.12.flag_ref, bf16[3088,512]{1,0:T(8,128)(2,1)} %collective-permute-done.13.a_ref.b_ref, bf16[3088,512]{1,0:T(8,128)(2,1)} %collective-permute-done.13.a_ref.b_ref, ...), custom_call_target="tpu_custom_call" | custom-call | bytes 6324224 | tf_op jit(solution)/shard_map/pallas_call | solution.py:413
  232.1 5.7 %shard_map.92.refs_1_.refs_6_ = bf16[1,512,512]{2,1,0:T(8,128)(2,1)S(1)} custom-call(f32[12,3]{1,0:T(8,128)S(1)} %copy.44.scalars, bf16[1024,512]{1,0:T(8,128)(2,1)} %copy-done.3, bf16[1024,512]{1,0:T(8,128)(2,1)} %get-tuple-element.46.refs_1_.refs_5_, bf16[1040,512]{1,0:T(8,128)(2,1)} %get-tuple-element.47.refs_2_.refs_6_, ...), custom_call_target="tpu_custom_call" | custom-call | flops 1610612736 | bytes 6815744 | tf_op jit(solution)/shard_map/pallas_call | solution.py:255
  241.2 5.7 %shard_map.94.refs_7_.refs_8_ = bf16[1,512,512]{2,1,0:T(8,128)(2,1)S(1)} custom-call(f32[12,3]{1,0:T(8,128)S(1)} %copy.44.scalars, bf16[1024,512]{1,0:T(8,128)(2,1)} %collective-permute-done.14.refs_0_.refs_3_, bf16[1024,512]{1,0:T(8,128)(2,1)} %collective-permute-done.15.refs_1_.refs_4_, bf16[1040,512]{1,0:T(8,128)(2,1)} %collective-permute-done.16.refs_2_.refs_5_, ...), custom_call_target="tpu_custom_call" | custom-call | flops 1610612736 | bytes 6815744 | tf_op jit(solution)/shard_map/pallas_call | solution.py:255
  246.9 11.3 %shard_map.95.refs_0_.refs_9_ = f32[3072,512]{1,0:T(8,128)} custom-call(bf16[1024,512]{1,0:T(8,128)(2,1)} %copy-done.3, bf16[1024,512]{1,0:T(8,128)(2,1)} %get-tuple-element.46.refs_1_.refs_5_, bf16[1040,512]{1,0:T(8,128)(2,1)} %get-tuple-element.47.refs_2_.refs_6_, bf16[1024,512]{1,0:T(8,128)(2,1)} %collective-permute-done.14.refs_0_.refs_3_, ...), custom_call_target="tpu_custom_call" | custom-call | flops 3221225472 | bytes 19922944 | tf_op jit(solution)/shard_map/pallas_call | solution.py:576
  258.2 3.5 %shard_map.96 = (bf16[1024,512]{1,0:T(8,128)(2,1)S(1)}, bf16[1024,512]{1,0:T(8,128)(2,1)}, bf16[1040,512]{1,0:T(8,128)(2,1)}) custom-call(s32[1]{0:T(128)} %dynamic_slice.12.flag_ref, bf16[3088,512]{1,0:T(8,128)(2,1)} %collective-permute-done.12.a_ref.b_ref, bf16[3088,512]{1,0:T(8,128)(2,1)} %collective-permute-done.12.a_ref.b_ref, ...), custom_call_target="tpu_custom_call" | custom-call | bytes 6324224 | tf_op jit(solution)/shard_map/pallas_call | solution.py:413
  262.6 5.7 %shard_map.97.refs_4_.refs_6_ = bf16[1,512,512]{2,1,0:T(8,128)(2,1)S(1)} custom-call(f32[12,3]{1,0:T(8,128)S(1)} %copy.44.scalars, bf16[1024,512]{1,0:T(8,128)(2,1)} %copy-done.2, bf16[1024,512]{1,0:T(8,128)(2,1)} %get-tuple-element.49.refs_1_.refs_5_, bf16[1040,512]{1,0:T(8,128)(2,1)} %get-tuple-element.50.refs_2_.refs_6_, ...), custom_call_target="tpu_custom_call" | custom-call | flops 1610612736 | bytes 6815744 | tf_op jit(solution)/shard_map/pallas_call | solution.py:255
  270.7 5.7 %shard_map.98.refs_7_.refs_8_ = bf16[1,512,512]{2,1,0:T(8,128)(2,1)S(1)} custom-call(f32[12,3]{1,0:T(8,128)S(1)} %copy.44.scalars, bf16[1024,512]{1,0:T(8,128)(2,1)} %copy-done.17, bf16[1024,512]{1,0:T(8,128)(2,1)} %copy-done.18, bf16[1040,512]{1,0:T(8,128)(2,1)} %copy-done.16, bf16[512,3072]{1,0:T(8,128)(2,1)} %slice_bitcast_fusion.refs_2_.refs_4_.refs_6_.refs_1_.refs_3_, ...), custom_call_target="tpu_custom_call" | custom-call | flops 1610612736 | bytes 6815744 | tf_op jit(solution)/shard_map/pallas_call | solution.py:255
  276.4 12.0 %shard_map.99 = f32[3072,512]{1,0:T(8,128)} custom-call(bf16[1024,512]{1,0:T(8,128)(2,1)} %copy-done.2, bf16[1024,512]{1,0:T(8,128)(2,1)} %get-tuple-element.49.refs_1_.refs_5_, bf16[1040,512]{1,0:T(8,128)(2,1)} %get-tuple-element.50.refs_2_.refs_6_, bf16[1024,512]{1,0:T(8,128)(2,1)} %copy-done.17, bf16[1024,512]{1,0:T(8,128)(2,1)} %copy-done.18, ...), custom_call_target="tpu_custom_call" | custom-call | flops 3221225472 | bytes 26214400 | tf_op jit(solution)/shard_map/pallas_call | solution.py:576
  (93 shorter events, 17.4 us)
Async XLA Ops:
  4.3 14.5 %collective-permute-start.2 = (bf16[3088,512]{1,0:T(8,128)(2,1)}, bf16[3088,512]{1,0:T(8,128)(2,1)}, u32[]{:S(2)}, u32[]{:S(2)}) collective-permute-start(bf16[3088,512]{1,0:T(8,128)(2,1)} %get-tuple-element.34.refs_0_.b_ref.refs_9_), channel_id=1, source_target_pairs={{0,2},{2,0},{4,6},{6,4},{8,10},{10,8},{12,14},{14,12},{16,18},{18,... | collective-permute-start | bytes 9486344 | tf_op jit(solution)/shard_map/ppermute | solution.py:609
  5.0 37.5 %collective-permute-start = (bf16[3088,512]{1,0:T(8,128)(2,1)}, bf16[3088,512]{1,0:T(8,128)(2,1)}, u32[]{:S(2)}, u32[]{:S(2)}) collective-permute-start(bf16[3088,512]{1,0:T(8,128)(2,1)} %get-tuple-element.34.refs_0_.b_ref.refs_9_), channel_id=1, source_target_pairs={{0,6},{2,26},{4,12},{6,0},{8,14},{10,2},{12,20},{14,8},{16,22},{18... | collective-permute-start | bytes 9486344 | tf_op jit(solution)/shard_map/ppermute | solution.py:609
  5.0 34.4 %collective-permute-start.1 = (bf16[1536,512]{1,0:T(8,128)(2,1)S(1)}, bf16[1536,512]{1,0:T(8,128)(2,1)}, u32[]{:S(2)}, u32[]{:S(2)}) collective-permute-start(bf16[1536,512]{1,0:T(8,128)(2,1)S(1)} %get-tuple-element.35), channel_id=1, source_target_pairs={{0,1},{1,0},{2,3},{3,2},{4,5},{5,4},{6,7},{7,6},{8,9},{9,8},{10,11... | collective-permute-start | bytes 4718600 | tf_op jit(solution)/shard_map/ppermute | solution.py:621
  6.5 6.3 %copy-start.24 = (f32[16]{0:T(128)S(1)}, f32[16]{0:T(128)}, u32[]{:S(2)}) copy-start(f32[16]{0:T(128)} %param.11) | copy-start | bytes 196
  6.5 6.3 %copy-start.25 = (s32[16]{0:T(128)S(1)}, s32[16]{0:T(128)}, u32[]{:S(2)}) copy-start(s32[16]{0:T(128)} %param.10) | copy-start | bytes 196
  6.5 6.9 %copy-start.22 = (f32[1024]{0:T(1024)S(1)}, f32[1024]{0:T(1024)}, u32[]{:S(2)}) copy-start(f32[1024]{0:T(1024)} %param.12) | copy-start | bytes 12292
  6.5 7.2 %copy-start.26 = (s32[16]{0:T(128)S(1)}, s32[16]{0:T(128)}, u32[]{:S(2)}) copy-start(s32[16]{0:T(128)} %constant.53.clone) | copy-start | bytes 196
  39.4 10.0 %copy-start.23 = (bf16[1552,512]{1,0:T(8,128)(2,1)S(1)}, bf16[1552,512]{1,0:T(8,128)(2,1)}, u32[]{:S(2)}) copy-start(bf16[1552,512]{1,0:T(8,128)(2,1)} %get-tuple-element.37) | copy-start | bytes 4767748
  48.0 6.3 %collective-permute-start.5 = (bf16[3088,512]{1,0:T(8,128)(2,1)}, bf16[3088,512]{1,0:T(8,128)(2,1)S(1)}, u32[]{:S(2)}, u32[]{:S(2)}) collective-permute-start(bf16[3088,512]{1,0:T(8,128)(2,1)} %get-tuple-element.38.refs_0_.refs_2_), channel_id=1, source_target_pairs={{0,2},{2,0},{4,6},{6,4},{8,10},{10,8},{12,14},{14,12},{16,18},{18,... | collective-permute-start | bytes 9486344 | tf_op jit(solution)/shard_map/ppermute | solution.py:609
  48.7 38.3 %collective-permute-start.3 = (bf16[3088,512]{1,0:T(8,128)(2,1)}, bf16[3088,512]{1,0:T(8,128)(2,1)S(1)}, u32[]{:S(2)}, u32[]{:S(2)}) collective-permute-start(bf16[3088,512]{1,0:T(8,128)(2,1)} %get-tuple-element.36.refs_3_), channel_id=1, source_target_pairs={{0,24},{2,4},{4,2},{6,14},{8,0},{10,12},{12,10},{14,22},{16,8},{18... | collective-permute-start | bytes 9486344 | tf_op jit(solution)/shard_map/ppermute | solution.py:609
  49.4 36.6 %collective-permute-start.4 = (bf16[1552,512]{1,0:T(8,128)(2,1)S(1)}, bf16[1552,512]{1,0:T(8,128)(2,1)S(1)}, u32[]{:S(2)}, u32[]{:S(2)}) collective-permute-start(bf16[1552,512]{1,0:T(8,128)(2,1)S(1)} %copy-done.23), channel_id=1, source_target_pairs={{0,1},{1,0},{2,3},{3,2},{4,5},{5,4},{6,7},{7,6},{8,9},{9,8},{10,11... | collective-permute-start | bytes 4767752 | tf_op jit(solution)/shard_map/ppermute | solution.py:621
  54.2 1.7 copy-start.10
  63.3 1.0 copy-start
  78.6 14.9 %copy-start.1 = (bf16[512,1536]{1,0:T(8,128)(2,1)}, bf16[512,1536]{1,0:T(8,128)(2,1)S(1)}, u32[]{:S(2)}) copy-start(bf16[512,1536]{1,0:T(8,128)(2,1)S(1)} %shard_map.78.refs_1_.refs_5_.refs_7_.refs_2_) | copy-start | bytes 4718596
  86.0 1.1 copy-start.11
  87.1 1.7 copy-start.19
  93.5 7.5 %collective-permute-start.7 = (bf16[3088,512]{1,0:T(8,128)(2,1)}, bf16[3088,512]{1,0:T(8,128)(2,1)S(1)}, u32[]{:S(2)}, u32[]{:S(2)}) collective-permute-start(bf16[3088,512]{1,0:T(8,128)(2,1)} %get-tuple-element.40.refs_0_.refs_2_), channel_id=1, source_target_pairs={{0,2},{2,0},{4,6},{6,4},{8,10},{10,8},{12,14},{14,12},{16,18},{18,... | collective-permute-start | bytes 9486344 | tf_op jit(solution)/shard_map/ppermute | solution.py:609
  95.5 37.4 %collective-permute-start.6 = (bf16[3088,512]{1,0:T(8,128)(2,1)}, bf16[3088,512]{1,0:T(8,128)(2,1)S(1)}, u32[]{:S(2)}, u32[]{:S(2)}) collective-permute-start(bf16[3088,512]{1,0:T(8,128)(2,1)} %get-tuple-element.39.refs_0_), channel_id=1, source_target_pairs={{0,6},{2,10},{4,28},{6,0},{8,14},{10,18},{12,4},{14,8},{16,22},{18... | collective-permute-start | bytes 9486344 | tf_op jit(solution)/shard_map/ppermute | solution.py:609
  98.1 1.2 copy-start.4
  101.1 1.6 copy-start.13
  130.8 12.4 %copy-start.12 = (bf16[1552,512]{1,0:T(8,128)(2,1)S(1)}, bf16[1552,512]{1,0:T(8,128)(2,1)}, u32[]{:S(2)}) copy-start(bf16[1552,512]{1,0:T(8,128)(2,1)} %copy-done.11) | copy-start | bytes 4767748
  132.9 1.7 copy-start.14
  138.1 20.1 %collective-permute-start.8 = (bf16[3088,512]{1,0:T(8,128)(2,1)}, bf16[3088,512]{1,0:T(8,128)(2,1)S(1)}, u32[]{:S(2)}, u32[]{:S(2)}) collective-permute-start(bf16[3088,512]{1,0:T(8,128)(2,1)} %shard_map.83.refs_8_.refs_4_.refs_0_), channel_id=1, source_target_pairs={{0,2},{2,0},{4,6},{6,4},{8,10},{10,8},{12,14},{14,12},{16,18},{18,... | collective-permute-start | bytes 9486344 | tf_op jit(solution)/shard_map/ppermute | solution.py:609
  139.3 38.6 %collective-permute-start.9 = (bf16[3088,512]{1,0:T(8,128)(2,1)}, bf16[3088,512]{1,0:T(8,128)(2,1)S(1)}, u32[]{:S(2)}, u32[]{:S(2)}) collective-permute-start(bf16[3088,512]{1,0:T(8,128)(2,1)} %shard_map.83.refs_8_.refs_4_.refs_0_), channel_id=1, source_target_pairs={{0,8},{2,4},{4,2},{6,30},{8,16},{10,12},{12,10},{14,6},{16,24},{18... | collective-permute-start | bytes 9486344 | tf_op jit(solution)/shard_map/ppermute | solution.py:609
  143.2 15.0 %collective-permute-start.11 = (bf16[1552,512]{1,0:T(8,128)(2,1)S(1)}, bf16[1552,512]{1,0:T(8,128)(2,1)S(1)}, u32[]{:S(2)}, u32[]{:S(2)}) collective-permute-start(bf16[1552,512]{1,0:T(8,128)(2,1)S(1)} %copy-done.12), channel_id=1, source_target_pairs={{0,2},{2,0},{4,6},{6,4},{8,10},{10,8},{12,14},{14,12},{16,18},{18,... | collective-permute-start | bytes 4767752 | tf_op jit(solution)/shard_map/ppermute | solution.py:609
  143.2 15.0 %collective-permute-start.10 = (bf16[1536,512]{1,0:T(8,128)(2,1)}, bf16[1536,512]{1,0:T(8,128)(2,1)S(1)}, u32[]{:S(2)}, u32[]{:S(2)}) collective-permute-start(bf16[1536,512]{1,0:T(8,128)(2,1)} %collective-permute-done.1.refs_0_.array_ref.refs_7_), channel_id=1, source_target_pairs={{0,2},{2,0},{4,6},{6,4},{8,10},{10,8},{12,14},{14,12},{16,18},{18,... | collective-permute-start | bytes 4718600 | tf_op jit(solution)/shard_map/ppermute | solution.py:609
  158.1 69.6 %collective-permute-start.13 = (bf16[3088,512]{1,0:T(8,128)(2,1)}, bf16[3088,512]{1,0:T(8,128)(2,1)}, u32[]{:S(2)}, u32[]{:S(2)}) collective-permute-start(bf16[3088,512]{1,0:T(8,128)(2,1)} %get-tuple-element.43), channel_id=1, source_target_pairs={{0,8},{2,4},{4,2},{6,30},{8,16},{10,12},{12,10},{14,6},{16,24},{18... | collective-permute-start | bytes 9486344 | tf_op jit(solution)/shard_map/ppermute | solution.py:609
  158.2 1.1 copy-start.21
  158.2 1.7 copy-start.20
  158.2 2.7 copy-start.9
  177.9 1.6 copy-start.8
  193.6 64.6 %collective-permute-start.12 = (bf16[3088,512]{1,0:T(8,128)(2,1)}, bf16[3088,512]{1,0:T(8,128)(2,1)}, u32[]{:S(2)}, u32[]{:S(2)}) collective-permute-start(bf16[3088,512]{1,0:T(8,128)(2,1)} %get-tuple-element.42), channel_id=1, source_target_pairs={{0,8},{2,4},{4,2},{6,30},{8,16},{10,12},{12,10},{14,6},{16,24},{18... | collective-permute-start | bytes 9486344 | tf_op jit(solution)/shard_map/ppermute | solution.py:609
  197.4 41.2 %collective-permute-start.17 = (bf16[1536,512]{1,0:T(8,128)(2,1)}, bf16[1536,512]{1,0:T(8,128)(2,1)S(1)}, u32[]{:S(2)}, u32[]{:S(2)}) collective-permute-start(bf16[1536,512]{1,0:T(8,128)(2,1)} %get-tuple-element.44.refs_6_), channel_id=1, source_target_pairs={{0,1},{1,0},{2,3},{3,2},{4,5},{5,4},{6,7},{7,6},{8,9},{9,8},{10,11... | collective-permute-start | bytes 4718600 | tf_op jit(solution)/shard_map/ppermute | solution.py:621
  231.1 1.0 copy-start.3
  231.1 9.3 %collective-permute-start.16 = (bf16[1040,512]{1,0:T(8,128)(2,1)}, bf16[1040,512]{1,0:T(8,128)(2,1)}, u32[]{:S(2)}, u32[]{:S(2)}) collective-permute-start(bf16[1040,512]{1,0:T(8,128)(2,1)} %get-tuple-element.47.refs_2_.refs_6_), channel_id=1, source_target_pairs={{0,2},{2,0},{4,6},{6,4},{8,10},{10,8},{12,14},{14,12},{16,18},{18,... | collective-permute-start | bytes 3194888 | tf_op jit(solution)/shard_map/ppermute | solution.py:609
  231.2 9.2 %collective-permute-start.14 = (bf16[1024,512]{1,0:T(8,128)(2,1)S(1)}, bf16[1024,512]{1,0:T(8,128)(2,1)}, u32[]{:S(2)}, u32[]{:S(2)}) collective-permute-start(bf16[1024,512]{1,0:T(8,128)(2,1)S(1)} %get-tuple-element.45.refs_0_.refs_4_), channel_id=1, source_target_pairs={{0,2},{2,0},{4,6},{6,4},{8,10},{10,8},{12,14},{14,12},{16,18},{18,... | collective-permute-start | bytes 3145736 | tf_op jit(solution)/shard_map/ppermute | solution.py:609
  231.7 8.7 %collective-permute-start.15 = (bf16[1024,512]{1,0:T(8,128)(2,1)}, bf16[1024,512]{1,0:T(8,128)(2,1)}, u32[]{:S(2)}, u32[]{:S(2)}) collective-permute-start(bf16[1024,512]{1,0:T(8,128)(2,1)} %get-tuple-element.46.refs_1_.refs_5_), channel_id=1, source_target_pairs={{0,2},{2,0},{4,6},{6,4},{8,10},{10,8},{12,14},{14,12},{16,18},{18,... | collective-permute-start | bytes 3145736 | tf_op jit(solution)/shard_map/ppermute | solution.py:609
  237.9 0.8 copy-start.5
  238.7 1.2 copy-start.15
  238.7 37.7 %collective-permute-start.21 = (bf16[1536,512]{1,0:T(8,128)(2,1)}, bf16[1536,512]{1,0:T(8,128)(2,1)}, u32[]{:S(2)}, u32[]{:S(2)}) collective-permute-start(bf16[1536,512]{1,0:T(8,128)(2,1)} %shard_map.88.refs_2_), channel_id=1, source_target_pairs={{0,1},{1,0},{2,3},{3,2},{4,5},{5,4},{6,7},{7,6},{8,9},{9,8},{10,11... | collective-permute-start | bytes 4718600 | tf_op jit(solution)/shard_map/ppermute | solution.py:621
  240.4 6.4 %copy-start.6 = (bf16[1,512,512]{2,1,0:T(8,128)(2,1)S(1)}, bf16[1,512,512]{2,1,0:T(8,128)(2,1)}, u32[]{:S(2)}) copy-start(bf16[1,512,512]{2,1,0:T(8,128)(2,1)} %copy-done.5) | copy-start | bytes 1572868
  261.6 1.0 copy-start.2
  261.6 6.7 %collective-permute-start.20 = (bf16[1040,512]{1,0:T(8,128)(2,1)}, bf16[1040,512]{1,0:T(8,128)(2,1)S(1)}, u32[]{:S(2)}, u32[]{:S(2)}) collective-permute-start(bf16[1040,512]{1,0:T(8,128)(2,1)} %get-tuple-element.50.refs_2_.refs_6_), channel_id=1, source_target_pairs={{0,2},{2,0},{4,6},{6,4},{8,10},{10,8},{12,14},{14,12},{16,18},{18,... | collective-permute-start | bytes 3194888 | tf_op jit(solution)/shard_map/ppermute | solution.py:609
  261.8 6.5 %collective-permute-start.18 = (bf16[1024,512]{1,0:T(8,128)(2,1)S(1)}, bf16[1024,512]{1,0:T(8,128)(2,1)S(1)}, u32[]{:S(2)}, u32[]{:S(2)}) collective-permute-start(bf16[1024,512]{1,0:T(8,128)(2,1)S(1)} %get-tuple-element.48.refs_0_.refs_4_), channel_id=1, source_target_pairs={{0,2},{2,0},{4,6},{6,4},{8,10},{10,8},{12,14},{14,12},{16,18},{18,... | collective-permute-start | bytes 3145736 | tf_op jit(solution)/shard_map/ppermute | solution.py:609
  262.2 6.1 %collective-permute-start.19 = (bf16[1024,512]{1,0:T(8,128)(2,1)}, bf16[1024,512]{1,0:T(8,128)(2,1)S(1)}, u32[]{:S(2)}, u32[]{:S(2)}) collective-permute-start(bf16[1024,512]{1,0:T(8,128)(2,1)} %get-tuple-element.49.refs_1_.refs_5_), channel_id=1, source_target_pairs={{0,2},{2,0},{4,6},{6,4},{8,10},{10,8},{12,14},{14,12},{16,18},{18,... | collective-permute-start | bytes 3145736 | tf_op jit(solution)/shard_map/ppermute | solution.py:609
  268.3 1.0 copy-start.17
  268.3 1.4 copy-start.18
  269.7 1.0 copy-start.16
  (1 other events, 0.7 us)
